TPU v7x, 32 devices: a whole 2x2x4 slice. The times are simulated.
32 devices in a mesh: row: 4 (over y, x), col: 8 (over z, core).
Axes of the slice: x: 2, y: 2, z: 4, core: 2. Of those that a mesh axis runs over, the one named last changes fastest.
Arguments:
- factor_blocks: bfloat16 [6, 8, 1024, 4, 2048], P(None, None, 'row', None, 'col'), may hold values from -0.03125 to 0.03125
- inverse_blocks: bfloat16 [4, 4, 2048, 8, 1024], P(None, None, 'col', None, 'row'), as said below
- right_side: bfloat16 [4, 8, 1024, 128], P(None, None, 'row'), may hold values from -4 to 4
- centers: bfloat16 [16, 2048, 512], P(None, 'col')
- owner_map: int32 [16, 8], P(None, 'col'), may hold values from 0 to 15, as said below
- test_pool: bfloat16 [24576, 512], P('row')
- test_rows: int32 [16384], P('row'), may hold values from 0 to 24575, as said below
Outputs:
- coefficients: float32 [4, 4, 2048, 128], P(None, None, 'col')
- predictions: float32 [16384, 128], P(('row', 'col'))
Inputs may be any that keep to these rules, and one draw needn't show every extreme that they name: `owner_map`: each column c is a permutation of 0 to 15. `test_rows`: entry i names a row of block i // 4096 of the pool, that is from (i // 4096) * 6144 to (i // 4096 + 1) * 6144 - 1; rows may repeat. `inverse_blocks`: read as D_k, each block is upper triangular with a positive diagonal.
All inputs are finite; a program needn't handle non-finite values.
Results may differ from a plain program's by a relative error of at most 0.019.
Values may be sent and summed in bfloat16 or wider, within the bound.
No kernel may reach another device: no remote copies, remote signals or barrier semaphores. Data moves between devices by JAX's collectives and lax.ppermute only.
A program may use at most 192 MiB of HBM per device.

v0:
```python
import jax
import jax.numpy as jnp
from jax import lax
from jax.sharding import PartitionSpec as P

inverse_width = 0.35


def pair_slot(early, successor):
    return successor * (successor - 1) // 2 + early


def shards(factor_blocks, inverse_blocks, right_side, centers, owner_map, test_pool, test_rows):
    panels = inverse_blocks.shape[0]
    col_tiles = inverse_blocks.shape[1]
    tile_size = inverse_blocks.shape[2]
    row_tiles = inverse_blocks.shape[3]
    width_out = right_side.shape[3]
    own_rows = row_tiles * tile_size
    own_cols = col_tiles * tile_size
    blocks = factor_blocks.reshape(factor_blocks.shape[0], own_rows, own_cols)
    inverse = inverse_blocks.reshape(panels, own_cols, own_rows)
    targets = right_side.reshape(panels, own_rows, width_out)
    solved = [None] * panels
    rounded = [None] * panels

    def subtract(current, partial_value):
        portion = lax.psum_scatter(partial_value, "col", scatter_dimension=0, tiled=True)
        height = portion.shape[0]
        offset = lax.axis_index("col") * height
        local_rhs = lax.dynamic_slice_in_dim(targets[current], offset, height, 0).astype(
            jnp.float32
        )
        reduced = (local_rhs - portion).astype(jnp.bfloat16)
        return lax.all_gather(reduced, "col", axis=0, tiled=True)

    def settle(current, partial_value):
        if partial_value is None:
            residue = targets[current]
        else:
            residue = subtract(current, partial_value)
        product_rows = jnp.dot(inverse[current], residue, preferred_element_type=jnp.float32)
        summed_rows = lax.psum(product_rows, "row")
        solved[current] = summed_rows
        rounded[current] = summed_rows.astype(jnp.bfloat16)

    final = panels - 1
    for current in range(final, -1, -1):
        partial_value = None
        for successor in range(current + 1, panels):
            product = jnp.dot(
                blocks[pair_slot(current, successor)],
                rounded[successor],
                preferred_element_type=jnp.float32,
            )
            partial_value = product if partial_value is None else partial_value + product
        settle(current, partial_value)
    coefficient = jnp.stack(rounded).reshape(panels * col_tiles, tile_size, width_out)
    paired = jnp.take(coefficient, owner_map[:, 0], axis=0).reshape(panels * own_cols, width_out)
    located = test_rows - lax.axis_index("row") * test_pool.shape[0]
    span_rows = jnp.take(test_pool, located, axis=0)
    flat_centers = centers.reshape(centers.shape[0] * centers.shape[1], centers.shape[2])
    center_sq = jnp.sum(jnp.square(flat_centers.astype(jnp.float32)), axis=1)
    test_sq = jnp.sum(jnp.square(span_rows.astype(jnp.float32)), axis=1)
    crossed = lax.dot_general(
        span_rows, flat_centers, (((1,), (1,)), ((), ())), preferred_element_type=jnp.float32
    )
    distance = test_sq[:, None] + center_sq[None, :] - 2.0 * crossed
    kernel = jnp.exp(-inverse_width * distance).astype(jnp.bfloat16)
    estimate = lax.psum_scatter(
        jnp.dot(kernel, paired, preferred_element_type=jnp.float32).astype(jnp.bfloat16),
        "col",
        scatter_dimension=0,
        tiled=True,
    ).astype(jnp.float32)
    alpha = jnp.stack(solved).reshape(panels, col_tiles, tile_size, width_out)
    return (alpha, estimate)


def solution(mesh):
    in_specs = (
        P(None, None, "row", None, "col"),
        P(None, None, "col", None, "row"),
        P(None, None, "row", None),
        P(None, "col", None),
        P(None, "col"),
        P("row", None),
        P("row"),
    )
    out_specs = (P(None, None, "col", None), P(("row", "col"), None))
    return jax.shard_map(shards, mesh=mesh, in_specs=in_specs, out_specs=out_specs, check_vma=False)
```

profile of v0, /device:TPU:0, one launch (start us, length us, event | category | flops | bytes accessed | tf_op | source)
XLA Modules:
  0.0 462.3 jit_solution(4652666799393301882)
XLA Ops:
  7.2 0.0 all-reduce.5.cloned.1.call-start
  7.2 10.8 %fusion.14 = (bf16[1,4,256,8,256]{4,3,2,1,0:T(8,128)(2,1)}, bf16[1,4,256,8,256]{4,3,2,1,0:T(8,128)(2,1)}, bf16[1,4,256,8,256]{4,3,2,1,0:T(8,128)(2,1)S(1)}, bf16[1,4,256,8,256]{4,3,2,1,0:T(8,128)(2,1)}) fusion(bf16[4,4,256,8,256]{4,3,2,1,0:T(8,128)(2,1)} %param.8), kind=kLoop, calls=%fused_computation.41 | loop fusion | bytes 33554432 | tf_op jit(solution)/shard_map/slice | solution.py:42
  18.0 1.5 copy.21
  19.5 0.1 copy-done.9
  19.6 0.1 fusion.15
  19.8 2.0 fusion.16
  21.8 0.0 all-reduce.5.cloned.1.call-update
  21.8 0.0 reduce-scatter.5.cloned.1.call-start
  21.9 17.3 %fusion.13 = (bf16[1,8,256,4,256]{4,3,2,1,0:T(4,128)(2,1)}, bf16[1,8,256,4,256]{4,3,2,1,0:T(4,128)(2,1)}, bf16[1,8,256,4,256]{4,3,2,1,0:T(4,128)(2,1)}, bf16[1,8...) fusion(bf16[6,8,256,4,256]{4,3,2,1,0:T(4,128)(2,1)} %param.7), kind=kLoop, calls=%fused_computation.40 | loop fusion | bytes 50331648 | tf_op jit(solution)/shard_map/slice | solution.py:52
  39.2 3.1 copy.20
  42.3 27.7 %all-reduce.5.cloned.1.call-done = f32[1024,128]{1,0:T(8,128)} async-done(((f32[1024,128]{1,0:T(8,128)}), f32[1024,128]{1,0:T(8,128)}) %all-reduce.5.cloned.1.call-update) | async-done | bytes 524304 | tf_op jit(solution)/shard_map/psum | solution.py:43
  70.0 4.5 convolution_bitcast_fusion
  74.5 0.0 reduce-scatter.5.cloned.1.call-update
  74.6 0.0 all-reduce.7.cloned.1.call-start
  74.6 5.7 %copy.19 = bf16[128,8,8,256]{3,1,2,0:T(8,128)(2,1)} copy(bf16[128,8,8,256]{3,2,1,0:T(8,128)(2,1)} %bitcast.105) | data formatting | bytes 8388608
  80.4 26.7 %reduce-scatter.5.cloned.1.call-done = f32[256,128]{1,0:T(8,128)} async-done(((f32[2048,128]{1,0:T(8,128)}), f32[256,128]{1,0:T(8,128)}) %reduce-scatter.5.cloned.1.call-update) | async-done | bytes 131088 | tf_op jit(solution)/shard_map/reduce_scatter | solution.py:28
  107.1 0.9 subtract_convert_fusion.2
  108.0 15.0 %all_gather.9 = bf16[2048,128]{1,0:T(8,128)(2,1)S(1)} all-gather(bf16[256,128]{1,0:T(8,128)(2,1)S(1)} %subtract_convert_fusion.2), channel_id=1, replica_groups=mesh['row'=4,'col'=8] {'col'}, dimensions={0}, use_global_device_ids=true | all-gather | bytes 589824 | tf_op jit(solution)/shard_map/all_gather | solution.py:35
  123.0 4.2 convolution_bitcast_fusion.3
  127.3 0.0 all-reduce.7.cloned.1.call-update
  127.3 0.2 reduce-scatter.7.cloned.1.call-start
  127.5 5.3 %copy.18 = bf16[256,8,4,256]{3,1,2,0:T(8,128)(2,1)} copy(bf16[256,8,4,256]{3,2,1,0:T(4,128)(2,1)} %bitcast.101) | data formatting | bytes 8388608
  132.9 3.0 copy.22
  135.9 35.2 %all-reduce.7.cloned.1.call-done = f32[1024,128]{1,0:T(8,128)} async-done(((f32[1024,128]{1,0:T(8,128)}), f32[1024,128]{1,0:T(8,128)}) %all-reduce.7.cloned.1.call-update) | async-done | bytes 524304 | tf_op jit(solution)/shard_map/psum | solution.py:43
  171.1 3.7 fusion.9
  174.9 2.2 fusion.1
  177.1 0.0 reduce-scatter.7.cloned.1.call-update
  177.1 0.0 all-reduce.9.cloned.1.call-start
  177.2 5.6 %copy.17 = bf16[128,8,8,256]{3,1,2,0:T(8,128)(2,1)} copy(bf16[128,8,8,256]{3,2,1,0:T(8,128)(2,1)} %bitcast.104) | data formatting | bytes 8388608
  182.8 26.8 %reduce-scatter.7.cloned.1.call-done = f32[256,128]{1,0:T(8,128)} async-done(((f32[2048,128]{1,0:T(8,128)}), f32[256,128]{1,0:T(8,128)}) %reduce-scatter.7.cloned.1.call-update) | async-done | bytes 131088 | tf_op jit(solution)/shard_map/reduce_scatter | solution.py:28
  209.6 0.9 subtract_convert_fusion.1
  210.6 15.0 %all_gather.10 = bf16[2048,128]{1,0:T(8,128)(2,1)S(1)} all-gather(bf16[256,128]{1,0:T(8,128)(2,1)S(1)} %subtract_convert_fusion.1), channel_id=1, replica_groups=mesh['row'=4,'col'=8] {'col'}, dimensions={0}, use_global_device_ids=true | all-gather | bytes 589824 | tf_op jit(solution)/shard_map/all_gather | solution.py:35
  225.6 4.2 convolution_bitcast_fusion.2
  229.8 0.0 all-reduce.9.cloned.1.call-update
  229.8 0.3 reduce-scatter.9.cloned.1.call-start
  230.1 5.4 %copy.16 = bf16[256,8,4,256]{3,1,2,0:T(8,128)(2,1)} copy(bf16[256,8,4,256]{3,2,1,0:T(4,128)(2,1)} %bitcast.99) | data formatting | bytes 8388608
  235.5 3.0 copy.23
  238.5 3.0 copy.24
  241.5 32.2 %all-reduce.9.cloned.1.call-done = f32[1024,128]{1,0:T(8,128)} async-done(((f32[1024,128]{1,0:T(8,128)}), f32[1024,128]{1,0:T(8,128)}) %all-reduce.9.cloned.1.call-update) | async-done | bytes 524304 | tf_op jit(solution)/shard_map/psum | solution.py:43
  273.7 3.7 fusion.2
  277.4 1.3 convolution_add_fusion.1
  278.7 0.9 copy-done.1
  279.6 2.2 fusion
  281.8 0.0 reduce-scatter.9.cloned.1.call-update
  281.9 0.0 all-reduce.11.cloned.1.call-start
  281.9 5.7 %copy.15 = bf16[128,8,8,256]{3,1,2,0:T(8,128)(2,1)} copy(bf16[128,8,8,256]{3,2,1,0:T(8,128)(2,1)} %bitcast.103) | data formatting | bytes 8388608
  287.6 0.1 broadcast_in_dim.31
  287.7 3.1 multiply_reduce_fusion
  290.8 21.1 %gather_fusion = bf16[4096,512]{1,0:T(8,128)(2,1)} fusion(bf16[6144,512]{1,0:T(8,128)(2,1)} %param.12, s32[4096]{0:T(1024)S(1)} %fusion.4), kind=kCustom, calls=%fused_computation | custom fusion | bytes 8404992 | tf_op jit(solution)/shard_map/jit(_take)/gather | solution.py:61
  311.9 3.4 multiply_reduce_fusion.1
  315.3 0.0 reduce-scatter.9.cloned.1.call-done
  315.3 0.9 subtract_convert_fusion
  316.3 15.0 %all_gather.11 = bf16[2048,128]{1,0:T(8,128)(2,1)S(1)} all-gather(bf16[256,128]{1,0:T(8,128)(2,1)S(1)} %subtract_convert_fusion), channel_id=1, replica_groups=mesh['row'=4,'col'=8] {'col'}, dimensions={0}, use_global_device_ids=true | all-gather | bytes 589824 | tf_op jit(solution)/shard_map/all_gather | solution.py:35
  331.3 4.3 convolution_bitcast_fusion.1
  335.6 0.0 reduce-scatter.11.cloned.1.call-start
  335.8 45.6 %all-reduce.11.cloned.1.call-done = f32[1024,128]{1,0:T(8,128)} async-done(((f32[1024,128]{1,0:T(8,128)}), f32[1024,128]{1,0:T(8,128)}) %all-reduce.11.cloned.1.call-update) | async-done | bytes 524304 | tf_op jit(solution)/shard_map/psum | solution.py:43
  381.3 1.1 convert_bitcast_fusion
  382.4 0.1 pad_maximum_fusion.1
  382.6 1.7 gather_fusion.1
  384.2 3.4 bitcast_select_fusion
  387.6 33.3 %convolution_convert_fusion = bf16[4096,128]{1,0:T(8,128)(2,1)} fusion(bf16[4096,128]{1,0:T(8,128)(2,1)S(1)} %bitcast_select_fusion, bf16[4096,512]{1,0:T(8,128)(2,1)} %bitcast.111, f32[4096]{0:T(1024)S(1)} %bitcast.118, f32[4096]{0:T(1024)S(1)} %multiply_reduce_fusion.1, bf16[4096,512]{1,0:T(8,128)(2,1)} %gather_fusion, pred[4096]{0:T(1024)(128)(4,1)S(1)} %compare_and_fusion), kind=kOutput, calls=%fused_computation.5 | convolution fusion | flops 21561344000 | bytes 10522624 | tf_op jit(solution)/shard_map/dot_general | solution.py:71
  420.9 1.5 pad_maximum_fusion
  422.4 31.1 %reduce-scatter.11.cloned.1.call-done = bf16[512,128]{1,0:T(8,128)(2,1)} async-done(((bf16[4096,128]{1,0:T(8,128)(2,1)}), bf16[512,128]{1,0:T(8,128)(2,1)}) %reduce-scatter.11.cloned.1.call-update) | async-done | bytes 131088 | tf_op jit(solution)/shard_map/reduce_scatter | solution.py:70
  453.4 1.6 convert_element_type.60
  (36 shorter events, 0.2 us)
Async XLA Ops:
  7.2 62.9 %all-reduce.5.cloned.1.call-start = ((), (), s32[]{:S(2)}) async-start(), calls=%async_computation.4 | async-start | bytes 1048576 | tf_op jit(solution)/shard_map/psum | solution.py:43
  18.0 1.6 copy-start.9
  21.8 85.3 %reduce-scatter.5.cloned.1.call-start = ((), (), s32[]{:S(2)}) async-start(), calls=%async_computation.5 | async-start | bytes 1179648 | tf_op jit(solution)/shard_map/reduce_scatter | solution.py:28
  74.6 96.5 %all-reduce.7.cloned.1.call-start = ((), (), s32[]{:S(2)}) async-start(), calls=%async_computation.6 | async-start | bytes 1048576 | tf_op jit(solution)/shard_map/psum | solution.py:43
  127.3 82.3 %reduce-scatter.7.cloned.1.call-start = ((), (), s32[]{:S(2)}) async-start(), calls=%async_computation.7 | async-start | bytes 1179648 | tf_op jit(solution)/shard_map/reduce_scatter | solution.py:28
  127.5 5.3 %copy-start.5 = (bf16[1,8,256,4,256]{4,3,2,1,0:T(4,128)(2,1)S(1)}, bf16[1,8,256,4,256]{4,3,2,1,0:T(4,128)(2,1)}, u32[]{:S(2)}) copy-start(bf16[1,8,256,4,256]{4,3,2,1,0:T(4,128)(2,1)} %get-tuple-element.4) | copy-start | bytes 12582916
  135.9 39.0 %copy-start.6 = (f32[1024,128]{1,0:T(8,128)S(1)}, f32[1024,128]{1,0:T(8,128)}, u32[]{:S(2)}) copy-start(f32[1024,128]{1,0:T(8,128)} %all-reduce.5.cloned.1.call-done) | copy-start | bytes 1572868
  171.1 3.7 copy-start.2
  177.1 96.6 %all-reduce.9.cloned.1.call-start = ((), (), s32[]{:S(2)}) async-start(), calls=%async_computation.8 | async-start | bytes 1048576 | tf_op jit(solution)/shard_map/psum | solution.py:43
  229.8 85.5 %reduce-scatter.9.cloned.1.call-start = ((), (), s32[]{:S(2)}) async-start(), calls=%async_computation.9 | async-start | bytes 1179648 | tf_op jit(solution)/shard_map/reduce_scatter | solution.py:28
  230.1 5.4 %copy-start.4 = (bf16[1,8,256,4,256]{4,3,2,1,0:T(4,128)(2,1)S(1)}, bf16[1,8,256,4,256]{4,3,2,1,0:T(4,128)(2,1)}, u32[]{:S(2)}) copy-start(bf16[1,8,256,4,256]{4,3,2,1,0:T(4,128)(2,1)} %get-tuple-element.7) | copy-start | bytes 12582916
  235.5 3.0 copy-start.3
  241.5 35.9 %copy-start.7 = (f32[1024,128]{1,0:T(8,128)S(1)}, f32[1024,128]{1,0:T(8,128)}, u32[]{:S(2)}) copy-start(f32[1024,128]{1,0:T(8,128)} %all-reduce.7.cloned.1.call-done) | copy-start | bytes 1572868
  273.7 3.7 copy-start
  277.4 2.2 copy-start.1
  281.9 99.5 %all-reduce.11.cloned.1.call-start = ((), (), s32[]{:S(2)}) async-start(), calls=%async_computation.10 | async-start | bytes 1048576 | tf_op jit(solution)/shard_map/psum | solution.py:43
  281.9 5.7 %copy-start.12 = (s32[16,1]{0,1:T(1,128)S(1)}, s32[16,1]{0,1:T(1,128)}, u32[]{:S(2)}) copy-start(s32[16,1]{0,1:T(1,128)} %param.11) | copy-start | bytes 196
  287.6 3.2 copy-start.11
  331.3 4.4 copy-start.8
  335.6 117.8 %reduce-scatter.11.cloned.1.call-start = ((), (), s32[]{:S(2)}) async-start(), calls=%async_computation.11 | async-start | bytes 1179648 | tf_op jit(solution)/shard_map/reduce_scatter | solution.py:70
  387.6 33.3 %copy-start.10 = (f32[1024,128]{1,0:T(8,128)S(1)}, f32[1024,128]{1,0:T(8,128)}, u32[]{:S(2)}) copy-start(f32[1024,128]{1,0:T(8,128)} %all-reduce.11.cloned.1.call-done) | copy-start | bytes 1572868
Sparse Core Ops, SparseCore 0:
  22.0 48.0 all-reduce.4
  74.7 32.3 reduce-scatter.4
  127.4 43.6 all-reduce.6
  177.2 32.3 reduce-scatter.6
  230.0 43.6 all-reduce.8
  282.0 32.1 reduce-scatter.8
  335.7 45.5 all-reduce.10
  421.0 32.3 reduce-scatter.10
where the time goes:
time: 471 us; the launch traced here: 462 us
  waiting for transfers between devices  226 us (48%)
  local copies, waits for them, and re-layouts  93.4 us (20%)
  matrix products  65.8 us (14%)
  blocking collectives  45 us (10%)
  other arithmetic  17 us (4%)
  between operations  14.8 us (3%)
    psum x4, waiting for transfers between devices, settle(): summed_rows = lax.psum(product_rows, 'row')  141 us
    reduce_scatter x3, waiting for transfers between devices, subtract(): lax.psum_scatter(partial_value, 'col', scatter_dimension=0, tiled=True)  53.6 us
    all_gather x3, blocking collectives, subtract(): return lax.all_gather(reduced, 'col', axis=0, tiled=True)  45 us
    unnamed x37, local copies, waits for them, and re-layouts  42.4 us
    dot_general x1, matrix products, shards(): jnp.dot(kernel, paired, preferred_element_type=jnp.float32)  33.3 us
    reduce_scatter x1, waiting for transfers between devices, shards(): lax.psum_scatter(jnp.dot(kernel, paired, preferred_element_type=jnp.float...  31.1 us
    gather x1, local copies, waits for them, and re-layouts, shards(): span_rows = jnp.take(test_pool, located, axis=0)  21.1 us
    dot_general x6, matrix products, shards(): jnp.dot(blocks[pair_slot(current, successor)], rounded[successor], prefer...  17.7 us
  transfers between devices with their start and end apart: 8, of which 7 were waited for; matrix products, arithmetic and copies ran while one was open for 19% of the time, Pallas kernels for 0%

commit v1 on v0

v1 whole, which is shorter than its diff:
```python
import math

import jax
import jax.numpy as jnp
from jax import lax
from jax.experimental import pallas as pl
from jax.experimental.pallas import tpu as pltpu
from jax.sharding import PartitionSpec as P

inverse_width = 0.35
log2e = math.log2(math.e)
scale = -inverse_width * log2e
bf16 = jnp.bfloat16
f32 = jnp.float32
vmem = pl.BlockSpec(memory_space=pltpu.VMEM)
anywhere = pl.BlockSpec(memory_space=pl.ANY)


def params(mib=48):
    return pltpu.CompilerParams(vmem_limit_bytes=mib * 2**20)


def pair_slot(early, successor):
    return successor * (successor - 1) // 2 + early


def panel_product(blocks, slot, vector, earlier, out_dtype, name):
    _, groups, rows, inner, width = blocks.shape
    depth = inner * width
    out_width = vector.shape[1]

    def body(*refs):
        if earlier is None:
            block_ref, vector_ref, out_ref, held, sem = refs
        else:
            block_ref, vector_ref, earlier_ref, out_ref, held, sem = refs
        copies = [
            pltpu.make_async_copy(block_ref.at[slot, g], held.at[g], sem.at[g]) for g in range(groups)
        ]
        for copy in copies:
            copy.start()
        for g in range(groups):
            copies[g].wait()
            at = pl.ds(g * rows, rows)
            value = jnp.dot(
                held[g].reshape(rows, depth), vector_ref[...], preferred_element_type=f32
            )
            if earlier is not None:
                value = value + earlier_ref[at, :]
            out_ref[at, :] = value.astype(out_dtype)

    operands = [blocks, vector] + ([] if earlier is None else [earlier])
    return pl.pallas_call(
        body,
        in_specs=[anywhere] + [vmem] * (len(operands) - 1),
        out_specs=vmem,
        out_shape=jax.ShapeDtypeStruct((groups * rows, out_width), out_dtype),
        scratch_shapes=[
            pltpu.VMEM((groups, rows, inner, width), bf16),
            pltpu.SemaphoreType.DMA((groups,)),
        ],
        compiler_params=params(),
        cost_estimate=pl.CostEstimate(
            flops=4 * groups * rows * depth * out_width,
            bytes_accessed=2 * groups * rows * depth,
            transcendentals=0,
        ),
        name=name,
    )(*operands)


def kernel_values(span, center, center_sq, test_sq):
    crossed = lax.dot_general(
        span, center, (((1,), (1,)), ((), ())), preferred_element_type=f32
    )
    reps = center.shape[0] // test_sq.shape[1]
    test_part = jnp.concatenate([test_sq] * reps, axis=1)
    return jnp.exp2((crossed * (-2.0 * scale) + center_sq) + test_part).astype(bf16)


def kernel_block(span, centers, center_sq, slots, name):
    tests, dim = span.shape
    tiles = slots.shape[0]
    size = centers.shape[1]
    step = min(512, tests)

    def body(slots_ref, span_ref, *refs):
        center_refs, sq_refs = refs[:tiles], refs[tiles : 2 * tiles]
        out_ref, norm_ref = refs[2 * tiles :]
        rows = span_ref[...]
        wide = rows.astype(f32)
        norm = scale * jnp.sum(wide * wide, axis=1, keepdims=True)
        norm = jnp.broadcast_to(norm, norm_ref.shape)
        norm_ref[...] = norm
        for t in range(tiles):
            out_ref[:, t * size : (t + 1) * size] = kernel_values(
                rows, center_refs[t][0], sq_refs[t][0], norm
            )

    center_specs = [
        pl.BlockSpec((1, size, dim), lambda i, s, t=t: (s[t], 0, 0)) for t in range(tiles)
    ]
    sq_specs = [pl.BlockSpec((1, 1, size), lambda i, s, t=t: (s[t], 0, 0)) for t in range(tiles)]
    return pl.pallas_call(
        body,
        grid_spec=pltpu.PrefetchScalarGridSpec(
            num_scalar_prefetch=1,
            grid=(tests // step,),
            in_specs=[pl.BlockSpec((step, dim), lambda i, s: (i, 0))] + center_specs + sq_specs,
            out_specs=[
                pl.BlockSpec((step, tiles * size), lambda i, s: (i, 0)),
                pl.BlockSpec((step, 128), lambda i, s: (i, 0)),
            ],
        ),
        out_shape=[
            jax.ShapeDtypeStruct((tests, tiles * size), bf16),
            jax.ShapeDtypeStruct((tests, 128), f32),
        ],
        compiler_params=params(),
        cost_estimate=pl.CostEstimate(
            flops=3 * tests * tiles * size * dim,
            bytes_accessed=2 * tests * tiles * size,
            transcendentals=tests * tiles * size,
        ),
        name=name,
    )(slots, span, *([centers] * tiles), *([center_sq] * tiles))


def scored_block(span, norms, centers, center_sq, slots, weights, earlier, name):
    tests, dim = span.shape
    tiles = slots.shape[0]
    size = centers.shape[1]
    width = weights.shape[1]
    step = min(512, tests)
    more = 0 if earlier is None else 1

    def body(slots_ref, span_ref, norm_ref, weight_ref, *refs):
        center_refs, sq_refs = refs[:tiles], refs[tiles : 2 * tiles]
        out_ref = refs[-1]
        rows = span_ref[...]
        norm = norm_ref[...]
        total = refs[2 * tiles][...] if more else None
        for t in range(tiles):
            values = kernel_values(rows, center_refs[t][0], sq_refs[t][0], norm)
            part = jnp.dot(
                values, weight_ref[t * size : (t + 1) * size, :], preferred_element_type=f32
            )
            total = part if total is None else total + part
        out_ref[...] = total

    center_specs = [
        pl.BlockSpec((1, size, dim), lambda i, s, t=t: (s[t], 0, 0)) for t in range(tiles)
    ]
    sq_specs = [pl.BlockSpec((1, 1, size), lambda i, s, t=t: (s[t], 0, 0)) for t in range(tiles)]
    row_spec = pl.BlockSpec((step, width), lambda i, s: (i, 0))
    return pl.pallas_call(
        body,
        grid_spec=pltpu.PrefetchScalarGridSpec(
            num_scalar_prefetch=1,
            grid=(tests // step,),
            in_specs=[
                pl.BlockSpec((step, dim), lambda i, s: (i, 0)),
                pl.BlockSpec((step, 128), lambda i, s: (i, 0)),
                pl.BlockSpec(weights.shape, lambda i, s: (0, 0)),
            ]
            + center_specs
            + sq_specs
            + [row_spec] * more,
            out_specs=row_spec,
        ),
        out_shape=jax.ShapeDtypeStruct((tests, width), f32),
        compiler_params=params(),
        cost_estimate=pl.CostEstimate(
            flops=3 * tests * tiles * size * (dim + 2 * width),
            bytes_accessed=2 * (tests + tiles * size) * dim,
            transcendentals=tests * tiles * size,
        ),
        name=name,
    )(
        slots, span, norms, weights, *([centers] * tiles), *([center_sq] * tiles),
        *([earlier] if more else []),
    )


def final_block(kernel, weights, earlier, name):
    tests, depth = kernel.shape
    width = weights.shape[1]
    step = min(1024, tests)

    def body(kernel_ref, weight_ref, earlier_ref, out_ref):
        value = jnp.dot(kernel_ref[...], weight_ref[...], preferred_element_type=f32)
        out_ref[...] = (value + earlier_ref[...]).astype(bf16)

    return pl.pallas_call(
        body,
        grid=(tests // step,),
        in_specs=[
            pl.BlockSpec((step, depth), lambda i: (i, 0)),
            pl.BlockSpec((depth, width), lambda i: (0, 0)),
            pl.BlockSpec((step, width), lambda i: (i, 0)),
        ],
        out_specs=pl.BlockSpec((step, width), lambda i: (i, 0)),
        out_shape=jax.ShapeDtypeStruct((tests, width), bf16),
        compiler_params=params(),
        cost_estimate=pl.CostEstimate(
            flops=4 * tests * depth * width, bytes_accessed=2 * tests * depth, transcendentals=0
        ),
        name=name,
    )(kernel, weights, earlier)


def swap(value, axis, mask):
    size = lax.axis_size(axis)
    return lax.ppermute(value, axis, [(i, i ^ mask) for i in range(size)])


def added(left, right):
    return left.astype(f32) + right.astype(f32)


def parted(value, pick):
    half = value.shape[0] // 2
    return (
        lax.dynamic_slice_in_dim(value, pick * half, half, 0),
        lax.dynamic_slice_in_dim(value, (1 - pick) * half, half, 0),
    )


def joined(mine, other, pick):
    first = jnp.where(pick == 0, mine, other)
    second = jnp.where(pick == 0, other, mine)
    return jnp.concatenate([first, second], axis=0)


def col_picks():
    size = lax.axis_size("col")
    bits = size.bit_length() - 1
    place = lax.axis_index("col")
    bit = [(place >> j) & 1 for j in range(bits)]
    picks = [(1 << j, bit[j]) for j in range(bits - 1)]
    last = 1 << (bits - 1)
    if bits >= 3:
        picks[-1] = (1 << (bits - 2), bit[bits - 2] ^ bit[bits - 1])
        last = last | (1 << (bits - 2))
    return picks, last


def row_sum(partial):
    bits = lax.axis_size("row").bit_length() - 1
    half = partial.shape[0] // 2
    parts = [partial[:half], partial[half:]]
    orders = [list(range(bits)), list(range(bits))[::-1]]
    for j in range(bits):
        received = [swap(p, "row", 1 << o[j]) for p, o in zip(parts, orders)]
        parts = [added(p, r) for p, r in zip(parts, received)]
        if j < bits - 1:
            parts = [p.astype(bf16) for p in parts]
    return jnp.concatenate(parts, axis=0)


def subtracted(targets, partial):
    picks, last = col_picks()
    total, own = partial, targets
    for mask, pick in picks:
        mine, other = parted(total, pick)
        total = added(mine, swap(other, "col", mask)).astype(bf16)
        own = parted(own, pick)[0]
    total = added(total, swap(total, "col", last))
    value = (own.astype(f32) - total).astype(bf16)
    for mask, pick in picks[::-1]:
        value = joined(value, swap(value, "col", mask), pick)
    return value


def scattered(partial):
    size = lax.axis_size("col")
    place = lax.axis_index("col")
    bits = size.bit_length() - 1
    height = partial.shape[0] // size
    total = partial.reshape((2,) * bits + (height, partial.shape[1]))
    total = total.transpose(tuple(range(bits))[::-1] + (bits, bits + 1))
    total = total.reshape(partial.shape)
    for j in range(bits):
        mine, other = parted(total, (place >> j) & 1)
        total = added(mine, swap(other, "col", 1 << j))
        if j < bits - 1:
            total = total.astype(bf16)
    return total


def shards(factor_blocks, inverse_blocks, right_side, centers, owner_map, test_pool, test_rows):
    panels = inverse_blocks.shape[0]
    col_tiles = inverse_blocks.shape[1]
    tile_size = inverse_blocks.shape[2]
    row_tiles = inverse_blocks.shape[3]
    width_out = right_side.shape[3]
    own_rows = row_tiles * tile_size
    targets = right_side.reshape(panels, own_rows, width_out)
    tests = test_rows.shape[0]
    chunks = 4
    chunk = tests // chunks

    slots = jnp.argsort(owner_map[:, 0]).astype(jnp.int32)
    located = test_rows - lax.axis_index("row") * test_pool.shape[0]
    span = [
        test_pool.at[located[i * chunk : (i + 1) * chunk]].get(mode="promise_in_bounds")
        for i in range(chunks)
    ]
    center_sq = scale * jnp.sum(jnp.square(centers.astype(f32)), axis=2)
    center_sq = center_sq[:, None, :]

    def panel_slots(k):
        return slots[k * col_tiles : (k + 1) * col_tiles]

    first = [
        kernel_block(span[i], centers, center_sq, panel_slots(0), f"kernel_0_{i}")
        for i in range(chunks)
    ]
    totals = [None] * chunks
    solved = [None] * panels
    rounded = [None] * panels
    partial = [None] * panels
    for k in range(panels - 1, -1, -1):
        if k == panels - 1:
            residue = targets[k]
        else:
            residue = subtracted(targets[k], partial[k])
        product = panel_product(inverse_blocks, k, residue, None, bf16, f"inverse_{k}")
        solved[k] = row_sum(product)
        rounded[k] = solved[k].astype(bf16)
        for early in range(k - 1, -1, -1):
            partial[early] = panel_product(
                factor_blocks,
                pair_slot(early, k),
                rounded[k],
                partial[early],
                bf16 if early == k - 1 else f32,
                f"factor_{early}_{k}",
            )
        if k > 0:
            totals = [
                scored_block(
                    span[i], first[i][1], centers, center_sq, panel_slots(k), rounded[k], totals[i],
                    f"scored_{k}_{i}",
                )
                for i in range(chunks)
            ]
    estimate = jnp.concatenate(
        [final_block(first[i][0], rounded[0], totals[i], f"final_{i}") for i in range(chunks)], axis=0
    )
    estimate = scattered(estimate)
    alpha = jnp.stack(solved).reshape(panels, col_tiles, tile_size, width_out)
    return (alpha, estimate)


def solution(mesh):
    in_specs = (
        P(None, None, "row", None, "col"),
        P(None, None, "col", None, "row"),
        P(None, None, "row", None),
        P(None, "col", None),
        P(None, "col"),
        P("row", None),
        P("row"),
    )
    out_specs = (P(None, None, "col", None), P(("row", "col"), None))
    return jax.shard_map(shards, mesh=mesh, in_specs=in_specs, out_specs=out_specs, check_vma=False)
```

time: 471 us -> 269 us (0.57)
  waiting for transfers between devices: 226 us -> 51.7 us
  Pallas kernels: 0 us -> 114 us
  matrix products: 65.8 us -> 0 us
  local copies, waits for them, and re-layouts: 93.4 us -> 42.4 us
  blocking collectives: 45 us -> 0 us
  starting transfers between devices: 0.72 us -> 43.8 us
  between operations: 14.8 us -> 1.84 us
  other arithmetic: 17 us -> 11.5 us
    psum x4 -> x0, waiting for transfers between devices: 141 us -> none  [settle(): summed_rows = lax.psum(product_rows, 'row')]
    pallas_call x0 -> x30, Pallas kernels: none -> 114 us  [the longest x12 52.1 us: scored_block(): pl.pallas_call(body, grid_spec=pltpu.PrefetchScalarGridSpec(num_scalar_pr...]
    reduce_scatter x4 -> x0, waiting for transfers between devices: 84.6 us -> none  [the longest x3 53.6 us: subtract(): lax.psum_scatter(partial_value, 'col', scatter_dimension=0, tiled=True)]
    dot_general x11 -> x0, matrix products: 65.8 us -> none  [the longest x1 33.3 us: shards(): jnp.dot(kernel, paired, preferred_element_type=jnp.float32)]
    ppermute x0 -> x34, waiting for transfers between devices: none -> 51.7 us  [swap(): return lax.ppermute(value, axis, [(i, i ^ mask) for i in range(size)])]
    all_gather x3 -> x0, blocking collectives: 45 us -> none  [subtract(): return lax.all_gather(reduced, 'col', axis=0, tiled=True)]
    ppermute x0 -> x34, starting transfers between devices: none -> 43.8 us  [swap(): return lax.ppermute(value, axis, [(i, i ^ mask) for i in range(size)])]
    unnamed x37 -> x48, local copies, waits for them, and re-layouts: 42.4 us -> 6.28 us
  transfers between devices with their start and end apart: 8 -> 34, of which waited for: 7 -> 20; matrix products, arithmetic and copies ran while one was open for 19% -> 14% of each run, Pallas kernels for 0% -> 29%
where the time goes in v1:
time: 269 us; the launch traced here: 265 us
  Pallas kernels  114 us (42%)
  waiting for transfers between devices  51.7 us (19%)
  starting transfers between devices  43.8 us (16%)
  local copies, waits for them, and re-layouts  42.4 us (16%)
  other arithmetic  11.5 us (4%)
    pallas_call x12, Pallas kernels, scored_block(): pl.pallas_call(body, grid_spec=pltpu.PrefetchScalarGridSpec(num_scalar_pr...  52.1 us
    ppermute x34, waiting for transfers between devices, swap(): return lax.ppermute(value, axis, [(i, i ^ mask) for i in range(size)])  51.7 us
    pallas_call x10, Pallas kernels, panel_product(): pl.pallas_call(body, in_specs=[anywhere] + [vmem] * (len(operands) - 1),...  45.3 us
    ppermute x34, starting transfers between devices, swap(): return lax.ppermute(value, axis, [(i, i ^ mask) for i in range(size)])  43.8 us
    gather x4, local copies, waits for them, and re-layouts, shards(): test_pool.at[located[i * chunk:(i + 1) * chunk]]  31.5 us
    pallas_call x4, Pallas kernels, kernel_block(): pl.pallas_call(body, grid_spec=pltpu.PrefetchScalarGridSpec(num_scalar_pr...  13.5 us
    unnamed x48, local copies, waits for them, and re-layouts  6.28 us
  transfers between devices with their start and end apart: 34, of which 20 were waited for; matrix products, arithmetic and copies ran while one was open for 14% of the time, Pallas kernels for 29%

profile of v1, /device:TPU:0, one launch (start us, length us, event | category | flops | bytes accessed | tf_op | source)
XLA Modules:
  0.0 264.9 jit_solution(8572684434463069251)
XLA Ops:
  0.6 2.7 %fusion.8 = (bf16[1,8,256,128]{3,2,1,0:T(8,128)(2,1)}, bf16[1,8,256,128]{3,2,1,0:T(8,128)(2,1)}, bf16[1,8,256,128]{3,2,1,0:T(8,128)(2,1)S(1)}, bf16[1,8,256,128]{3,2,1,0:T(8,128)(2,1)S(1)}) fusion(bf16[4,8,256,128]{3,2,1,0:T(8,128)(2,1)} %param.9), kind=kLoop, calls=%fused_computation.80 | loop fusion | bytes 4194304 | tf_op jit(solution)/shard_map/slice | solution.py:327
  3.4 3.3 %inverse_3.1 = bf16[1024,128]{1,0:T(8,128)(2,1)S(1)} custom-call(bf16[4,4,256,8,256]{4,3,2,1,0:T(8,128)(2,1)} %refs_0_.35, bf16[2048,128]{1,0:T(8,128)(2,1)S(1)} %bitcast.13), custom_call_target="tpu_custom_call" | custom-call | flops 1073741824 | bytes 4194304 | tf_op jit(solution)/shard_map/inverse_3/pallas_call | solution.py:53
  6.7 3.0 %collective-permute-start = (bf16[512,128]{1,0:T(8,128)(2,1)S(1)}, bf16[512,128]{1,0:T(8,128)(2,1)S(1)}, u32[]{:S(2)}, u32[]{:S(2)}) collective-permute-start(bf16[512,128]{1,0:T(8,128)(2,1)S(1)} %get-tuple-element.50), channel_id=1, source_target_pairs={{0,8},{8,0},{16,24},{24,16},{1,9},{9,1},{17,25},{25,17},{2,10},{10... | collective-permute-start | bytes 393224 | tf_op jit(solution)/shard_map/ppermute | solution.py:214
  9.7 1.5 collective-permute-start.2
  11.2 2.0 collective-permute-done
  13.2 1.5 collective-permute-done.2
  15.1 1.7 collective-permute-start.1
  16.8 2.9 %collective-permute-done.3 = bf16[512,128]{1,0:T(8,128)(2,1)S(1)} collective-permute-done((bf16[512,128]{1,0:T(8,128)(2,1)S(1)}, bf16[512,128]{1,0:T(8,128)(2,1)S(1)}, u32[]{:S(2)}, u32[]{:S(2)}) %collective-permute-start.3) | collective-permute-done | bytes 131104 | tf_op jit(solution)/shard_map/ppermute | solution.py:214
  21.2 3.6 %factor_2_3.1 = bf16[2048,128]{1,0:T(8,128)(2,1)S(1)} custom-call(bf16[6,8,256,4,256]{4,3,2,1,0:T(4,128)(2,1)} %refs_0_.34, bf16[1024,128]{1,0:T(8,128)(2,1)S(1)} %fusion.7.refs_1_.weight_ref), custom_call_target="tpu_custom_call" | custom-call | flops 1073741824 | bytes 4194304 | tf_op jit(solution)/shard_map/factor_2_3/pallas_call | solution.py:53
  24.9 1.5 collective-permute-done.4
  26.5 1.6 collective-permute-start.5
  28.2 4.0 %collective-permute-done.5 = bf16[512,128]{1,0:T(8,128)(2,1)S(1)} collective-permute-done((bf16[512,128]{1,0:T(8,128)(2,1)S(1)}, bf16[512,128]{1,0:T(8,128)(2,1)S(1)}, u32[]{:S(2)}, u32[]{:S(2)}) %collective-permute-start.5) | collective-permute-done | bytes 131104 | tf_op jit(solution)/shard_map/ppermute | solution.py:214
  32.2 3.7 %collective-permute-start.6 = (bf16[512,128]{1,0:T(8,128)(2,1)S(1)}, bf16[512,128]{1,0:T(8,128)(2,1)S(1)}, u32[]{:S(2)}, u32[]{:S(2)}) collective-permute-start(bf16[512,128]{1,0:T(8,128)(2,1)S(1)} %add_convert_fusion.13), channel_id=1, source_target_pairs={{0,6},{1,7},{2,4},{3,5},{4,2},{5,3},{6,0},{7,1},{8,14},{9,15},{10,... | collective-permute-start | bytes 393224 | tf_op jit(solution)/shard_map/ppermute | solution.py:214
  35.9 3.2 %collective-permute-done.6 = bf16[512,128]{1,0:T(8,128)(2,1)S(1)} collective-permute-done((bf16[512,128]{1,0:T(8,128)(2,1)S(1)}, bf16[512,128]{1,0:T(8,128)(2,1)S(1)}, u32[]{:S(2)}, u32[]{:S(2)}) %collective-permute-start.6) | collective-permute-done | bytes 131104 | tf_op jit(solution)/shard_map/ppermute | solution.py:214
  39.1 2.3 collective-permute-start.7
  41.5 2.9 %collective-permute-done.7 = bf16[512,128]{1,0:T(8,128)(2,1)S(1)} collective-permute-done((bf16[512,128]{1,0:T(8,128)(2,1)S(1)}, bf16[512,128]{1,0:T(8,128)(2,1)S(1)}, u32[]{:S(2)}, u32[]{:S(2)}) %collective-permute-start.7) | collective-permute-done | bytes 131104 | tf_op jit(solution)/shard_map/ppermute | solution.py:214
  44.6 3.1 %multiply_reduce_fusion = f32[16,256]{1,0:T(8,128)S(1)} fusion(bf16[16,256,512]{2,1,0:T(8,128)(2,1)} %refs_3_.31), kind=kLoop, calls=%fused_computation.4 | loop fusion | flops 6287360 | bytes 4210688 | tf_op jit(solution)/shard_map/reduce_sum | solution.py:309
  47.9 3.3 %inverse_2.1 = bf16[1024,128]{1,0:T(8,128)(2,1)S(1)} custom-call(bf16[4,4,256,8,256]{4,3,2,1,0:T(8,128)(2,1)} %refs_0_.35, bf16[2048,128]{1,0:T(8,128)(2,1)S(1)} %pad_maximum_fusion.3.refs_1_), custom_call_target="tpu_custom_call" | custom-call | flops 1073741824 | bytes 4194304 | tf_op jit(solution)/shard_map/inverse_2/pallas_call | solution.py:53
  51.2 1.4 collective-permute-start.9
  52.6 1.5 collective-permute-start.11
  54.1 3.0 %collective-permute-done.9 = bf16[512,128]{1,0:T(8,128)(2,1)S(1)} collective-permute-done((bf16[512,128]{1,0:T(8,128)(2,1)S(1)}, bf16[512,128]{1,0:T(8,128)(2,1)S(1)}, u32[]{:S(2)}, u32[]{:S(2)}) %collective-permute-start.9) | collective-permute-done | bytes 131104 | tf_op jit(solution)/shard_map/ppermute | solution.py:214
  60.3 3.5 %factor_1_3.1.refs_2_ = f32[2048,128]{1,0:T(8,128)S(1)} custom-call(bf16[6,8,256,4,256]{4,3,2,1,0:T(4,128)(2,1)} %refs_0_.34, bf16[1024,128]{1,0:T(8,128)(2,1)S(1)} %fusion.7.refs_1_.weight_ref), custom_call_target="tpu_custom_call" | custom-call | flops 1073741824 | bytes 4194304 | tf_op jit(solution)/shard_map/factor_1_3/pallas_call | solution.py:53
  63.9 1.6 collective-permute-start.10
  65.5 3.4 %collective-permute-done.10 = bf16[512,128]{1,0:T(8,128)(2,1)S(1)} collective-permute-done((bf16[512,128]{1,0:T(8,128)(2,1)S(1)}, bf16[512,128]{1,0:T(8,128)(2,1)S(1)}, u32[]{:S(2)}, u32[]{:S(2)}) %collective-permute-start.10) | collective-permute-done | bytes 131104 | tf_op jit(solution)/shard_map/ppermute | solution.py:214
  69.7 14.4 %factor_1_2.1 = bf16[2048,128]{1,0:T(8,128)(2,1)S(1)} custom-call(bf16[6,8,256,4,256]{4,3,2,1,0:T(4,128)(2,1)} %refs_0_.34, bf16[1024,128]{1,0:T(8,128)(2,1)S(1)} %fusion.6.refs_1_.weight_ref, f32[2048,128]{1,0:T(8,128)S(1)} %factor_1_3.1.refs_2_), custom_call_target="tpu_custom_call" | custom-call | flops 1073741824 | bytes 4194304 | tf_op jit(solution)/shard_map/factor_1_2/pallas_call | solution.py:53
  85.0 8.7 %gather_fusion.3 = bf16[1024,512]{1,0:T(8,128)(2,1)} fusion(bf16[6144,512]{1,0:T(8,128)(2,1)} %param.12, s32[1024]{0:T(1024)S(1)} %get-tuple-element.53), kind=kCustom, calls=%fused_computation.3 | custom fusion | bytes 2101248 | tf_op jit(solution)/shard_map/gather | solution.py:306
  93.7 7.6 %gather_fusion.2 = bf16[1024,512]{1,0:T(8,128)(2,1)S(1)} fusion(bf16[6144,512]{1,0:T(8,128)(2,1)} %param.12, s32[1024]{0:T(1024)S(1)} %get-tuple-element.54), kind=kCustom, calls=%fused_computation.2 | custom fusion | bytes 2101248 | tf_op jit(solution)/shard_map/gather | solution.py:306
  101.3 7.6 %gather_fusion.1 = bf16[1024,512]{1,0:T(8,128)(2,1)S(1)} fusion(bf16[6144,512]{1,0:T(8,128)(2,1)} %param.12, s32[1024]{0:T(1024)S(1)} %get-tuple-element.55), kind=kCustom, calls=%fused_computation.1 | custom fusion | bytes 2101248 | tf_op jit(solution)/shard_map/gather | solution.py:306
  108.9 7.6 %gather_fusion = bf16[1024,512]{1,0:T(8,128)(2,1)S(1)} fusion(bf16[6144,512]{1,0:T(8,128)(2,1)} %param.12, s32[1024]{0:T(1024)S(1)} %get-tuple-element.52), kind=kCustom, calls=%fused_computation | custom fusion | bytes 2101248 | tf_op jit(solution)/shard_map/gather | solution.py:306
  117.7 3.3 %kernel_0_3.1 = (bf16[1024,1024]{1,0:T(8,128)(2,1)S(1)}, f32[1024,128]{1,0:T(8,128)S(1)}) custom-call(s32[4]{0:T(128)S(1)} %get-tuple-element.59.slots_ref, bf16[1024,512]{1,0:T(8,128)(2,1)S(1)} %copy-done, bf16[16,256,512]{2,1,0:T(8,128)(2,1)} %refs_3_.31, bf16[16,256,512]{2,1,0:T(8,128)(2,1)} %refs_3_.31, bf16[16,256,512]{2,1,0:T(8,128)(2,1)} %refs_3_.31, ...), custom_call_target="tpu_custom_call" | custom-call | flops 1610612736 | bytes 2097152 | tf_op jit(solution)/shard_map/kernel_0_3/pallas_call | solution.py:104
  122.2 2.1 collective-permute-start.14
  124.3 3.4 %kernel_0_2.1 = (bf16[1024,1024]{1,0:T(8,128)(2,1)S(1)}, f32[1024,128]{1,0:T(8,128)S(1)}) custom-call(s32[4]{0:T(128)S(1)} %get-tuple-element.59.slots_ref, bf16[1024,512]{1,0:T(8,128)(2,1)S(1)} %gather_fusion.2, bf16[16,256,512]{2,1,0:T(8,128)(2,1)} %refs_3_.31, bf16[16,256,512]{2,1,0:T(8,128)(2,1)} %refs_3_.31, bf16[16,256,512]{2,1,0:T(8,128)(2,1)} %refs_3_.31, ...), custom_call_target="tpu_custom_call" | custom-call | flops 1610612736 | bytes 2097152 | tf_op jit(solution)/shard_map/kernel_0_2/pallas_call | solution.py:104
  128.5 3.1 %collective-permute-start.15 = (bf16[512,128]{1,0:T(8,128)(2,1)S(1)}, bf16[512,128]{1,0:T(8,128)(2,1)S(1)}, u32[]{:S(2)}, u32[]{:S(2)}) collective-permute-start(bf16[512,128]{1,0:T(8,128)(2,1)S(1)} %add_convert_fusion.10), channel_id=1, source_target_pairs={{0,6},{1,7},{2,4},{3,5},{4,2},{5,3},{6,0},{7,1},{8,14},{9,15},{10,... | collective-permute-start | bytes 393224 | tf_op jit(solution)/shard_map/ppermute | solution.py:214
  131.6 3.4 %kernel_0_1.1 = (bf16[1024,1024]{1,0:T(8,128)(2,1)S(1)}, f32[1024,128]{1,0:T(8,128)S(1)}) custom-call(s32[4]{0:T(128)S(1)} %get-tuple-element.59.slots_ref, bf16[1024,512]{1,0:T(8,128)(2,1)S(1)} %gather_fusion.1, bf16[16,256,512]{2,1,0:T(8,128)(2,1)} %refs_3_.31, bf16[16,256,512]{2,1,0:T(8,128)(2,1)} %refs_3_.31, bf16[16,256,512]{2,1,0:T(8,128)(2,1)} %refs_3_.31, ...), custom_call_target="tpu_custom_call" | custom-call | flops 1610612736 | bytes 2097152 | tf_op jit(solution)/shard_map/kernel_0_1/pallas_call | solution.py:104
  136.8 2.6 collective-permute-start.16
  139.4 3.4 %kernel_0_0.1 = (bf16[1024,1024]{1,0:T(8,128)(2,1)S(1)}, f32[1024,128]{1,0:T(8,128)S(1)}) custom-call(s32[4]{0:T(128)S(1)} %get-tuple-element.59.slots_ref, bf16[1024,512]{1,0:T(8,128)(2,1)S(1)} %gather_fusion, bf16[16,256,512]{2,1,0:T(8,128)(2,1)} %refs_3_.31, bf16[16,256,512]{2,1,0:T(8,128)(2,1)} %refs_3_.31, bf16[16,256,512]{2,1,0:T(8,128)(2,1)} %refs_3_.31, ...), custom_call_target="tpu_custom_call" | custom-call | flops 1610612736 | bytes 2097152 | tf_op jit(solution)/shard_map/kernel_0_0/pallas_call | solution.py:104
  144.3 4.1 %scored_3_3.1.refs_8_ = f32[1024,128]{1,0:T(8,128)S(1)} custom-call(s32[4]{0:T(128)S(1)} %get-tuple-element.56.slots_ref, bf16[1024,512]{1,0:T(8,128)(2,1)S(1)} %copy-done.1, f32[1024,128]{1,0:T(8,128)S(1)} %get-tuple-element.19.norm_ref, bf16[1024,128]{1,0:T(8,128)(2,1)S(1)} %fusion.7.refs_1_.weight_ref, bf16[16,256,512]{2,1,0:T(8,128)(2,1)} %refs_3_.31, ...), custom_call_target="tpu_custom_call" | custom-call | flops 2415919104 | bytes 2097152 | tf_op jit(solution)/shard_map/scored_3_3/pallas_call | solution.py:156
  148.4 4.2 %scored_3_2.1.refs_8_ = f32[1024,128]{1,0:T(8,128)S(1)} custom-call(s32[4]{0:T(128)S(1)} %get-tuple-element.56.slots_ref, bf16[1024,512]{1,0:T(8,128)(2,1)S(1)} %gather_fusion.2, f32[1024,128]{1,0:T(8,128)S(1)} %get-tuple-element.17.norm_ref, bf16[1024,128]{1,0:T(8,128)(2,1)S(1)} %fusion.7.refs_1_.weight_ref, bf16[16,256,512]{2,1,0:T(8,128)(2,1)} %refs_3_.31, ...), custom_call_target="tpu_custom_call" | custom-call | flops 2415919104 | bytes 2097152 | tf_op jit(solution)/shard_map/scored_3_2/pallas_call | solution.py:156
  152.7 3.3 %inverse_1.1 = bf16[1024,128]{1,0:T(8,128)(2,1)S(1)} custom-call(bf16[4,4,256,8,256]{4,3,2,1,0:T(8,128)(2,1)} %refs_0_.35, bf16[2048,128]{1,0:T(8,128)(2,1)S(1)} %pad_maximum_fusion.5.refs_1_), custom_call_target="tpu_custom_call" | custom-call | flops 1073741824 | bytes 4194304 | tf_op jit(solution)/shard_map/inverse_1/pallas_call | solution.py:53
  156.0 1.4 collective-permute-start.18
  157.4 1.5 collective-permute-start.20
  159.0 4.6 %scored_3_1.1.refs_8_ = f32[1024,128]{1,0:T(8,128)S(1)} custom-call(s32[4]{0:T(128)S(1)} %get-tuple-element.56.slots_ref, bf16[1024,512]{1,0:T(8,128)(2,1)S(1)} %gather_fusion.1, f32[1024,128]{1,0:T(8,128)S(1)} %get-tuple-element.15.norm_ref, bf16[1024,128]{1,0:T(8,128)(2,1)S(1)} %fusion.7.refs_1_.weight_ref, bf16[16,256,512]{2,1,0:T(8,128)(2,1)} %refs_3_.31, ...), custom_call_target="tpu_custom_call" | custom-call | flops 2415919104 | bytes 2097152 | tf_op jit(solution)/shard_map/scored_3_1/pallas_call | solution.py:156
  164.4 3.5 %factor_0_3.1.refs_2_ = f32[2048,128]{1,0:T(8,128)S(1)} custom-call(bf16[6,8,256,4,256]{4,3,2,1,0:T(4,128)(2,1)} %refs_0_.34, bf16[1024,128]{1,0:T(8,128)(2,1)S(1)} %fusion.7.refs_1_.weight_ref), custom_call_target="tpu_custom_call" | custom-call | flops 1073741824 | bytes 4194304 | tf_op jit(solution)/shard_map/factor_0_3/pallas_call | solution.py:53
  168.0 3.6 %factor_0_2.1.refs_2_ = f32[2048,128]{1,0:T(8,128)S(1)} custom-call(bf16[6,8,256,4,256]{4,3,2,1,0:T(4,128)(2,1)} %refs_0_.34, bf16[1024,128]{1,0:T(8,128)(2,1)S(1)} %copy-done.3, f32[2048,128]{1,0:T(8,128)S(1)} %factor_0_3.1.refs_2_), custom_call_target="tpu_custom_call" | custom-call | flops 1073741824 | bytes 4194304 | tf_op jit(solution)/shard_map/factor_0_2/pallas_call | solution.py:53
  172.6 4.0 %collective-permute-done.19 = bf16[512,128]{1,0:T(8,128)(2,1)S(1)} collective-permute-done((bf16[512,128]{1,0:T(8,128)(2,1)S(1)}, bf16[512,128]{1,0:T(8,128)(2,1)S(1)}, u32[]{:S(2)}, u32[]{:S(2)}) %collective-permute-start.19) | collective-permute-done | bytes 131104 | tf_op jit(solution)/shard_map/ppermute | solution.py:214
  177.4 3.6 %factor_0_1.1 = bf16[2048,128]{1,0:T(8,128)(2,1)S(1)} custom-call(bf16[6,8,256,4,256]{4,3,2,1,0:T(4,128)(2,1)} %refs_0_.34, bf16[1024,128]{1,0:T(8,128)(2,1)S(1)} %fusion.5.refs_1_.weight_ref, f32[2048,128]{1,0:T(8,128)S(1)} %factor_0_2.1.refs_2_), custom_call_target="tpu_custom_call" | custom-call | flops 1073741824 | bytes 4194304 | tf_op jit(solution)/shard_map/factor_0_1/pallas_call | solution.py:53
  181.0 4.2 %scored_3_0.1.refs_8_ = f32[1024,128]{1,0:T(8,128)S(1)} custom-call(s32[4]{0:T(128)S(1)} %get-tuple-element.56.slots_ref, bf16[1024,512]{1,0:T(8,128)(2,1)S(1)} %gather_fusion, f32[1024,128]{1,0:T(8,128)S(1)} %get-tuple-element.13.norm_ref, bf16[1024,128]{1,0:T(8,128)(2,1)S(1)} %fusion.7.refs_1_.weight_ref, bf16[16,256,512]{2,1,0:T(8,128)(2,1)} %refs_3_.31, ...), custom_call_target="tpu_custom_call" | custom-call | flops 2415919104 | bytes 2097152 | tf_op jit(solution)/shard_map/scored_3_0/pallas_call | solution.py:156
  185.2 4.3 %scored_2_3.1.refs_8_ = f32[1024,128]{1,0:T(8,128)S(1)} custom-call(s32[4]{0:T(128)S(1)} %get-tuple-element.57.slots_ref, bf16[1024,512]{1,0:T(8,128)(2,1)S(1)} %copy-done.1, f32[1024,128]{1,0:T(8,128)S(1)} %get-tuple-element.19.norm_ref, bf16[1024,128]{1,0:T(8,128)(2,1)S(1)} %copy-done.3, bf16[16,256,512]{2,1,0:T(8,128)(2,1)} %refs_3_.31, ...), custom_call_target="tpu_custom_call" | custom-call | flops 2415919104 | bytes 2097152 | tf_op jit(solution)/shard_map/scored_2_3/pallas_call | solution.py:156
  190.0 4.4 %scored_2_2.1.refs_8_ = f32[1024,128]{1,0:T(8,128)S(1)} custom-call(s32[4]{0:T(128)S(1)} %get-tuple-element.57.slots_ref, bf16[1024,512]{1,0:T(8,128)(2,1)S(1)} %gather_fusion.2, f32[1024,128]{1,0:T(8,128)S(1)} %get-tuple-element.17.norm_ref, bf16[1024,128]{1,0:T(8,128)(2,1)S(1)} %copy-done.3, bf16[16,256,512]{2,1,0:T(8,128)(2,1)} %refs_3_.31, ...), custom_call_target="tpu_custom_call" | custom-call | flops 2415919104 | bytes 2097152 | tf_op jit(solution)/shard_map/scored_2_2/pallas_call | solution.py:156
  195.7 2.7 %collective-permute-start.24 = (bf16[512,128]{1,0:T(8,128)(2,1)S(1)}, bf16[512,128]{1,0:T(8,128)(2,1)S(1)}, u32[]{:S(2)}, u32[]{:S(2)}) collective-permute-start(bf16[512,128]{1,0:T(8,128)(2,1)S(1)} %add_convert_fusion.7), channel_id=1, source_target_pairs={{0,6},{1,7},{2,4},{3,5},{4,2},{5,3},{6,0},{7,1},{8,14},{9,15},{10,... | collective-permute-start | bytes 393224 | tf_op jit(solution)/shard_map/ppermute | solution.py:214
  198.3 4.5 %scored_2_1.1.refs_8_ = f32[1024,128]{1,0:T(8,128)S(1)} custom-call(s32[4]{0:T(128)S(1)} %get-tuple-element.57.slots_ref, bf16[1024,512]{1,0:T(8,128)(2,1)S(1)} %gather_fusion.1, f32[1024,128]{1,0:T(8,128)S(1)} %get-tuple-element.15.norm_ref, bf16[1024,128]{1,0:T(8,128)(2,1)S(1)} %copy-done.3, bf16[16,256,512]{2,1,0:T(8,128)(2,1)} %refs_3_.31, ...), custom_call_target="tpu_custom_call" | custom-call | flops 2415919104 | bytes 2097152 | tf_op jit(solution)/shard_map/scored_2_1/pallas_call | solution.py:156
  203.9 1.8 collective-permute-start.25
  205.7 4.4 %scored_2_0.1.refs_8_ = f32[1024,128]{1,0:T(8,128)S(1)} custom-call(s32[4]{0:T(128)S(1)} %get-tuple-element.57.slots_ref, bf16[1024,512]{1,0:T(8,128)(2,1)S(1)} %gather_fusion, f32[1024,128]{1,0:T(8,128)S(1)} %get-tuple-element.13.norm_ref, bf16[1024,128]{1,0:T(8,128)(2,1)S(1)} %copy-done.3, bf16[16,256,512]{2,1,0:T(8,128)(2,1)} %refs_3_.31, ...), custom_call_target="tpu_custom_call" | custom-call | flops 2415919104 | bytes 2097152 | tf_op jit(solution)/shard_map/scored_2_0/pallas_call | solution.py:156
  210.3 4.3 %scored_1_3.1.earlier_ref = f32[1024,128]{1,0:T(8,128)S(1)} custom-call(s32[4]{0:T(128)S(1)} %get-tuple-element.58.slots_ref, bf16[1024,512]{1,0:T(8,128)(2,1)S(1)} %copy-done.1, f32[1024,128]{1,0:T(8,128)S(1)} %get-tuple-element.19.norm_ref, bf16[1024,128]{1,0:T(8,128)(2,1)S(1)} %fusion.5.refs_1_.weight_ref, bf16[16,256,512]{2,1,0:T(8,128)(2,1)} %refs_3_.31, ...), custom_call_target="tpu_custom_call" | custom-call | flops 2415919104 | bytes 2097152 | tf_op jit(solution)/shard_map/scored_1_3/pallas_call | solution.py:156
  214.6 4.4 %scored_1_2.1.earlier_ref = f32[1024,128]{1,0:T(8,128)S(1)} custom-call(s32[4]{0:T(128)S(1)} %get-tuple-element.58.slots_ref, bf16[1024,512]{1,0:T(8,128)(2,1)S(1)} %gather_fusion.2, f32[1024,128]{1,0:T(8,128)S(1)} %get-tuple-element.17.norm_ref, bf16[1024,128]{1,0:T(8,128)(2,1)S(1)} %fusion.5.refs_1_.weight_ref, bf16[16,256,512]{2,1,0:T(8,128)(2,1)} %refs_3_.31, ...), custom_call_target="tpu_custom_call" | custom-call | flops 2415919104 | bytes 2097152 | tf_op jit(solution)/shard_map/scored_1_2/pallas_call | solution.py:156
  219.2 3.3 %inverse_0.1 = bf16[1024,128]{1,0:T(8,128)(2,1)S(1)} custom-call(bf16[4,4,256,8,256]{4,3,2,1,0:T(8,128)(2,1)} %refs_0_.35, bf16[2048,128]{1,0:T(8,128)(2,1)S(1)} %pad_maximum_fusion.7.refs_1_), custom_call_target="tpu_custom_call" | custom-call | flops 1073741824 | bytes 4194304 | tf_op jit(solution)/shard_map/inverse_0/pallas_call | solution.py:53
  224.8 4.4 %scored_1_1.1.earlier_ref = f32[1024,128]{1,0:T(8,128)S(1)} custom-call(s32[4]{0:T(128)S(1)} %get-tuple-element.58.slots_ref, bf16[1024,512]{1,0:T(8,128)(2,1)S(1)} %gather_fusion.1, f32[1024,128]{1,0:T(8,128)S(1)} %get-tuple-element.15.norm_ref, bf16[1024,128]{1,0:T(8,128)(2,1)S(1)} %fusion.5.refs_1_.weight_ref, bf16[16,256,512]{2,1,0:T(8,128)(2,1)} %refs_3_.31, ...), custom_call_target="tpu_custom_call" | custom-call | flops 2415919104 | bytes 2097152 | tf_op jit(solution)/shard_map/scored_1_1/pallas_call | solution.py:156
  230.3 4.4 %scored_1_0.1.earlier_ref = f32[1024,128]{1,0:T(8,128)S(1)} custom-call(s32[4]{0:T(128)S(1)} %get-tuple-element.58.slots_ref, bf16[1024,512]{1,0:T(8,128)(2,1)S(1)} %gather_fusion, f32[1024,128]{1,0:T(8,128)S(1)} %get-tuple-element.13.norm_ref, bf16[1024,128]{1,0:T(8,128)(2,1)S(1)} %fusion.5.refs_1_.weight_ref, bf16[16,256,512]{2,1,0:T(8,128)(2,1)} %refs_3_.31, ...), custom_call_target="tpu_custom_call" | custom-call | flops 2415919104 | bytes 2097152 | tf_op jit(solution)/shard_map/scored_1_0/pallas_call | solution.py:156
  235.7 4.0 %collective-permute-done.28 = bf16[512,128]{1,0:T(8,128)(2,1)S(1)} collective-permute-done((bf16[512,128]{1,0:T(8,128)(2,1)S(1)}, bf16[512,128]{1,0:T(8,128)(2,1)S(1)}, u32[]{:S(2)}, u32[]{:S(2)}) %collective-permute-start.28) | collective-permute-done | bytes 131104 | tf_op jit(solution)/shard_map/ppermute | solution.py:214
  244.8 2.0 collective-permute-done.31
  247.8 7.6 %collective-permute-done.32 = bf16[1024,128]{1,0:T(8,128)(2,1)S(1)} collective-permute-done((bf16[1024,128]{1,0:T(8,128)(2,1)S(1)}, bf16[1024,128]{1,0:T(8,128)(2,1)S(1)}, u32[]{:S(2)}, u32[]{:S(2)}) %collective-permute-start.32) | collective-permute-done | bytes 262176 | tf_op jit(solution)/shard_map/ppermute | solution.py:214
  255.5 1.8 collective-permute-start.33
  257.3 1.5 pad_maximum_fusion
  258.8 5.2 %collective-permute-done.33 = bf16[512,128]{1,0:T(8,128)(2,1)S(1)} collective-permute-done((bf16[512,128]{1,0:T(8,128)(2,1)S(1)}, bf16[512,128]{1,0:T(8,128)(2,1)S(1)}, u32[]{:S(2)}, u32[]{:S(2)}) %collective-permute-start.33) | collective-permute-done | bytes 131104 | tf_op jit(solution)/shard_map/ppermute | solution.py:214
  (155 shorter events, 30.8 us)
Async XLA Ops:
  6.7 6.5 %collective-permute-start = (bf16[512,128]{1,0:T(8,128)(2,1)S(1)}, bf16[512,128]{1,0:T(8,128)(2,1)S(1)}, u32[]{:S(2)}, u32[]{:S(2)}) collective-permute-start(bf16[512,128]{1,0:T(8,128)(2,1)S(1)} %get-tuple-element.50), channel_id=1, source_target_pairs={{0,8},{8,0},{16,24},{24,16},{1,9},{9,1},{17,25},{25,17},{2,10},{10... | collective-permute-start | bytes 393224 | tf_op jit(solution)/shard_map/ppermute | solution.py:214
  9.7 5.0 %collective-permute-start.2 = (bf16[512,128]{1,0:T(8,128)(2,1)S(1)}, bf16[512,128]{1,0:T(8,128)(2,1)S(1)}, u32[]{:S(2)}, u32[]{:S(2)}) collective-permute-start(bf16[512,128]{1,0:T(8,128)(2,1)S(1)} %get-tuple-element.51), channel_id=1, source_target_pairs={{0,16},{8,24},{16,0},{24,8},{1,17},{9,25},{17,1},{25,9},{2,18},{10... | collective-permute-start | bytes 393224 | tf_op jit(solution)/shard_map/ppermute | solution.py:214
  14.7 5.0 %collective-permute-start.3 = (bf16[512,128]{1,0:T(8,128)(2,1)S(1)}, bf16[512,128]{1,0:T(8,128)(2,1)S(1)}, u32[]{:S(2)}, u32[]{:S(2)}) collective-permute-start(bf16[512,128]{1,0:T(8,128)(2,1)S(1)} %get-tuple-element.49), channel_id=1, source_target_pairs={{0,8},{8,0},{16,24},{24,16},{1,9},{9,1},{17,25},{25,17},{2,10},{10... | collective-permute-start | bytes 393224 | tf_op jit(solution)/shard_map/ppermute | solution.py:214
  15.1 5.0 %collective-permute-start.1 = (bf16[512,128]{1,0:T(8,128)(2,1)S(1)}, bf16[512,128]{1,0:T(8,128)(2,1)S(1)}, u32[]{:S(2)}, u32[]{:S(2)}) collective-permute-start(bf16[512,128]{1,0:T(8,128)(2,1)S(1)} %get-tuple-element.48), channel_id=1, source_target_pairs={{0,16},{8,24},{16,0},{24,8},{1,17},{9,25},{17,1},{25,9},{2,18},{10... | collective-permute-start | bytes 393224 | tf_op jit(solution)/shard_map/ppermute | solution.py:214
  19.8 0.7 copy-start.10
  20.5 0.7 copy-start.12
  24.8 1.6 collective-permute-start.4
  26.5 5.6 %collective-permute-start.5 = (bf16[512,128]{1,0:T(8,128)(2,1)S(1)}, bf16[512,128]{1,0:T(8,128)(2,1)S(1)}, u32[]{:S(2)}, u32[]{:S(2)}) collective-permute-start(bf16[512,128]{1,0:T(8,128)(2,1)S(1)} %constant_dynamic-slice_fusion.7), channel_id=1, source_target_pairs={{0,2},{1,3},{2,0},{3,1},{4,6},{5,7},{6,4},{7,5},{8,10},{9,11},{10,... | collective-permute-start | bytes 393224 | tf_op jit(solution)/shard_map/ppermute | solution.py:214
  32.2 6.9 %collective-permute-start.6 = (bf16[512,128]{1,0:T(8,128)(2,1)S(1)}, bf16[512,128]{1,0:T(8,128)(2,1)S(1)}, u32[]{:S(2)}, u32[]{:S(2)}) collective-permute-start(bf16[512,128]{1,0:T(8,128)(2,1)S(1)} %add_convert_fusion.13), channel_id=1, source_target_pairs={{0,6},{1,7},{2,4},{3,5},{4,2},{5,3},{6,0},{7,1},{8,14},{9,15},{10,... | collective-permute-start | bytes 393224 | tf_op jit(solution)/shard_map/ppermute | solution.py:214
  39.1 5.3 %collective-permute-start.7 = (bf16[512,128]{1,0:T(8,128)(2,1)S(1)}, bf16[512,128]{1,0:T(8,128)(2,1)S(1)}, u32[]{:S(2)}, u32[]{:S(2)}) collective-permute-start(bf16[512,128]{1,0:T(8,128)(2,1)S(1)} %subtract_convert_fusion.2), channel_id=1, source_target_pairs={{0,2},{1,3},{2,0},{3,1},{4,6},{5,7},{6,4},{7,5},{8,10},{9,11},{10,... | collective-permute-start | bytes 393224 | tf_op jit(solution)/shard_map/ppermute | solution.py:214
  44.5 3.2 %collective-permute-start.8 = (bf16[1024,128]{1,0:T(8,128)(2,1)S(1)}, bf16[1024,128]{1,0:T(8,128)(2,1)S(1)}, u32[]{:S(2)}, u32[]{:S(2)}) collective-permute-start(bf16[1024,128]{1,0:T(8,128)(2,1)S(1)} %pad_maximum_fusion.9), channel_id=1, source_target_pairs={{0,1},{1,0},{2,3},{3,2},{4,5},{5,4},{6,7},{7,6},{8,9},{9,8},{10,11... | collective-permute-start | bytes 786440 | tf_op jit(solution)/shard_map/ppermute | solution.py:214
  47.8 6.3 %copy-start.22 = (s32[4096]{0:T(1024)S(1)}, s32[4096]{0:T(1024)}, u32[]{:S(2)}) copy-start(s32[4096]{0:T(1024)} %param.13) | copy-start | bytes 49156
  47.9 11.2 %copy-start.23 = (s32[16,1]{0,1:T(1,128)S(1)}, s32[16,1]{0,1:T(1,128)}, u32[]{:S(2)}) copy-start(s32[16,1]{0,1:T(1,128)} %param.11) | copy-start | bytes 196
  51.2 6.0 %collective-permute-start.9 = (bf16[512,128]{1,0:T(8,128)(2,1)S(1)}, bf16[512,128]{1,0:T(8,128)(2,1)S(1)}, u32[]{:S(2)}, u32[]{:S(2)}) collective-permute-start(bf16[512,128]{1,0:T(8,128)(2,1)S(1)} %get-tuple-element.44), channel_id=1, source_target_pairs={{0,8},{8,0},{16,24},{24,16},{1,9},{9,1},{17,25},{25,17},{2,10},{10... | collective-permute-start | bytes 393224 | tf_op jit(solution)/shard_map/ppermute | solution.py:214
  52.6 5.6 %collective-permute-start.11 = (bf16[512,128]{1,0:T(8,128)(2,1)S(1)}, bf16[512,128]{1,0:T(8,128)(2,1)S(1)}, u32[]{:S(2)}, u32[]{:S(2)}) collective-permute-start(bf16[512,128]{1,0:T(8,128)(2,1)S(1)} %get-tuple-element.45), channel_id=1, source_target_pairs={{0,16},{8,24},{16,0},{24,8},{1,17},{9,25},{17,1},{25,9},{2,18},{10... | collective-permute-start | bytes 393224 | tf_op jit(solution)/shard_map/ppermute | solution.py:214
  58.3 7.2 %collective-permute-start.12 = (bf16[512,128]{1,0:T(8,128)(2,1)S(1)}, bf16[512,128]{1,0:T(8,128)(2,1)S(1)}, u32[]{:S(2)}, u32[]{:S(2)}) collective-permute-start(bf16[512,128]{1,0:T(8,128)(2,1)S(1)} %get-tuple-element.43), channel_id=1, source_target_pairs={{0,8},{8,0},{16,24},{24,16},{1,9},{9,1},{17,25},{25,17},{2,10},{10... | collective-permute-start | bytes 393224 | tf_op jit(solution)/shard_map/ppermute | solution.py:214
  63.9 5.0 %collective-permute-start.10 = (bf16[512,128]{1,0:T(8,128)(2,1)S(1)}, bf16[512,128]{1,0:T(8,128)(2,1)S(1)}, u32[]{:S(2)}, u32[]{:S(2)}) collective-permute-start(bf16[512,128]{1,0:T(8,128)(2,1)S(1)} %get-tuple-element.42), channel_id=1, source_target_pairs={{0,16},{8,24},{16,0},{24,8},{1,17},{9,25},{17,1},{25,9},{2,18},{10... | collective-permute-start | bytes 393224 | tf_op jit(solution)/shard_map/ppermute | solution.py:214
  65.5 3.4 %copy-start.14 = (f32[512,128]{1,0:T(8,128)}, f32[512,128]{1,0:T(8,128)S(1)}, u32[]{:S(2)}) copy-start(f32[512,128]{1,0:T(8,128)S(1)} %convert_add_fusion.5) | copy-start | bytes 786436
  68.9 0.7 copy-start.16
  69.7 14.4 %copy-start.2 = (bf16[1024,128]{1,0:T(8,128)(2,1)}, bf16[1024,128]{1,0:T(8,128)(2,1)S(1)}, u32[]{:S(2)}) copy-start(bf16[1024,128]{1,0:T(8,128)(2,1)S(1)} %fusion.6.refs_1_.weight_ref) | copy-start | bytes 786436
  84.1 0.9 copy-start.4
  84.9 36.2 %collective-permute-start.13 = (bf16[1024,128]{1,0:T(8,128)(2,1)}, bf16[1024,128]{1,0:T(8,128)(2,1)}, u32[]{:S(2)}, u32[]{:S(2)}) collective-permute-start(bf16[1024,128]{1,0:T(8,128)(2,1)} %constant_dynamic-slice_fusion.6), channel_id=1, source_target_pairs={{0,1},{1,0},{2,3},{3,2},{4,5},{5,4},{6,7},{7,6},{8,9},{9,8},{10,11... | collective-permute-start | bytes 786440 | tf_op jit(solution)/shard_map/ppermute | solution.py:214
  116.5 1.2 copy-start
  117.7 3.4 %copy-start.5 = (bf16[2048,128]{1,0:T(8,128)(2,1)S(1)}, bf16[2048,128]{1,0:T(8,128)(2,1)}, u32[]{:S(2)}) copy-start(bf16[2048,128]{1,0:T(8,128)(2,1)} %copy-done.4) | copy-start | bytes 1572868
  122.2 6.3 %collective-permute-start.14 = (bf16[512,128]{1,0:T(8,128)(2,1)S(1)}, bf16[512,128]{1,0:T(8,128)(2,1)S(1)}, u32[]{:S(2)}, u32[]{:S(2)}) collective-permute-start(bf16[512,128]{1,0:T(8,128)(2,1)S(1)} %constant_dynamic-slice_fusion.5), channel_id=1, source_target_pairs={{0,2},{1,3},{2,0},{3,1},{4,6},{5,7},{6,4},{7,5},{8,10},{9,11},{10,... | collective-permute-start | bytes 393224 | tf_op jit(solution)/shard_map/ppermute | solution.py:214
  128.5 7.3 %collective-permute-start.15 = (bf16[512,128]{1,0:T(8,128)(2,1)S(1)}, bf16[512,128]{1,0:T(8,128)(2,1)S(1)}, u32[]{:S(2)}, u32[]{:S(2)}) collective-permute-start(bf16[512,128]{1,0:T(8,128)(2,1)S(1)} %add_convert_fusion.10), channel_id=1, source_target_pairs={{0,6},{1,7},{2,4},{3,5},{4,2},{5,3},{6,0},{7,1},{8,14},{9,15},{10,... | collective-permute-start | bytes 393224 | tf_op jit(solution)/shard_map/ppermute | solution.py:214
  135.0 7.8 %copy-start.6 = (bf16[1024,1024]{1,0:T(8,128)(2,1)}, bf16[1024,1024]{1,0:T(8,128)(2,1)S(1)}, u32[]{:S(2)}) copy-start(bf16[1024,1024]{1,0:T(8,128)(2,1)S(1)} %get-tuple-element.14.kernel_ref) | copy-start | bytes 6291460
  136.7 7.5 %copy-start.1 = (bf16[1024,512]{1,0:T(8,128)(2,1)S(1)}, bf16[1024,512]{1,0:T(8,128)(2,1)}, u32[]{:S(2)}) copy-start(bf16[1024,512]{1,0:T(8,128)(2,1)} %gather_fusion.3) | copy-start | bytes 3145732
  136.8 7.4 %collective-permute-start.16 = (bf16[512,128]{1,0:T(8,128)(2,1)S(1)}, bf16[512,128]{1,0:T(8,128)(2,1)S(1)}, u32[]{:S(2)}, u32[]{:S(2)}) collective-permute-start(bf16[512,128]{1,0:T(8,128)(2,1)S(1)} %subtract_convert_fusion.1), channel_id=1, source_target_pairs={{0,2},{1,3},{2,0},{3,1},{4,6},{5,7},{6,4},{7,5},{8,10},{9,11},{10,... | collective-permute-start | bytes 393224 | tf_op jit(solution)/shard_map/ppermute | solution.py:214
  142.8 1.3 copy-start.8
  144.2 8.4 %collective-permute-start.17 = (bf16[1024,128]{1,0:T(8,128)(2,1)S(1)}, bf16[1024,128]{1,0:T(8,128)(2,1)S(1)}, u32[]{:S(2)}, u32[]{:S(2)}) collective-permute-start(bf16[1024,128]{1,0:T(8,128)(2,1)S(1)} %pad_maximum_fusion.10), channel_id=1, source_target_pairs={{0,1},{1,0},{2,3},{3,2},{4,5},{5,4},{6,7},{7,6},{8,9},{9,8},{10,11... | collective-permute-start | bytes 786440 | tf_op jit(solution)/shard_map/ppermute | solution.py:214
  156.0 7.5 %collective-permute-start.18 = (bf16[512,128]{1,0:T(8,128)(2,1)S(1)}, bf16[512,128]{1,0:T(8,128)(2,1)S(1)}, u32[]{:S(2)}, u32[]{:S(2)}) collective-permute-start(bf16[512,128]{1,0:T(8,128)(2,1)S(1)} %get-tuple-element.38), channel_id=1, source_target_pairs={{0,8},{8,0},{16,24},{24,16},{1,9},{9,1},{17,25},{25,17},{2,10},{10... | collective-permute-start | bytes 393224 | tf_op jit(solution)/shard_map/ppermute | solution.py:214
  157.4 6.1 %collective-permute-start.20 = (bf16[512,128]{1,0:T(8,128)(2,1)S(1)}, bf16[512,128]{1,0:T(8,128)(2,1)S(1)}, u32[]{:S(2)}, u32[]{:S(2)}) collective-permute-start(bf16[512,128]{1,0:T(8,128)(2,1)S(1)} %get-tuple-element.39), channel_id=1, source_target_pairs={{0,16},{8,24},{16,0},{24,8},{1,17},{9,25},{17,1},{25,9},{2,18},{10... | collective-permute-start | bytes 393224 | tf_op jit(solution)/shard_map/ppermute | solution.py:214
  163.6 4.3 %copy-start.3 = (bf16[1024,128]{1,0:T(8,128)(2,1)S(1)}, bf16[1024,128]{1,0:T(8,128)(2,1)}, u32[]{:S(2)}) copy-start(bf16[1024,128]{1,0:T(8,128)(2,1)} %copy-done.2) | copy-start | bytes 786436
  163.7 8.9 %collective-permute-start.21 = (bf16[512,128]{1,0:T(8,128)(2,1)S(1)}, bf16[512,128]{1,0:T(8,128)(2,1)S(1)}, u32[]{:S(2)}, u32[]{:S(2)}) collective-permute-start(bf16[512,128]{1,0:T(8,128)(2,1)S(1)} %get-tuple-element.37), channel_id=1, source_target_pairs={{0,8},{8,0},{16,24},{24,16},{1,9},{9,1},{17,25},{25,17},{2,10},{10... | collective-permute-start | bytes 393224 | tf_op jit(solution)/shard_map/ppermute | solution.py:214
  171.5 5.0 %collective-permute-start.19 = (bf16[512,128]{1,0:T(8,128)(2,1)S(1)}, bf16[512,128]{1,0:T(8,128)(2,1)S(1)}, u32[]{:S(2)}, u32[]{:S(2)}) collective-permute-start(bf16[512,128]{1,0:T(8,128)(2,1)S(1)} %get-tuple-element.36), channel_id=1, source_target_pairs={{0,16},{8,24},{16,0},{24,8},{1,17},{9,25},{17,1},{25,9},{2,18},{10... | collective-permute-start | bytes 393224 | tf_op jit(solution)/shard_map/ppermute | solution.py:214
  172.6 4.0 %copy-start.18 = (f32[512,128]{1,0:T(8,128)}, f32[512,128]{1,0:T(8,128)S(1)}, u32[]{:S(2)}) copy-start(f32[512,128]{1,0:T(8,128)S(1)} %convert_add_fusion.3) | copy-start | bytes 786436
  176.6 0.7 copy-start.20
  181.0 8.6 %collective-permute-start.22 = (bf16[1024,128]{1,0:T(8,128)(2,1)S(1)}, bf16[1024,128]{1,0:T(8,128)(2,1)S(1)}, u32[]{:S(2)}, u32[]{:S(2)}) collective-permute-start(bf16[1024,128]{1,0:T(8,128)(2,1)S(1)} %constant_dynamic-slice_fusion.4), channel_id=1, source_target_pairs={{0,1},{1,0},{2,3},{3,2},{4,5},{5,4},{6,7},{7,6},{8,9},{9,8},{10,11... | collective-permute-start | bytes 786440 | tf_op jit(solution)/shard_map/ppermute | solution.py:214
  189.7 5.9 %collective-permute-start.23 = (bf16[512,128]{1,0:T(8,128)(2,1)S(1)}, bf16[512,128]{1,0:T(8,128)(2,1)S(1)}, u32[]{:S(2)}, u32[]{:S(2)}) collective-permute-start(bf16[512,128]{1,0:T(8,128)(2,1)S(1)} %constant_dynamic-slice_fusion.3), channel_id=1, source_target_pairs={{0,2},{1,3},{2,0},{3,1},{4,6},{5,7},{6,4},{7,5},{8,10},{9,11},{10,... | collective-permute-start | bytes 393224 | tf_op jit(solution)/shard_map/ppermute | solution.py:214
  195.7 7.2 %collective-permute-start.24 = (bf16[512,128]{1,0:T(8,128)(2,1)S(1)}, bf16[512,128]{1,0:T(8,128)(2,1)S(1)}, u32[]{:S(2)}, u32[]{:S(2)}) collective-permute-start(bf16[512,128]{1,0:T(8,128)(2,1)S(1)} %add_convert_fusion.7), channel_id=1, source_target_pairs={{0,6},{1,7},{2,4},{3,5},{4,2},{5,3},{6,0},{7,1},{8,14},{9,15},{10,... | collective-permute-start | bytes 393224 | tf_op jit(solution)/shard_map/ppermute | solution.py:214
  203.9 6.2 %collective-permute-start.25 = (bf16[512,128]{1,0:T(8,128)(2,1)S(1)}, bf16[512,128]{1,0:T(8,128)(2,1)S(1)}, u32[]{:S(2)}, u32[]{:S(2)}) collective-permute-start(bf16[512,128]{1,0:T(8,128)(2,1)S(1)} %subtract_convert_fusion), channel_id=1, source_target_pairs={{0,2},{1,3},{2,0},{3,1},{4,6},{5,7},{6,4},{7,5},{8,10},{9,11},{10,... | collective-permute-start | bytes 393224 | tf_op jit(solution)/shard_map/ppermute | solution.py:214
  210.2 8.8 %collective-permute-start.26 = (bf16[1024,128]{1,0:T(8,128)(2,1)S(1)}, bf16[1024,128]{1,0:T(8,128)(2,1)S(1)}, u32[]{:S(2)}, u32[]{:S(2)}) collective-permute-start(bf16[1024,128]{1,0:T(8,128)(2,1)S(1)} %pad_maximum_fusion.11), channel_id=1, source_target_pairs={{0,1},{1,0},{2,3},{3,2},{4,5},{5,4},{6,7},{7,6},{8,9},{9,8},{10,11... | collective-permute-start | bytes 786440 | tf_op jit(solution)/shard_map/ppermute | solution.py:214
  222.5 6.7 %collective-permute-start.27 = (bf16[512,128]{1,0:T(8,128)(2,1)S(1)}, bf16[512,128]{1,0:T(8,128)(2,1)S(1)}, u32[]{:S(2)}, u32[]{:S(2)}) collective-permute-start(bf16[512,128]{1,0:T(8,128)(2,1)S(1)} %get-tuple-element.32), channel_id=1, source_target_pairs={{0,8},{8,0},{16,24},{24,16},{1,9},{9,1},{17,25},{25,17},{2,10},{10... | collective-permute-start | bytes 393224 | tf_op jit(solution)/shard_map/ppermute | solution.py:214
  223.9 5.6 %collective-permute-start.29 = (bf16[512,128]{1,0:T(8,128)(2,1)S(1)}, bf16[512,128]{1,0:T(8,128)(2,1)S(1)}, u32[]{:S(2)}, u32[]{:S(2)}) collective-permute-start(bf16[512,128]{1,0:T(8,128)(2,1)S(1)} %get-tuple-element.33), channel_id=1, source_target_pairs={{0,16},{8,24},{16,0},{24,8},{1,17},{9,25},{17,1},{25,9},{2,18},{10... | collective-permute-start | bytes 393224 | tf_op jit(solution)/shard_map/ppermute | solution.py:214
  229.6 6.2 %collective-permute-start.30 = (bf16[512,128]{1,0:T(8,128)(2,1)S(1)}, bf16[512,128]{1,0:T(8,128)(2,1)S(1)}, u32[]{:S(2)}, u32[]{:S(2)}) collective-permute-start(bf16[512,128]{1,0:T(8,128)(2,1)S(1)} %get-tuple-element.31), channel_id=1, source_target_pairs={{0,8},{8,0},{16,24},{24,16},{1,9},{9,1},{17,25},{25,17},{2,10},{10... | collective-permute-start | bytes 393224 | tf_op jit(solution)/shard_map/ppermute | solution.py:214
  234.7 5.0 %collective-permute-start.28 = (bf16[512,128]{1,0:T(8,128)(2,1)S(1)}, bf16[512,128]{1,0:T(8,128)(2,1)S(1)}, u32[]{:S(2)}, u32[]{:S(2)}) collective-permute-start(bf16[512,128]{1,0:T(8,128)(2,1)S(1)} %get-tuple-element.30), channel_id=1, source_target_pairs={{0,16},{8,24},{16,0},{24,8},{1,17},{9,25},{17,1},{25,9},{2,18},{10... | collective-permute-start | bytes 393224 | tf_op jit(solution)/shard_map/ppermute | solution.py:214
  240.5 1.6 copy-start.7
  241.2 1.7 copy-start.9
  243.8 1.0 copy-start.11
  243.8 1.0 copy-start.13
  243.9 3.8 %copy-start.15 = (f32[512,128]{1,0:T(8,128)S(1)}, f32[512,128]{1,0:T(8,128)}, u32[]{:S(2)}) copy-start(f32[512,128]{1,0:T(8,128)} %copy-done.14) | copy-start | bytes 786436
  243.9 3.8 %copy-start.17 = (f32[512,128]{1,0:T(8,128)S(1)}, f32[512,128]{1,0:T(8,128)}, u32[]{:S(2)}) copy-start(f32[512,128]{1,0:T(8,128)} %copy-done.16) | copy-start | bytes 786436
  244.7 2.1 collective-permute-start.31
  244.8 2.9 %copy-start.19 = (f32[512,128]{1,0:T(8,128)S(1)}, f32[512,128]{1,0:T(8,128)}, u32[]{:S(2)}) copy-start(f32[512,128]{1,0:T(8,128)} %copy-done.18) | copy-start | bytes 786436
  244.8 2.9 %copy-start.21 = (f32[512,128]{1,0:T(8,128)S(1)}, f32[512,128]{1,0:T(8,128)}, u32[]{:S(2)}) copy-start(f32[512,128]{1,0:T(8,128)} %copy-done.20) | copy-start | bytes 786436
  247.0 8.4 %collective-permute-start.32 = (bf16[1024,128]{1,0:T(8,128)(2,1)S(1)}, bf16[1024,128]{1,0:T(8,128)(2,1)S(1)}, u32[]{:S(2)}, u32[]{:S(2)}) collective-permute-start(bf16[1024,128]{1,0:T(8,128)(2,1)S(1)} %constant_dynamic-slice_fusion.1), channel_id=1, source_target_pairs={{0,2},{1,3},{2,0},{3,1},{4,6},{5,7},{6,4},{7,5},{8,10},{9,11},{10,... | collective-permute-start | bytes 786440 | tf_op jit(solution)/shard_map/ppermute | solution.py:214
  255.5 8.5 %collective-permute-start.33 = (bf16[512,128]{1,0:T(8,128)(2,1)S(1)}, bf16[512,128]{1,0:T(8,128)(2,1)S(1)}, u32[]{:S(2)}, u32[]{:S(2)}) collective-permute-start(bf16[512,128]{1,0:T(8,128)(2,1)S(1)} %constant_dynamic-slice_fusion), channel_id=1, source_target_pairs={{0,4},{1,5},{2,6},{3,7},{4,0},{5,1},{6,2},{7,3},{8,12},{9,13},{10,... | collective-permute-start | bytes 393224 | tf_op jit(solution)/shard_map/ppermute | solution.py:214

commit v2 on v0

v2 whole, which is shorter than its diff:
```python
import math

import jax
import jax.numpy as jnp
import numpy as np
from jax import lax
from jax.experimental import pallas as pl
from jax.experimental.pallas import tpu as pltpu
from jax.sharding import PartitionSpec as P

inverse_width = 0.35
log2e = math.log2(math.e)
scale = -inverse_width * log2e
row_room, core_room, near_room, far_room = 3.3, 1.2, 3.0, 5.5
row_parts = 2
flying = 8
bf16 = jnp.bfloat16
f32 = jnp.float32
vmem = pl.BlockSpec(memory_space=pltpu.VMEM)
smem = pl.BlockSpec(memory_space=pltpu.SMEM)
stays = pl.BlockSpec(memory_space=pltpu.HBM)


def params(mib):
    return pltpu.CompilerParams(vmem_limit_bytes=mib * 2**20)


def pair_slot(early, successor):
    return successor * (successor - 1) // 2 + early


def fetches(block_ref, slot, held, sem):
    return [
        pltpu.make_async_copy(block_ref.at[slot, g], held.at[g], sem.at[g])
        for g in range(held.shape[0])
    ]


def panel_product(blocks, slot, kept, vector, vector_flip, earlier, out_parts, out_flip, out_dtype, name):
    _, groups, rows, inner, width = blocks.shape
    depth = inner * width
    out_width = vector.shape[-1]
    in_parts = vector.shape[0]
    part_rows = groups * rows // out_parts
    unit = min(rows, part_rows)
    flips = [f for f in (vector_flip, out_flip) if f is not None]
    more = [] if earlier is None else [earlier]

    def body(*refs):
        flip_refs, refs = list(refs[: len(flips)]), refs[len(flips) :]
        block_ref, vector_ref = refs[:2]
        out_ref = refs[2 + len(more)]
        held, sem = refs[3 + len(more) :] if kept is None else (block_ref, None)
        in_flip = 0 if vector_flip is None else flip_refs.pop(0)[0]
        flip = 0 if out_flip is None else flip_refs.pop(0)[0]
        copies = []
        if kept is None:
            copies = fetches(block_ref, slot, held, sem)
        for copy in copies[:flying]:
            copy.start()
        if in_parts == 1:
            column = vector_ref[0]
        elif vector_flip is None:
            column = vector_ref[...].reshape(depth, out_width)
        else:
            column = jnp.concatenate([vector_ref[p ^ in_flip] for p in range(in_parts)], axis=0)
        for g in range(groups):
            if kept is None:
                copies[g].wait()
                for copy in copies[g + flying : g + flying + 1]:
                    copy.start()
            for u in range(rows // unit):
                part, at = divmod(g * rows + u * unit, part_rows)
                at = pl.ds(at, unit)
                value = jnp.dot(
                    held[g, u * unit : (u + 1) * unit].reshape(unit, depth),
                    column,
                    preferred_element_type=f32,
                )
                if more:
                    value = value + refs[2][part ^ flip, at, :]
                out_ref[part ^ flip, at, :] = value.astype(out_dtype)

    source = pltpu.with_memory_space_constraint(blocks, pltpu.HBM) if kept is None else kept
    return pl.pallas_call(
        body,
        in_specs=[smem] * len(flips) + [stays if kept is None else vmem] + [vmem] * (1 + len(more)),
        out_specs=vmem,
        out_shape=jax.ShapeDtypeStruct((out_parts, part_rows, out_width), out_dtype),
        scratch_shapes=[
            pltpu.VMEM((groups, rows, inner, width), bf16),
            pltpu.SemaphoreType.DMA((groups,)),
        ]
        if kept is None
        else [],
        compiler_params=params(8),
        cost_estimate=pl.CostEstimate(
            flops=4 * groups * rows * depth * out_width,
            bytes_accessed=2 * groups * rows * depth,
            transcendentals=0,
        ),
        name=name,
    )(*flips, source, vector, *more)


def gathered(located, pool, chunks, name):
    count = located.shape[0]
    rows, dim = pool.shape
    cuts = dim // 128
    chunk = count // chunks
    group = 64
    step = 128
    block = min(1024, rows)
    stages = min(6, rows // block)

    def body(located_ref, pool_ref, *refs):
        out_refs, norm_refs = refs[:chunks], refs[chunks : 2 * chunks]
        wide, held, staged, sem, rows_out, norms_out, out_sem = refs[2 * chunks :]
        copies = [
            pltpu.make_async_copy(
                pool_ref.at[pl.ds(b * block, block)], staged.at[b % stages], sem.at[b % stages]
            )
            for b in range(rows // block)
        ]

        def widen(b):
            def convert(i, carry):
                at = pl.multiple_of(i * step, step)
                value = staged[b % stages, pl.ds(at, step), :].astype(f32)
                for h in range(cuts):
                    to = pl.ds((b * block + at) * cuts + h, step, stride=cuts)
                    wide[to, :] = value[:, h * 128 : (h + 1) * 128]
                return carry

            lax.fori_loop(0, block // step, convert, 0)

        def part(j):
            def fetch(i, carry):
                for u in range(group):
                    at = i * group + u
                    source = pl.multiple_of(located_ref[j * chunk + at] * cuts, cuts)
                    held[pl.ds(pl.multiple_of(at * cuts, cuts), cuts), :] = wide[pl.ds(source, cuts), :]
                return carry

            def store(i, carry):
                at = pl.multiple_of(i * step, step)
                parts = [held[pl.ds(at * cuts + h, step, stride=cuts), :] for h in range(cuts)]
                rows_out[j % 2, pl.ds(at, step), :] = jnp.concatenate(parts, axis=1).astype(bf16)
                total = sum(p * p for p in parts)
                norm = scale * jnp.sum(total, axis=1, keepdims=True)
                norms_out[j % 2, pl.ds(at, step), :] = jnp.broadcast_to(norm, (step, 128))
                return carry

            lax.fori_loop(0, chunk // group, fetch, 0)
            lax.fori_loop(0, chunk // step, store, 0)

        for copy in copies[:stages]:
            copy.start()
        for b in range(len(copies)):
            copies[b].wait()
            widen(b)
            for copy in copies[b + stages : b + stages + 1]:
                copy.start()
        writes = []
        for j in range(chunks):
            for copy in writes[2 * (j - 2) : 2 * (j - 1)] if j >= 2 else []:
                copy.wait()
            part(j)
            for n, (source, to) in enumerate(((rows_out, out_refs), (norms_out, norm_refs))):
                writes.append(pltpu.make_async_copy(source.at[j % 2], to[j], out_sem.at[j % 2, n]))
                writes[-1].start()
        for copy in writes[2 * max(chunks - 2, 0) :]:
            copy.wait()

    return pl.pallas_call(
        body,
        in_specs=[smem, stays],
        out_specs=[stays] * (2 * chunks),
        out_shape=[pltpu.HBM((chunk, dim), bf16)] * chunks + [pltpu.HBM((chunk, 128), f32)] * chunks,
        scratch_shapes=[
            pltpu.VMEM((rows * cuts, 128), f32),
            pltpu.VMEM((chunk * cuts, 128), f32),
            pltpu.VMEM((stages, block, dim), bf16),
            pltpu.SemaphoreType.DMA((stages,)),
            pltpu.VMEM((2, chunk, dim), bf16),
            pltpu.VMEM((2, chunk, 128), f32),
            pltpu.SemaphoreType.DMA((2, 2)),
        ],
        compiler_params=params(28),
        cost_estimate=pl.CostEstimate(
            flops=0, bytes_accessed=6 * rows * dim + 16 * count * dim, transcendentals=0
        ),
        name=name,
    )(located, pltpu.with_memory_space_constraint(pool, pltpu.HBM))


def scored(span, norms, centers, center_sq, slots, weights, earlier, fetch, name):
    tests, dim = span.shape
    tiles = slots.shape[0]
    size = centers.shape[1]
    step = min(512 if weights is not None else 256, tests)
    steps = tests // step
    depth = tiles * size
    more = [x for x in (weights, earlier) if x is not None]
    fresh = center_sq is None

    def body(slots_ref, span_ref, norm_ref, center_ref, *refs):
        refs = list(refs)
        sq_ref = None if fresh else refs.pop(0)
        more_refs = [refs.pop(0) for _ in more]
        source = None if fetch is None else refs.pop(0)
        out_ref = refs.pop(0)
        if fresh:
            sq_ref = refs.pop(0)
        copies = []
        if fetch is not None:
            copies = fetches(source, fetch[1], refs.pop(0), refs.pop())
            for copy in copies:
                copy.start()
        if fresh:
            for t in range(tiles):
                value = center_ref[slots_ref[t]].astype(f32)
                sq_ref[t] = scale * jnp.sum(value * value, axis=1, keepdims=True).T
        writes = []
        if weights is None:
            values, sem = refs
            writes = [
                pltpu.make_async_copy(values.at[i], out_ref.at[pl.ds(i * step, step)], sem.at[i])
                for i in range(steps)
            ]
        for i in range(steps):
            at = slice(i * step, (i + 1) * step)
            rows = span_ref[at, :]
            norm = jnp.concatenate([norm_ref[at, :]] * (size // 128), axis=1)
            total = None if earlier is None else more_refs[1][at, :]
            for t in range(tiles):
                slot = slots_ref[t]
                crossed = lax.dot_general(
                    rows, center_ref[slot], (((1,), (1,)), ((), ())), preferred_element_type=f32
                )
                value = jnp.exp2((crossed * (-2.0 * scale) + sq_ref[t]) + norm).astype(bf16)
                place = slice(t * size, (t + 1) * size)
                if weights is None:
                    values[i, :, place] = value
                else:
                    part = jnp.dot(value, more_refs[0][place, :], preferred_element_type=f32)
                    total = part if total is None else total + part
            if weights is None:
                writes[i].start()
            else:
                out_ref[at, :] = total
        for copy in writes + copies:
            copy.wait()

    if weights is None:
        out_shapes, out_specs = [jax.ShapeDtypeStruct((tests, depth), bf16)], [stays]
        scratch = [pltpu.VMEM((steps, step, depth), bf16), pltpu.SemaphoreType.DMA((steps,))]
    else:
        out_shapes, out_specs = [jax.ShapeDtypeStruct((tests, weights.shape[1]), f32)], [vmem]
        scratch = []
    operands = [slots, span, norms, centers] + ([] if fresh else [center_sq]) + more
    in_specs = [smem] + [vmem] * (len(operands) - 1)
    if fresh:
        out_shapes = out_shapes + [jax.ShapeDtypeStruct((tiles, 1, size), f32)]
        out_specs = out_specs + [vmem]
    if fetch is not None:
        in_specs = in_specs + [stays]
        operands = operands + [pltpu.with_memory_space_constraint(fetch[0], pltpu.HBM)]
        out_shapes = out_shapes + [jax.ShapeDtypeStruct(fetch[0].shape[1:], fetch[0].dtype)]
        out_specs = out_specs + [vmem]
        scratch = scratch + [pltpu.SemaphoreType.DMA((fetch[0].shape[1],))]
    if weights is None:
        out_shapes[0] = pltpu.HBM(out_shapes[0].shape, out_shapes[0].dtype)
    made = pl.pallas_call(
        body,
        in_specs=in_specs,
        out_specs=out_specs,
        out_shape=out_shapes,
        scratch_shapes=scratch,
        compiler_params=params(8),
        cost_estimate=pl.CostEstimate(
            flops=3 * tests * depth * dim,
            bytes_accessed=2 * tests * dim,
            transcendentals=tests * depth,
        ),
        name=name,
    )(*operands)
    sq = made[1] if fresh else center_sq
    return made[0], sq, made[-1] if fetch is not None else None


def finished(kernels, weights, totals, places):
    blocks = places.shape[0]
    tests, depth = kernels[0].shape
    width = weights.shape[1]
    height = len(kernels) * tests // blocks
    unit = min(height, tests)

    def body(places_ref, *refs):
        kernel_refs, weight_ref = refs[: len(kernels)], refs[len(kernels)]
        total_refs, out_ref = refs[len(kernels) + 1 : -1], refs[-1]
        for start in range(0, blocks * height, unit):
            c, at = divmod(start, tests)
            block, within = divmod(start, height)
            value = jnp.dot(
                kernel_refs[c][at : at + unit, :], weight_ref[...], preferred_element_type=f32
            )
            value = value + total_refs[c][at : at + unit, :]
            out_ref[places_ref[block], within : within + unit, :] = value.astype(bf16)

    return pl.pallas_call(
        body,
        in_specs=[smem] + [vmem] * (len(kernels) + 1 + len(totals)),
        out_specs=vmem,
        out_shape=jax.ShapeDtypeStruct((blocks, height, width), bf16),
        compiler_params=params(8),
        cost_estimate=pl.CostEstimate(
            flops=4 * blocks * height * depth * width,
            bytes_accessed=2 * blocks * height * depth,
            transcendentals=0,
        ),
        name="finished",
    )(places, *kernels, weights, *totals)


class Piece:
    def __init__(self, cost, make, fetches=False):
        self.cost, self.make, self.done, self.fetches = cost, make, False, fetches

    def run(self, before, fetch=None):
        if not self.done:
            self.done = True
            return self.make(before, fetch) if fetch else self.make(before)


class Beside:
    def __init__(self):
        self.pieces = []
        self.wanted = None
        self.fetched = None

    def want(self, wanted):
        self.wanted, self.fetched = wanted, None

    def take(self):
        fetched, self.wanted, self.fetched = self.fetched, None, None
        return fetched

    def tie(self, before, received, room, fetch=False):
        while True:
            self.pieces = [p for p in self.pieces if not p.done]
            fitting = [p for p in self.pieces if p.cost <= 2 * room]
            if not fitting:
                return received
            piece = fitting[0]
            room -= piece.cost
            if fetch and self.wanted and piece.fetches:
                made = piece.run(before, self.wanted)
                self.wanted, self.fetched = None, made[-1]
                made = made[:-1]
            else:
                made = piece.run(before)
                made = made[:-1] if piece.fetches else made
            received, _ = lax.optimization_barrier((received, made))

    def rest(self):
        for piece in self.pieces:
            piece.run(None)


def after(value, before):
    if before is None:
        return value
    return lax.optimization_barrier((value, before))[0]


def swap(value, axis, mask):
    size = lax.axis_size(axis)
    return lax.ppermute(value, axis, [(i, i ^ mask) for i in range(size)])


def added(left, right):
    return left.astype(f32) + right.astype(f32)


def col_steps():
    bits = lax.axis_size("col").bit_length() - 1
    place = lax.axis_index("col")
    bit = [(place >> j) & 1 for j in range(bits)]
    masks = [1 << j for j in range(bits)]
    if bits >= 3:
        bit[bits - 2] = bit[bits - 2] ^ bit[bits - 1]
        masks[-1] += masks[-2]
    return masks, bit


def packed(bits):
    number = jnp.int32(0)
    for b in bits:
        number = number * 2 + b
    return number


def row_sum(partial, work):
    bits = lax.axis_size("row").bit_length() - 1
    parts = [partial[p] for p in range(partial.shape[0])]
    orders = [list(range(bits)), list(range(bits))[::-1]]
    for j in range(bits):
        received = [swap(p, "row", 1 << o[j]) for p, o in zip(parts, orders)]
        received = work.tie(parts, received, row_room, j == bits - 1)
        parts = [added(p, r) for p, r in zip(parts, received)]
        if j < bits - 1:
            parts = [p.astype(bf16) for p in parts]
    return jnp.concatenate(parts, axis=0)


def subtracted(own, total, work):
    masks, _ = col_steps()
    for j, mask in enumerate(masks[:-1]):
        half = total.shape[0] // 2
        mine, other = total[:half], total[half:]
        received = work.tie(other, swap(other, "col", mask), core_room if j == 0 else near_room)
        total = added(mine, received).astype(bf16)
    received = work.tie(total, swap(total, "col", masks[-1]), far_room)
    value = (own.astype(f32) - added(total, received)).astype(bf16)
    for j, mask in reversed(list(enumerate(masks[:-1]))):
        received = work.tie(
            value, swap(value, "col", mask), core_room if j == 0 else near_room, True
        )
        value = jnp.concatenate([value, received], axis=0)
    return value


def scattered(total):
    masks, _ = col_steps()
    for j, mask in enumerate(masks):
        half = total.shape[0] // 2
        total = added(total[:half], swap(total[half:], "col", mask))
        if j < len(masks) - 1:
            total = total.astype(bf16)
    return total[0]


def shards(factor_blocks, inverse_blocks, right_side, centers, owner_map, test_pool, test_rows):
    panels = inverse_blocks.shape[0]
    col_tiles = inverse_blocks.shape[1]
    tile_size = inverse_blocks.shape[2]
    row_tiles = inverse_blocks.shape[3]
    width_out = right_side.shape[3]
    own_rows = row_tiles * tile_size
    tests = test_rows.shape[0]
    chunks = 4
    chunk = tests // chunks
    group = chunks

    _, kept = col_steps()
    parts = 2 ** (len(kept) - 1)
    flip = packed(kept[:-1])
    flip_ref = flip.reshape(1)
    targets = right_side.reshape(panels, parts, own_rows // parts, width_out)
    size = 2 ** len(kept)
    blocks = np.arange(size)
    digits = [(blocks >> j) & 1 for j in range(len(kept))]
    if len(kept) >= 3:
        digits[-2] = digits[-2] ^ digits[-1]
    places = sum(d << (len(kept) - 1 - j) for j, d in enumerate(digits)).astype(np.int32)
    places = jnp.asarray(places) ^ packed(kept)

    work = Beside()
    span = [None] * chunks
    norms = [None] * chunks
    center_sq = [None] * panels
    first = [None] * chunks
    totals = [None] * chunks
    solved = [None] * panels
    rounded = [None] * panels
    partial = [None] * panels

    tiles = owner_map.shape[0]
    match = owner_map == jnp.arange(tiles, dtype=jnp.int32)[None, :]
    slots = jnp.sum(match * jnp.arange(tiles, dtype=jnp.int32)[:, None], axis=0)
    located = test_rows - lax.axis_index("row") * test_pool.shape[0]

    def gather(i, count):
        def make(before):
            made = gathered(
                after(located[i * chunk : (i + count) * chunk], before), test_pool, count, f"gathered_{i}"
            )
            span[i : i + count] = made[:count]
            norms[i : i + count] = made[count:]
            return made

        return Piece(min(1.3 + 2.6 * count, 6.0), make)

    def panel_slots(k, before):
        return after(slots[k * col_tiles : (k + 1) * col_tiles], before)

    def score(k, i):
        def make(before, fetch=None):
            made, center_sq[k], fetched = scored(
                span[i], norms[i], centers, center_sq[k], panel_slots(k, before),
                rounded[k] if k > 0 else None, totals[i] if k > 0 else None, fetch,
                f"scored_{k}_{i}",
            )
            if k > 0:
                totals[i] = made
            else:
                first[i] = made
            return made, fetched

        return Piece(2.9 if k > 0 else 2.7, make, True)

    def factor(early, k, kept=None):
        def make(before):
            partial[early] = panel_product(
                factor_blocks,
                pair_slot(early, k),
                kept,
                after(rounded[k], before)[None],
                None,
                partial[early],
                parts,
                flip_ref,
                bf16 if early == k - 1 else f32,
                f"factor_{early}_{k}",
            )
            return partial[early]

        return Piece(3.6, make)

    work.pieces += [gather(i, group) for i in range(0, chunks, group)]
    ahead = []
    for k in range(panels - 1, -1, -1):
        if k == panels - 1:
            residue, residue_flip = targets[k], None
        else:
            for early, piece in ahead:
                if early == k:
                    piece.run(None)
            factor(k, k + 1, work.take()).run(None)
            own = lax.dynamic_slice(
                targets, (k, flip, 0, 0), (1, 1) + targets.shape[2:]
            )[0]
            residue, residue_flip = subtracted(own, partial[k], work), flip_ref
        product = panel_product(
            inverse_blocks, k, work.take(), residue, residue_flip, None, row_parts, None, bf16,
            f"inverse_{k}",
        )
        if k > 0:
            work.want((factor_blocks, pair_slot(k - 1, k)))
        solved[k] = row_sum(product, work)
        rounded[k] = solved[k].astype(bf16)
        early = [(e, factor(e, k)) for e in range(k - 2, -1, -1)]
        ahead += early
        if k == panels - 1:
            work.pieces += [score(0, i) for i in range(chunks)]
        if k > 0:
            place = len(work.pieces) - (0 if k == 1 else chunks)
            place = max(place, 0)
            later = [score(k, i) for i in range(chunks)]
            early = [piece for _, piece in early]
            work.pieces[place:place] = early[:1] + later + early[1:]
    work.rest()
    estimate = scattered(finished(first, rounded[0], totals, places))
    alpha = jnp.stack(solved).reshape(panels, col_tiles, tile_size, width_out)
    return (alpha, estimate)


def solution(mesh):
    in_specs = (
        P(None, None, "row", None, "col"),
        P(None, None, "col", None, "row"),
        P(None, None, "row", None),
        P(None, "col", None),
        P(None, "col"),
        P("row", None),
        P("row"),
    )
    out_specs = (P(None, None, "col", None), P(("row", "col"), None))
    return jax.shard_map(shards, mesh=mesh, in_specs=in_specs, out_specs=out_specs, check_vma=False)
```

time: 471 us -> 186 us (0.39); the launches traced: 462 us -> 183 us
  waiting for transfers between devices: 226 us -> 35.2 us
  Pallas kernels: 0 us -> 96.3 us
  local copies, waits for them, and re-layouts: 93.4 us -> 5.23 us
  matrix products: 65.8 us -> 0 us
  blocking collectives: 45 us -> 0 us
  starting transfers between devices: 0.72 us -> 34.4 us
  between operations: 14.8 us -> 1.84 us
  other arithmetic: 17 us -> 10.6 us
    psum x4 -> x0, waiting for transfers between devices: 141 us -> none  [settle(): summed_rows = lax.psum(product_rows, 'row')]
    pallas_call x0 -> x28, Pallas kernels: none -> 96.3 us  [the longest x16 46.3 us: scored(): pl.pallas_call(body, in_specs=in_specs, out_specs=out_specs, out_shape=ou...]
    reduce_scatter x4 -> x0, waiting for transfers between devices: 84.6 us -> none  [the longest x3 53.6 us: subtract(): lax.psum_scatter(partial_value, 'col', scatter_dimension=0, tiled=True)]
    dot_general x11 -> x0, matrix products: 65.8 us -> none  [the longest x1 33.3 us: shards(): jnp.dot(kernel, paired, preferred_element_type=jnp.float32)]
    all_gather x3 -> x0, blocking collectives: 45 us -> none  [subtract(): return lax.all_gather(reduced, 'col', axis=0, tiled=True)]
    unnamed x37 -> x80, local copies, waits for them, and re-layouts: 42.4 us -> 3.14 us
    ppermute x0 -> x34, waiting for transfers between devices: none -> 35.2 us  [swap(): return lax.ppermute(value, axis, [(i, i ^ mask) for i in range(size)])]
    ppermute x0 -> x34, starting transfers between devices: none -> 34.4 us  [swap(): return lax.ppermute(value, axis, [(i, i ^ mask) for i in range(size)])]
  transfers between devices with their start and end apart: 8 -> 34, of which waited for: 7 -> 25; matrix products, arithmetic and copies ran while one was open for 19% -> 2% of each run, Pallas kernels for 0% -> 38%
where the time goes in v2:
time: 186 us; the launch traced here: 183 us
  Pallas kernels  96.3 us (52%)
  waiting for transfers between devices  35.2 us (19%)
  starting transfers between devices  34.4 us (18%)
  other arithmetic  10.6 us (6%)
  local copies, waits for them, and re-layouts  5.23 us (3%)
    pallas_call x16, Pallas kernels, scored(): pl.pallas_call(body, in_specs=in_specs, out_specs=out_specs, out_shape=ou...  46.3 us
    ppermute x34, waiting for transfers between devices, swap(): return lax.ppermute(value, axis, [(i, i ^ mask) for i in range(size)])  35.2 us
    ppermute x34, starting transfers between devices, swap(): return lax.ppermute(value, axis, [(i, i ^ mask) for i in range(size)])  34.4 us
    pallas_call x10, Pallas kernels, panel_product(): pl.pallas_call(body, in_specs=[smem] * len(flips) + [stays if kept is Non...  33.9 us
    pallas_call x1, Pallas kernels, gathered(): pl.pallas_call(body, in_specs=[smem, stays], out_specs=[stays] * (2 * chu...  13.1 us
  transfers between devices with their start and end apart: 34, of which 25 were waited for; matrix products, arithmetic and copies ran while one was open for 2% of the time, Pallas kernels for 38%

profile of v2, /device:TPU:0, one launch (start us, length us, event | category | flops | bytes accessed | tf_op | source)
XLA Modules:
  0.0 183.5 jit_solution(9702763467352022441)
XLA Ops:
  0.6 1.1 slice.107
  1.7 3.3 %inverse_3.1 = bf16[2,512,128]{2,1,0:T(8,128)(2,1)S(1)} custom-call(bf16[4,4,256,8,256]{4,3,2,1,0:T(8,128)(2,1)} %refs_1_.15, bf16[4,512,128]{2,1,0:T(8,128)(2,1)S(1)} %bitcast.69), custom_call_target="tpu_custom_call" | custom-call | flops 1073741824 | bytes 4194304 | tf_op jit(solution)/shard_map/inverse_3/pallas_call | solution.py:85
  5.0 3.0 %collective-permute-start.1 = (bf16[512,128]{1,0:T(8,128)(2,1)S(1)}, bf16[512,128]{1,0:T(8,128)(2,1)S(1)}, u32[]{:S(2)}, u32[]{:S(2)}) collective-permute-start(bf16[512,128]{1,0:T(8,128)(2,1)S(1)} %get-tuple-element.146), channel_id=1, source_target_pairs={{0,16},{8,24},{16,0},{24,8},{1,17},{9,25},{17,1},{25,9},{2,18},{10... | collective-permute-start | bytes 393224 | tf_op jit(solution)/shard_map/ppermute | solution.py:379
  8.1 1.5 collective-permute-start
  9.6 13.1 %gathered_0.1 = (bf16[1024,512]{1,0:T(8,128)(2,1)}, bf16[1024,512]{1,0:T(8,128)(2,1)}, bf16[1024,512]{1,0:T(8,128)(2,1)}, bf16[1024,512]{1,0:T(8,128)(2,1)}, f32...) custom-call(s32[4096]{0:T(1024)S(1)} %broadcast_subtract_fusion.located_ref, ...), custom_call_target="tpu_custom_call" | custom-call | bytes 52428800 | tf_op jit(solution)/shard_map/gathered_0/pallas_call | solution.py:175
  23.5 4.3 %collective-permute-done.2 = bf16[512,128]{1,0:T(8,128)(2,1)S(1)} collective-permute-done((bf16[512,128]{1,0:T(8,128)(2,1)S(1)}, bf16[512,128]{1,0:T(8,128)(2,1)S(1)}, u32[]{:S(2)}, u32[]{:S(2)}) %collective-permute-start.2) | collective-permute-done | bytes 131104 | tf_op jit(solution)/shard_map/ppermute | solution.py:379
  28.4 3.7 %factor_2_3.1 = bf16[4,512,128]{2,1,0:T(8,128)(2,1)S(1)} custom-call(s32[1]{0:T(128)} %bitcast.refs_0_, bf16[6,8,256,4,256]{4,3,2,1,0:T(4,128)(2,1)} %refs_0_.3, bf16[1,1024,128]{2,1,0:T(8,128)(2,1)S(1)} %pad_maximum_fusion.8.refs_2_), custom_call_target="tpu_custom_call" | custom-call | flops 1073741824 | bytes 4194304 | tf_op jit(solution)/shard_map/factor_2_3/pallas_call | solution.py:85
  32.4 1.3 collective-permute-done.4
  33.8 1.6 collective-permute-start.5
  35.5 3.7 %factor_1_3.1.refs_3_ = f32[4,512,128]{2,1,0:T(8,128)S(1)} custom-call(s32[1]{0:T(128)} %bitcast.refs_0_, bf16[6,8,256,4,256]{4,3,2,1,0:T(4,128)(2,1)} %refs_0_.3, bf16[1,1024,128]{2,1,0:T(8,128)(2,1)S(1)} %bitcast.66), custom_call_target="tpu_custom_call" | custom-call | flops 1073741824 | bytes 4194304 | tf_op jit(solution)/shard_map/factor_1_3/pallas_call | solution.py:85
  39.5 3.7 %collective-permute-start.6 = (bf16[1,512,128]{2,1,0:T(8,128)(2,1)S(1)}, bf16[1,512,128]{2,1,0:T(8,128)(2,1)S(1)}, u32[]{:S(2)}, u32[]{:S(2)}) collective-permute-start(bf16[1,512,128]{2,1,0:T(8,128)(2,1)S(1)} %add_convert_fusion.13), channel_id=1, source_target_pairs={{0,6},{1,7},{2,4},{3,5},{4,2},{5,3},{6,0},{7,1},{8,14},{9,15},{10,... | collective-permute-start | bytes 393224 | tf_op jit(solution)/shard_map/ppermute | solution.py:379
  43.2 2.6 %scored_3_0.1 = (f32[1024,128]{1,0:T(8,128)S(1)}, f32[4,1,256]{2,1,0:T(1,128)S(1)}) custom-call(s32[4]{0:T(128)S(1)} %get-tuple-element.81.slots_ref, bf16[1024,512]{1,0:T(8,128)(2,1)S(1)} %copy-done.6, f32[1024,128]{1,0:T(8,128)S(1)} %copy-done.8, bf16[16,256,512]{2,1,0:T(8,128)(2,1)S(1)} %copy-done, bf16[1024,128]{1,0:T(8,128)(2,1)S(1)} %fusion.6.refs_0_.refs_1_), custom_call_target="tpu_custom_call" | custom-call | flops 1610612736 | bytes 1048576 | tf_op jit(solution)/shard_map/scored_3_0/pallas_call | solution.py:274
  45.8 2.6 %scored_3_1.1.refs_2_ = f32[1024,128]{1,0:T(8,128)S(1)} custom-call(s32[4]{0:T(128)S(1)} %get-tuple-element.81.slots_ref, bf16[1024,512]{1,0:T(8,128)(2,1)S(1)} %copy-done.4, f32[1024,128]{1,0:T(8,128)S(1)} %copy-done.12, bf16[16,256,512]{2,1,0:T(8,128)(2,1)S(1)} %copy-done, f32[4,1,256]{2,1,0:T(1,128)S(1)} %get-tuple-element.77.refs_0_, ...), custom_call_target="tpu_custom_call" | custom-call | flops 1610612736 | bytes 1048576 | tf_op jit(solution)/shard_map/scored_3_1/pallas_call | solution.py:274
  48.4 1.0 fusion
  49.9 2.6 %scored_3_2.1.refs_2_ = f32[1024,128]{1,0:T(8,128)S(1)} custom-call(s32[4]{0:T(128)S(1)} %get-tuple-element.81.slots_ref, bf16[1024,512]{1,0:T(8,128)(2,1)S(1)} %copy-done.3, f32[1024,128]{1,0:T(8,128)S(1)} %copy-done.10, bf16[16,256,512]{2,1,0:T(8,128)(2,1)S(1)} %copy-done, f32[4,1,256]{2,1,0:T(1,128)S(1)} %get-tuple-element.77.refs_0_, ...), custom_call_target="tpu_custom_call" | custom-call | flops 1610612736 | bytes 1048576 | tf_op jit(solution)/shard_map/scored_3_2/pallas_call | solution.py:274
  52.5 1.9 %collective-permute-done.7 = bf16[1,512,128]{2,1,0:T(8,128)(2,1)S(1)} collective-permute-done((bf16[1,512,128]{2,1,0:T(8,128)(2,1)S(1)}, bf16[1,512,128]{2,1,0:T(8,128)(2,1)S(1)}, u32[]{:S(2)}, u32[]{:S(2)}) %collective-permute-start.7) | collective-permute-done | bytes 131104 | tf_op jit(solution)/shard_map/ppermute | solution.py:379
  54.6 1.5 collective-permute-done.8
  56.1 3.6 %inverse_2.1 = bf16[2,512,128]{2,1,0:T(8,128)(2,1)S(1)} custom-call(s32[1]{0:T(128)} %bitcast.refs_0_, bf16[4,4,256,8,256]{4,3,2,1,0:T(8,128)(2,1)} %refs_1_.15, bf16[4,512,128]{2,1,0:T(8,128)(2,1)S(1)} %pad_maximum_fusion.2.refs_2_), custom_call_target="tpu_custom_call" | custom-call | flops 1073741824 | bytes 4194304 | tf_op jit(solution)/shard_map/inverse_2/pallas_call | solution.py:85
  59.8 1.6 collective-permute-start.10
  61.9 2.6 %scored_3_3.1.refs_2_ = f32[1024,128]{1,0:T(8,128)S(1)} custom-call(s32[4]{0:T(128)S(1)} %get-tuple-element.81.slots_ref, bf16[1024,512]{1,0:T(8,128)(2,1)S(1)} %copy-done.5, f32[1024,128]{1,0:T(8,128)S(1)} %copy-done.14, bf16[16,256,512]{2,1,0:T(8,128)(2,1)S(1)} %copy-done, f32[4,1,256]{2,1,0:T(1,128)S(1)} %get-tuple-element.77.refs_0_, ...), custom_call_target="tpu_custom_call" | custom-call | flops 1610612736 | bytes 1048576 | tf_op jit(solution)/shard_map/scored_3_3/pallas_call | solution.py:274
  65.4 1.2 collective-permute-done.9
  67.8 3.6 %factor_0_3.1.refs_3_ = f32[4,512,128]{2,1,0:T(8,128)S(1)} custom-call(s32[1]{0:T(128)} %bitcast.refs_0_, bf16[6,8,256,4,256]{4,3,2,1,0:T(4,128)(2,1)} %refs_0_.3, bf16[1,1024,128]{2,1,0:T(8,128)(2,1)S(1)} %bitcast.67), custom_call_target="tpu_custom_call" | custom-call | flops 1073741824 | bytes 4194304 | tf_op jit(solution)/shard_map/factor_0_3/pallas_call | solution.py:85
  72.4 3.7 %factor_1_2.1 = bf16[4,512,128]{2,1,0:T(8,128)(2,1)S(1)} custom-call(s32[1]{0:T(128)} %bitcast.refs_0_, bf16[6,8,256,4,256]{4,3,2,1,0:T(4,128)(2,1)} %refs_0_.3, bf16[1,1024,128]{2,1,0:T(8,128)(2,1)S(1)} %pad_maximum_fusion.10.refs_2_, f32[4,512,128]{2,1,0:T(8,128)S(1)} %factor_1_3.1.refs_3_), custom_call_target="tpu_custom_call" | custom-call | flops 1073741824 | bytes 4194304 | tf_op jit(solution)/shard_map/factor_1_2/pallas_call | solution.py:85
  76.2 1.5 collective-permute-done.13
  78.3 3.6 %factor_0_2.1.refs_3_ = f32[4,512,128]{2,1,0:T(8,128)S(1)} custom-call(s32[1]{0:T(128)} %bitcast.refs_0_, bf16[6,8,256,4,256]{4,3,2,1,0:T(4,128)(2,1)} %refs_0_.3, bf16[1,1024,128]{2,1,0:T(8,128)(2,1)S(1)} %bitcast.68, f32[4,512,128]{2,1,0:T(8,128)S(1)} %factor_0_3.1.refs_3_), custom_call_target="tpu_custom_call" | custom-call | flops 1073741824 | bytes 4194304 | tf_op jit(solution)/shard_map/factor_0_2/pallas_call | solution.py:85
  81.9 1.5 collective-permute-done.14
  83.4 1.6 collective-permute-start.15
  85.0 3.1 %scored_2_0.1 = (f32[1024,128]{1,0:T(8,128)S(1)}, f32[4,1,256]{2,1,0:T(1,128)S(1)}) custom-call(s32[4]{0:T(128)S(1)} %get-tuple-element.96.slots_ref, bf16[1024,512]{1,0:T(8,128)(2,1)S(1)} %copy-done.6, f32[1024,128]{1,0:T(8,128)S(1)} %copy-done.8, bf16[16,256,512]{2,1,0:T(8,128)(2,1)S(1)} %copy-done, bf16[1024,128]{1,0:T(8,128)(2,1)S(1)} %fusion.5.refs_0_.refs_1_, ...), custom_call_target="tpu_custom_call" | custom-call | flops 1610612736 | bytes 1048576 | tf_op jit(solution)/shard_map/scored_2_0/pallas_call | solution.py:274
  88.2 2.9 %scored_2_1.1.refs_2_ = f32[1024,128]{1,0:T(8,128)S(1)} custom-call(s32[4]{0:T(128)S(1)} %get-tuple-element.96.slots_ref, bf16[1024,512]{1,0:T(8,128)(2,1)S(1)} %copy-done.4, f32[1024,128]{1,0:T(8,128)S(1)} %copy-done.12, bf16[16,256,512]{2,1,0:T(8,128)(2,1)S(1)} %copy-done, f32[4,1,256]{2,1,0:T(1,128)S(1)} %get-tuple-element.92.refs_0_, ...), custom_call_target="tpu_custom_call" | custom-call | flops 1610612736 | bytes 1048576 | tf_op jit(solution)/shard_map/scored_2_1/pallas_call | solution.py:274
  91.1 1.1 fusion.1
  93.0 2.9 %scored_2_2.1.refs_2_ = f32[1024,128]{1,0:T(8,128)S(1)} custom-call(s32[4]{0:T(128)S(1)} %get-tuple-element.96.slots_ref, bf16[1024,512]{1,0:T(8,128)(2,1)S(1)} %copy-done.3, f32[1024,128]{1,0:T(8,128)S(1)} %copy-done.10, bf16[16,256,512]{2,1,0:T(8,128)(2,1)S(1)} %copy-done, f32[4,1,256]{2,1,0:T(1,128)S(1)} %get-tuple-element.92.refs_0_, ...), custom_call_target="tpu_custom_call" | custom-call | flops 1610612736 | bytes 1048576 | tf_op jit(solution)/shard_map/scored_2_2/pallas_call | solution.py:274
  95.9 1.4 collective-permute-done.16
  97.4 1.5 collective-permute-done.17
  99.0 3.3 %inverse_1.1 = bf16[2,512,128]{2,1,0:T(8,128)(2,1)S(1)} custom-call(s32[1]{0:T(128)} %bitcast.refs_0_, bf16[4,4,256,8,256]{4,3,2,1,0:T(8,128)(2,1)} %refs_1_.15, bf16[4,512,128]{2,1,0:T(8,128)(2,1)S(1)} %pad_maximum_fusion.4.refs_2_), custom_call_target="tpu_custom_call" | custom-call | flops 1073741824 | bytes 4194304 | tf_op jit(solution)/shard_map/inverse_1/pallas_call | solution.py:85
  103.0 1.5 collective-permute-start.18
  104.5 2.9 %scored_2_3.1.refs_2_ = f32[1024,128]{1,0:T(8,128)S(1)} custom-call(s32[4]{0:T(128)S(1)} %get-tuple-element.96.slots_ref, bf16[1024,512]{1,0:T(8,128)(2,1)S(1)} %copy-done.5, f32[1024,128]{1,0:T(8,128)S(1)} %copy-done.14, bf16[16,256,512]{2,1,0:T(8,128)(2,1)S(1)} %copy-done, f32[4,1,256]{2,1,0:T(1,128)S(1)} %get-tuple-element.92.refs_0_, ...), custom_call_target="tpu_custom_call" | custom-call | flops 1610612736 | bytes 1048576 | tf_op jit(solution)/shard_map/scored_2_3/pallas_call | solution.py:274
  108.4 1.6 collective-permute-start.21
  109.9 1.3 collective-permute-start.20
  111.3 4.0 %scored_0_0.1 = (bf16[1024,1024]{1,0:T(8,128)(2,1)}, f32[4,1,256]{2,1,0:T(1,128)S(1)}, bf16[8,256,4,256]{3,2,1,0:T(4,128)(2,1)S(1)}) custom-call(s32[4]{0:T(128)S(1)} %get-tuple-element.107.slots_ref, bf16[1024,512]{1,0:T(8,128)(2,1)S(1)} %copy-done.6, f32[1024,128]{1,0:T(8,128)S(1)} %copy-done.8, bf16[16,256,512]{2,1,0:T(8,128)(2,1)S(1)} %copy-done, ...), custom_call_target="tpu_custom_call" | custom-call | flops 1610612736 | bytes 1048576 | tf_op jit(solution)/shard_map/scored_0_0/pallas_call | solution.py:274
  116.8 2.2 %factor_0_1.1 = bf16[4,512,128]{2,1,0:T(8,128)(2,1)S(1)} custom-call(s32[1]{0:T(128)} %bitcast.refs_0_, bf16[8,256,4,256]{3,2,1,0:T(4,128)(2,1)S(1)} %get-tuple-element.100.refs_1_, bf16[1,1024,128]{2,1,0:T(8,128)(2,1)S(1)} %pad_maximum_fusion.12.refs_2_, f32[4,512,128]{2,1,0:T(8,128)S(1)} %factor_0_2.1.refs_3_), custom_call_target="tpu_custom_call" | custom-call | flops 1073741824 | bytes 4194304 | tf_op jit(solution)/shard_map/factor_0_1/pallas_call | solution.py:85
  120.6 1.1 fusion.4.refs_0_.refs_1_
  122.4 1.1 add_convert_fusion.2
  124.3 2.2 %copy-done.1 = bf16[16,256,512]{2,1,0:T(8,128)(2,1)S(1)} copy-done((bf16[16,256,512]{2,1,0:T(8,128)(2,1)S(1)}, bf16[16,256,512]{2,1,0:T(8,128)(2,1)}, u32[]{:S(2)}) %copy-start.1) | copy-done | bytes 4194328
  126.5 2.7 %scored_0_1.1.refs_1_ = bf16[1024,1024]{1,0:T(8,128)(2,1)} custom-call(s32[4]{0:T(128)S(1)} %get-tuple-element.107.slots_ref, bf16[1024,512]{1,0:T(8,128)(2,1)S(1)} %copy-done.4, f32[1024,128]{1,0:T(8,128)S(1)} %copy-done.13, bf16[16,256,512]{2,1,0:T(8,128)(2,1)S(1)} %copy-done.1, f32[4,1,256]{2,1,0:T(1,128)S(1)} %get-tuple-element.105.refs_0_), custom_call_target="tpu_custom_call" | custom-call | flops 1610612736 | bytes 1048576 | tf_op jit(solution)/shard_map/scored_0_1/pallas_call | solution.py:274
  129.2 2.3 %collective-permute-start.24 = (bf16[1,512,128]{2,1,0:T(8,128)(2,1)S(1)}, bf16[1,512,128]{2,1,0:T(8,128)(2,1)S(1)}, u32[]{:S(2)}, u32[]{:S(2)}) collective-permute-start(bf16[1,512,128]{2,1,0:T(8,128)(2,1)S(1)} %add_convert_fusion.7), channel_id=1, source_target_pairs={{0,6},{1,7},{2,4},{3,5},{4,2},{5,3},{6,0},{7,1},{8,14},{9,15},{10,... | collective-permute-start | bytes 393224 | tf_op jit(solution)/shard_map/ppermute | solution.py:379
  131.6 2.8 %scored_0_3.1.refs_3_ = bf16[1024,1024]{1,0:T(8,128)(2,1)} custom-call(s32[4]{0:T(128)S(1)} %get-tuple-element.107.slots_ref, bf16[1024,512]{1,0:T(8,128)(2,1)S(1)} %copy-done.5, f32[1024,128]{1,0:T(8,128)S(1)} %copy-done.15, bf16[16,256,512]{2,1,0:T(8,128)(2,1)S(1)} %copy-done.2, f32[4,1,256]{2,1,0:T(1,128)S(1)} %get-tuple-element.105.refs_0_), custom_call_target="tpu_custom_call" | custom-call | flops 1610612736 | bytes 1048576 | tf_op jit(solution)/shard_map/scored_0_3/pallas_call | solution.py:274
  134.4 2.7 %scored_0_2.1.refs_2_ = bf16[1024,1024]{1,0:T(8,128)(2,1)} custom-call(s32[4]{0:T(128)S(1)} %get-tuple-element.107.slots_ref, bf16[1024,512]{1,0:T(8,128)(2,1)S(1)} %copy-done.3, f32[1024,128]{1,0:T(8,128)S(1)} %copy-done.11, bf16[16,256,512]{2,1,0:T(8,128)(2,1)S(1)} %copy-done.2, f32[4,1,256]{2,1,0:T(1,128)S(1)} %get-tuple-element.105.refs_0_), custom_call_target="tpu_custom_call" | custom-call | flops 1610612736 | bytes 1048576 | tf_op jit(solution)/shard_map/scored_0_2/pallas_call | solution.py:274
  137.1 1.0 fusion.2
  138.1 1.7 collective-permute-start.25
  139.8 2.9 %scored_1_0.1 = (f32[1024,128]{1,0:T(8,128)S(1)}, f32[4,1,256]{2,1,0:T(1,128)S(1)}) custom-call(s32[4]{0:T(128)S(1)} %get-tuple-element.117.slots_ref, bf16[1024,512]{1,0:T(8,128)(2,1)S(1)} %copy-done.7, f32[1024,128]{1,0:T(8,128)S(1)} %copy-done.9, bf16[16,256,512]{2,1,0:T(8,128)(2,1)S(1)} %copy-done.2, bf16[1024,128]{1,0:T(8,128)(2,1)S(1)} %fusion.4.refs_0_.refs_1_, ...), custom_call_target="tpu_custom_call" | custom-call | flops 1610612736 | bytes 1048576 | tf_op jit(solution)/shard_map/scored_1_0/pallas_call | solution.py:274
  143.3 2.9 %scored_1_3.1.refs_8_ = f32[1024,128]{1,0:T(8,128)S(1)} custom-call(s32[4]{0:T(128)S(1)} %get-tuple-element.117.slots_ref, bf16[1024,512]{1,0:T(8,128)(2,1)S(1)} %copy-done.5, f32[1024,128]{1,0:T(8,128)S(1)} %copy-done.15, bf16[16,256,512]{2,1,0:T(8,128)(2,1)S(1)} %copy-done.2, f32[4,1,256]{2,1,0:T(1,128)S(1)} %get-tuple-element.114.refs_0_, ...), custom_call_target="tpu_custom_call" | custom-call | flops 1610612736 | bytes 1048576 | tf_op jit(solution)/shard_map/scored_1_3/pallas_call | solution.py:274
  146.3 3.3 %inverse_0.1 = bf16[2,512,128]{2,1,0:T(8,128)(2,1)S(1)} custom-call(s32[1]{0:T(128)} %bitcast.refs_0_, bf16[4,4,256,8,256]{4,3,2,1,0:T(8,128)(2,1)} %refs_1_.15, bf16[4,512,128]{2,1,0:T(8,128)(2,1)S(1)} %pad_maximum_fusion.6.refs_2_), custom_call_target="tpu_custom_call" | custom-call | flops 1073741824 | bytes 4194304 | tf_op jit(solution)/shard_map/inverse_0/pallas_call | solution.py:85
  149.7 1.0 collective-permute-start.28
  151.2 3.1 %scored_1_1.1.refs_6_ = f32[1024,128]{1,0:T(8,128)S(1)} custom-call(s32[4]{0:T(128)S(1)} %get-tuple-element.117.slots_ref, bf16[1024,512]{1,0:T(8,128)(2,1)S(1)} %copy-done.4, f32[1024,128]{1,0:T(8,128)S(1)} %copy-done.13, bf16[16,256,512]{2,1,0:T(8,128)(2,1)S(1)} %copy-done.2, f32[4,1,256]{2,1,0:T(1,128)S(1)} %get-tuple-element.114.refs_0_, ...), custom_call_target="tpu_custom_call" | custom-call | flops 1610612736 | bytes 1048576 | tf_op jit(solution)/shard_map/scored_1_1/pallas_call | solution.py:274
  154.3 1.3 collective-permute-done.28
  156.9 1.1 collective-permute-start.29
  158.1 2.9 %scored_1_2.1.refs_7_ = f32[1024,128]{1,0:T(8,128)S(1)} custom-call(s32[4]{0:T(128)S(1)} %get-tuple-element.117.slots_ref, bf16[1024,512]{1,0:T(8,128)(2,1)S(1)} %copy-done.3, f32[1024,128]{1,0:T(8,128)S(1)} %copy-done.11, bf16[16,256,512]{2,1,0:T(8,128)(2,1)S(1)} %copy-done.2, f32[4,1,256]{2,1,0:T(1,128)S(1)} %get-tuple-element.114.refs_0_, ...), custom_call_target="tpu_custom_call" | custom-call | flops 1610612736 | bytes 1048576 | tf_op jit(solution)/shard_map/scored_1_2/pallas_call | solution.py:274
  162.0 2.9 %finished.1 = bf16[8,512,128]{2,1,0:T(8,128)(2,1)S(1)} custom-call(s32[8]{0:T(128)S(1)} %broadcast_xor_fusion.places_ref, bf16[1024,1024]{1,0:T(8,128)(2,1)S(1)} %copy-done.26, bf16[1024,1024]{1,0:T(8,128)(2,1)S(1)} %copy-done.16, bf16[1024,1024]{1,0:T(8,128)(2,1)S(1)} %copy-done.18, bf16[1024,1024]{1,0:T(8,128)(2,1)S(1)} %copy-done.17, ...), custom_call_target="tpu_custom_call" | custom-call | flops 2147483648 | bytes 8388608 | tf_op jit(solution)/shard_map/finished/pallas_call | solution.py:311
  165.2 1.8 collective-permute-done.31
  167.2 1.6 collective-permute-start.32
  169.0 6.6 %collective-permute-done.32 = bf16[2,512,128]{2,1,0:T(8,128)(2,1)S(1)} collective-permute-done((bf16[2,512,128]{2,1,0:T(8,128)(2,1)S(1)}, bf16[2,512,128]{2,1,0:T(8,128)(2,1)S(1)}, u32[]{:S(2)}, u32[]{:S(2)}) %collective-permute-start.32) | collective-permute-done | bytes 262176 | tf_op jit(solution)/shard_map/ppermute | solution.py:379
  175.7 2.2 %collective-permute-start.33 = (bf16[1,512,128]{2,1,0:T(8,128)(2,1)S(1)}, bf16[1,512,128]{2,1,0:T(8,128)(2,1)S(1)}, u32[]{:S(2)}, u32[]{:S(2)}) collective-permute-start(bf16[1,512,128]{2,1,0:T(8,128)(2,1)S(1)} %slice.162), channel_id=1, source_target_pairs={{0,6},{1,7},{2,4},{3,5},{4,2},{5,3},{6,0},{7,1},{8,14},{9,15},{10,... | collective-permute-start | bytes 393224 | tf_op jit(solution)/shard_map/ppermute | solution.py:379
  177.9 1.5 pad_maximum_fusion
  179.4 3.2 %collective-permute-done.33 = bf16[1,512,128]{2,1,0:T(8,128)(2,1)S(1)} collective-permute-done((bf16[1,512,128]{2,1,0:T(8,128)(2,1)S(1)}, bf16[1,512,128]{2,1,0:T(8,128)(2,1)S(1)}, u32[]{:S(2)}, u32[]{:S(2)}) %collective-permute-start.33) | collective-permute-done | bytes 131104 | tf_op jit(solution)/shard_map/ppermute | solution.py:379
  (171 shorter events, 18.8 us)
Async XLA Ops:
  1.7 7.9 %copy-start.37 = (s32[4096]{0:T(1024)S(1)}, s32[4096]{0:T(1024)}, u32[]{:S(2)}) copy-start(s32[4096]{0:T(1024)} %param.14) | copy-start | bytes 49156
  5.0 17.6 %collective-permute-start.1 = (bf16[512,128]{1,0:T(8,128)(2,1)S(1)}, bf16[512,128]{1,0:T(8,128)(2,1)S(1)}, u32[]{:S(2)}, u32[]{:S(2)}) collective-permute-start(bf16[512,128]{1,0:T(8,128)(2,1)S(1)} %get-tuple-element.146), channel_id=1, source_target_pairs={{0,16},{8,24},{16,0},{24,8},{1,17},{9,25},{17,1},{25,9},{2,18},{10... | collective-permute-start | bytes 393224 | tf_op jit(solution)/shard_map/ppermute | solution.py:379
  8.1 14.6 %collective-permute-start = (bf16[512,128]{1,0:T(8,128)(2,1)S(1)}, bf16[512,128]{1,0:T(8,128)(2,1)S(1)}, u32[]{:S(2)}, u32[]{:S(2)}) collective-permute-start(bf16[512,128]{1,0:T(8,128)(2,1)S(1)} %get-tuple-element.147), channel_id=1, source_target_pairs={{0,8},{8,0},{16,24},{24,16},{1,9},{9,1},{17,25},{25,17},{2,10},{10... | collective-permute-start | bytes 393224 | tf_op jit(solution)/shard_map/ppermute | solution.py:379
  22.8 5.0 %collective-permute-start.2 = (bf16[512,128]{1,0:T(8,128)(2,1)S(1)}, bf16[512,128]{1,0:T(8,128)(2,1)S(1)}, u32[]{:S(2)}, u32[]{:S(2)}) collective-permute-start(bf16[512,128]{1,0:T(8,128)(2,1)S(1)} %get-tuple-element.144), channel_id=1, source_target_pairs={{0,16},{8,24},{16,0},{24,8},{1,17},{9,25},{17,1},{25,9},{2,18},{10... | collective-permute-start | bytes 393224 | tf_op jit(solution)/shard_map/ppermute | solution.py:379
  23.4 5.0 %collective-permute-start.3 = (bf16[512,128]{1,0:T(8,128)(2,1)S(1)}, bf16[512,128]{1,0:T(8,128)(2,1)S(1)}, u32[]{:S(2)}, u32[]{:S(2)}) collective-permute-start(bf16[512,128]{1,0:T(8,128)(2,1)S(1)} %get-tuple-element.145), channel_id=1, source_target_pairs={{0,8},{8,0},{16,24},{24,16},{1,9},{9,1},{17,25},{25,17},{2,10},{10... | collective-permute-start | bytes 393224 | tf_op jit(solution)/shard_map/ppermute | solution.py:379
  27.9 7.6 %copy-start.31 = (f32[512,128]{1,0:T(8,128)}, f32[512,128]{1,0:T(8,128)S(1)}, u32[]{:S(2)}) copy-start(f32[512,128]{1,0:T(8,128)S(1)} %get-tuple-element.141) | copy-start | bytes 786436
  28.4 7.1 %copy-start.33 = (f32[512,128]{1,0:T(8,128)}, f32[512,128]{1,0:T(8,128)S(1)}, u32[]{:S(2)}) copy-start(f32[512,128]{1,0:T(8,128)S(1)} %get-tuple-element.143) | copy-start | bytes 786436
  28.4 3.8 %copy-start.38 = (s32[16,1]{0,1:T(1,128)S(1)}, s32[16,1]{0,1:T(1,128)}, u32[]{:S(2)}) copy-start(s32[16,1]{0,1:T(1,128)} %param.12) | copy-start | bytes 196
  32.1 1.6 collective-permute-start.4
  33.8 5.6 %collective-permute-start.5 = (bf16[1,512,128]{2,1,0:T(8,128)(2,1)S(1)}, bf16[1,512,128]{2,1,0:T(8,128)(2,1)S(1)}, u32[]{:S(2)}, u32[]{:S(2)}) collective-permute-start(bf16[1,512,128]{2,1,0:T(8,128)(2,1)S(1)} %slice.142), channel_id=1, source_target_pairs={{0,2},{1,3},{2,0},{3,1},{4,6},{5,7},{6,4},{7,5},{8,10},{9,11},{10,... | collective-permute-start | bytes 393224 | tf_op jit(solution)/shard_map/ppermute | solution.py:379
  35.5 7.6 %copy-start = (bf16[16,256,512]{2,1,0:T(8,128)(2,1)S(1)}, bf16[16,256,512]{2,1,0:T(8,128)(2,1)}, u32[]{:S(2)}) copy-start(bf16[16,256,512]{2,1,0:T(8,128)(2,1)} %center_ref.31) | copy-start | bytes 12582916
  35.5 7.6 %copy-start.6 = (bf16[1024,512]{1,0:T(8,128)(2,1)S(1)}, bf16[1024,512]{1,0:T(8,128)(2,1)}, u32[]{:S(2)}) copy-start(bf16[1024,512]{1,0:T(8,128)(2,1)} %get-tuple-element.62.span_ref) | copy-start | bytes 3145732
  35.5 7.6 %copy-start.8 = (f32[1024,128]{1,0:T(8,128)S(1)}, f32[1024,128]{1,0:T(8,128)}, u32[]{:S(2)}) copy-start(f32[1024,128]{1,0:T(8,128)} %get-tuple-element.66.norm_ref) | copy-start | bytes 1572868
  39.5 9.0 %collective-permute-start.6 = (bf16[1,512,128]{2,1,0:T(8,128)(2,1)S(1)}, bf16[1,512,128]{2,1,0:T(8,128)(2,1)S(1)}, u32[]{:S(2)}, u32[]{:S(2)}) collective-permute-start(bf16[1,512,128]{2,1,0:T(8,128)(2,1)S(1)} %add_convert_fusion.13), channel_id=1, source_target_pairs={{0,6},{1,7},{2,4},{3,5},{4,2},{5,3},{6,0},{7,1},{8,14},{9,15},{10,... | collective-permute-start | bytes 393224 | tf_op jit(solution)/shard_map/ppermute | solution.py:379
  45.8 4.1 %copy-start.3 = (bf16[1024,512]{1,0:T(8,128)(2,1)S(1)}, bf16[1024,512]{1,0:T(8,128)(2,1)}, u32[]{:S(2)}) copy-start(bf16[1024,512]{1,0:T(8,128)(2,1)} %get-tuple-element.64.span_ref) | copy-start | bytes 3145732
  45.8 4.1 %copy-start.10 = (f32[1024,128]{1,0:T(8,128)S(1)}, f32[1024,128]{1,0:T(8,128)}, u32[]{:S(2)}) copy-start(f32[1024,128]{1,0:T(8,128)} %get-tuple-element.68.norm_ref) | copy-start | bytes 1572868
  49.4 5.0 %collective-permute-start.7 = (bf16[1,512,128]{2,1,0:T(8,128)(2,1)S(1)}, bf16[1,512,128]{2,1,0:T(8,128)(2,1)S(1)}, u32[]{:S(2)}, u32[]{:S(2)}) collective-permute-start(bf16[1,512,128]{2,1,0:T(8,128)(2,1)S(1)} %fusion), channel_id=1, source_target_pairs={{0,2},{1,3},{2,0},{3,1},{4,6},{5,7},{6,4},{7,5},{8,10},{9,11},{10,... | collective-permute-start | bytes 393224 | tf_op jit(solution)/shard_map/ppermute | solution.py:379
  54.5 1.6 collective-permute-start.8
  56.1 5.8 %copy-start.5 = (bf16[1024,512]{1,0:T(8,128)(2,1)S(1)}, bf16[1024,512]{1,0:T(8,128)(2,1)}, u32[]{:S(2)}) copy-start(bf16[1024,512]{1,0:T(8,128)(2,1)} %get-tuple-element.65.span_ref) | copy-start | bytes 3145732
  56.1 5.8 %copy-start.14 = (f32[1024,128]{1,0:T(8,128)S(1)}, f32[1024,128]{1,0:T(8,128)}, u32[]{:S(2)}) copy-start(f32[1024,128]{1,0:T(8,128)} %get-tuple-element.69.norm_ref) | copy-start | bytes 1572868
  59.8 5.6 %collective-permute-start.10 = (bf16[512,128]{1,0:T(8,128)(2,1)S(1)}, bf16[512,128]{1,0:T(8,128)(2,1)S(1)}, u32[]{:S(2)}, u32[]{:S(2)}) collective-permute-start(bf16[512,128]{1,0:T(8,128)(2,1)S(1)} %get-tuple-element.138), channel_id=1, source_target_pairs={{0,16},{8,24},{16,0},{24,8},{1,17},{9,25},{17,1},{25,9},{2,18},{10... | collective-permute-start | bytes 393224 | tf_op jit(solution)/shard_map/ppermute | solution.py:379
  61.3 5.3 %collective-permute-start.9 = (bf16[512,128]{1,0:T(8,128)(2,1)S(1)}, bf16[512,128]{1,0:T(8,128)(2,1)S(1)}, u32[]{:S(2)}, u32[]{:S(2)}) collective-permute-start(bf16[512,128]{1,0:T(8,128)(2,1)S(1)} %get-tuple-element.139), channel_id=1, source_target_pairs={{0,8},{8,0},{16,24},{24,16},{1,9},{9,1},{17,25},{25,17},{2,10},{10... | collective-permute-start | bytes 393224 | tf_op jit(solution)/shard_map/ppermute | solution.py:379
  66.7 5.0 %collective-permute-start.12 = (bf16[512,128]{1,0:T(8,128)(2,1)S(1)}, bf16[512,128]{1,0:T(8,128)(2,1)S(1)}, u32[]{:S(2)}, u32[]{:S(2)}) collective-permute-start(bf16[512,128]{1,0:T(8,128)(2,1)S(1)} %get-tuple-element.136), channel_id=1, source_target_pairs={{0,8},{8,0},{16,24},{24,16},{1,9},{9,1},{17,25},{25,17},{2,10},{10... | collective-permute-start | bytes 393224 | tf_op jit(solution)/shard_map/ppermute | solution.py:379
  67.3 5.0 %collective-permute-start.11 = (bf16[512,128]{1,0:T(8,128)(2,1)S(1)}, bf16[512,128]{1,0:T(8,128)(2,1)S(1)}, u32[]{:S(2)}, u32[]{:S(2)}) collective-permute-start(bf16[512,128]{1,0:T(8,128)(2,1)S(1)} %get-tuple-element.137), channel_id=1, source_target_pairs={{0,16},{8,24},{16,0},{24,8},{1,17},{9,25},{17,1},{25,9},{2,18},{10... | collective-permute-start | bytes 393224 | tf_op jit(solution)/shard_map/ppermute | solution.py:379
  72.3 6.0 %copy-start.29 = (f32[512,128]{1,0:T(8,128)}, f32[512,128]{1,0:T(8,128)S(1)}, u32[]{:S(2)}) copy-start(f32[512,128]{1,0:T(8,128)S(1)} %get-tuple-element.152) | copy-start | bytes 786436
  76.1 1.6 collective-permute-start.13
  77.8 5.6 %collective-permute-start.14 = (bf16[1,512,128]{2,1,0:T(8,128)(2,1)S(1)}, bf16[1,512,128]{2,1,0:T(8,128)(2,1)S(1)}, u32[]{:S(2)}, u32[]{:S(2)}) collective-permute-start(bf16[1,512,128]{2,1,0:T(8,128)(2,1)S(1)} %slice.148), channel_id=1, source_target_pairs={{0,2},{1,3},{2,0},{3,1},{4,6},{5,7},{6,4},{7,5},{8,10},{9,11},{10,... | collective-permute-start | bytes 393224 | tf_op jit(solution)/shard_map/ppermute | solution.py:379
  83.4 7.7 %collective-permute-start.15 = (bf16[1,512,128]{2,1,0:T(8,128)(2,1)S(1)}, bf16[1,512,128]{2,1,0:T(8,128)(2,1)S(1)}, u32[]{:S(2)}, u32[]{:S(2)}) collective-permute-start(bf16[1,512,128]{2,1,0:T(8,128)(2,1)S(1)} %add_convert_fusion.10), channel_id=1, source_target_pairs={{0,6},{1,7},{2,4},{3,5},{4,2},{5,3},{6,0},{7,1},{8,14},{9,15},{10,... | collective-permute-start | bytes 393224 | tf_op jit(solution)/shard_map/ppermute | solution.py:379
  92.3 5.0 %collective-permute-start.16 = (bf16[1,512,128]{2,1,0:T(8,128)(2,1)S(1)}, bf16[1,512,128]{2,1,0:T(8,128)(2,1)S(1)}, u32[]{:S(2)}, u32[]{:S(2)}) collective-permute-start(bf16[1,512,128]{2,1,0:T(8,128)(2,1)S(1)} %fusion.1), channel_id=1, source_target_pairs={{0,2},{1,3},{2,0},{3,1},{4,6},{5,7},{6,4},{7,5},{8,10},{9,11},{10,... | collective-permute-start | bytes 393224 | tf_op jit(solution)/shard_map/ppermute | solution.py:379
  95.9 6.4 %copy-start.19 = (f32[1024,128]{1,0:T(8,128)}, f32[1024,128]{1,0:T(8,128)S(1)}, u32[]{:S(2)}) copy-start(f32[1024,128]{1,0:T(8,128)S(1)} %scored_2_2.1.refs_2_) | copy-start | bytes 1572868
  97.3 1.6 collective-permute-start.17
  102.3 5.6 %collective-permute-start.19 = (bf16[512,128]{1,0:T(8,128)(2,1)S(1)}, bf16[512,128]{1,0:T(8,128)(2,1)S(1)}, u32[]{:S(2)}, u32[]{:S(2)}) collective-permute-start(bf16[512,128]{1,0:T(8,128)(2,1)S(1)} %get-tuple-element.130), channel_id=1, source_target_pairs={{0,16},{8,24},{16,0},{24,8},{1,17},{9,25},{17,1},{25,9},{2,18},{10... | collective-permute-start | bytes 393224 | tf_op jit(solution)/shard_map/ppermute | solution.py:379
  103.0 5.3 %collective-permute-start.18 = (bf16[512,128]{1,0:T(8,128)(2,1)S(1)}, bf16[512,128]{1,0:T(8,128)(2,1)S(1)}, u32[]{:S(2)}, u32[]{:S(2)}) collective-permute-start(bf16[512,128]{1,0:T(8,128)(2,1)S(1)} %get-tuple-element.131), channel_id=1, source_target_pairs={{0,8},{8,0},{16,24},{24,16},{1,9},{9,1},{17,25},{25,17},{2,10},{10... | collective-permute-start | bytes 393224 | tf_op jit(solution)/shard_map/ppermute | solution.py:379
  107.5 7.9 %copy-start.23 = (f32[1024,128]{1,0:T(8,128)}, f32[1024,128]{1,0:T(8,128)S(1)}, u32[]{:S(2)}) copy-start(f32[1024,128]{1,0:T(8,128)S(1)} %scored_2_3.1.refs_2_) | copy-start | bytes 1572868
  108.4 7.0 %collective-permute-start.21 = (bf16[512,128]{1,0:T(8,128)(2,1)S(1)}, bf16[512,128]{1,0:T(8,128)(2,1)S(1)}, u32[]{:S(2)}, u32[]{:S(2)}) collective-permute-start(bf16[512,128]{1,0:T(8,128)(2,1)S(1)} %get-tuple-element.128), channel_id=1, source_target_pairs={{0,8},{8,0},{16,24},{24,16},{1,9},{9,1},{17,25},{25,17},{2,10},{10... | collective-permute-start | bytes 393224 | tf_op jit(solution)/shard_map/ppermute | solution.py:379
  109.9 5.4 %collective-permute-start.20 = (bf16[512,128]{1,0:T(8,128)(2,1)S(1)}, bf16[512,128]{1,0:T(8,128)(2,1)S(1)}, u32[]{:S(2)}, u32[]{:S(2)}) collective-permute-start(bf16[512,128]{1,0:T(8,128)(2,1)S(1)} %get-tuple-element.129), channel_id=1, source_target_pairs={{0,16},{8,24},{16,0},{24,8},{1,17},{9,25},{17,1},{25,9},{2,18},{10... | collective-permute-start | bytes 393224 | tf_op jit(solution)/shard_map/ppermute | solution.py:379
  120.6 1.9 %collective-permute-start.22 = (bf16[2,512,128]{2,1,0:T(8,128)(2,1)}, bf16[2,512,128]{2,1,0:T(8,128)(2,1)}, u32[]{:S(2)}, u32[]{:S(2)}) collective-permute-start(bf16[2,512,128]{2,1,0:T(8,128)(2,1)} %slice.152), channel_id=1, source_target_pairs={{0,1},{1,0},{2,3},{3,2},{4,5},{5,4},{6,7},{7,6},{8,9},{9,8},{10,11... | collective-permute-start | bytes 786440 | tf_op jit(solution)/shard_map/ppermute | solution.py:379
  120.6 3.7 %copy-start.13 = (f32[1024,128]{1,0:T(8,128)S(1)}, f32[1024,128]{1,0:T(8,128)}, u32[]{:S(2)}) copy-start(f32[1024,128]{1,0:T(8,128)} %get-tuple-element.67.norm_ref) | copy-start | bytes 1572868
  123.6 5.6 %collective-permute-start.23 = (bf16[1,512,128]{2,1,0:T(8,128)(2,1)S(1)}, bf16[1,512,128]{2,1,0:T(8,128)(2,1)S(1)}, u32[]{:S(2)}, u32[]{:S(2)}) collective-permute-start(bf16[1,512,128]{2,1,0:T(8,128)(2,1)S(1)} %slice.154), channel_id=1, source_target_pairs={{0,2},{1,3},{2,0},{3,1},{4,6},{5,7},{6,4},{7,5},{8,10},{9,11},{10,... | collective-permute-start | bytes 393224 | tf_op jit(solution)/shard_map/ppermute | solution.py:379
  126.5 5.1 %copy-start.2 = (bf16[16,256,512]{2,1,0:T(8,128)(2,1)S(1)}, bf16[16,256,512]{2,1,0:T(8,128)(2,1)}, u32[]{:S(2)}) copy-start(bf16[16,256,512]{2,1,0:T(8,128)(2,1)} %center_ref.31) | copy-start | bytes 12582916
  126.5 5.1 %copy-start.15 = (f32[1024,128]{1,0:T(8,128)S(1)}, f32[1024,128]{1,0:T(8,128)}, u32[]{:S(2)}) copy-start(f32[1024,128]{1,0:T(8,128)} %get-tuple-element.69.norm_ref) | copy-start | bytes 1572868
  129.2 5.2 %copy-start.11 = (f32[1024,128]{1,0:T(8,128)S(1)}, f32[1024,128]{1,0:T(8,128)}, u32[]{:S(2)}) copy-start(f32[1024,128]{1,0:T(8,128)} %get-tuple-element.68.norm_ref) | copy-start | bytes 1572868
  129.2 7.9 %collective-permute-start.24 = (bf16[1,512,128]{2,1,0:T(8,128)(2,1)S(1)}, bf16[1,512,128]{2,1,0:T(8,128)(2,1)S(1)}, u32[]{:S(2)}, u32[]{:S(2)}) collective-permute-start(bf16[1,512,128]{2,1,0:T(8,128)(2,1)S(1)} %add_convert_fusion.7), channel_id=1, source_target_pairs={{0,6},{1,7},{2,4},{3,5},{4,2},{5,3},{6,0},{7,1},{8,14},{9,15},{10,... | collective-permute-start | bytes 393224 | tf_op jit(solution)/shard_map/ppermute | solution.py:379
  134.4 5.4 %copy-start.7 = (bf16[1024,512]{1,0:T(8,128)(2,1)S(1)}, bf16[1024,512]{1,0:T(8,128)(2,1)}, u32[]{:S(2)}) copy-start(bf16[1024,512]{1,0:T(8,128)(2,1)} %get-tuple-element.62.span_ref) | copy-start | bytes 3145732
  134.4 5.4 %copy-start.9 = (f32[1024,128]{1,0:T(8,128)S(1)}, f32[1024,128]{1,0:T(8,128)}, u32[]{:S(2)}) copy-start(f32[1024,128]{1,0:T(8,128)} %get-tuple-element.66.norm_ref) | copy-start | bytes 1572868
  134.4 5.3 %copy-start.28 = (f32[1024,128]{1,0:T(8,128)S(1)}, f32[1024,128]{1,0:T(8,128)}, u32[]{:S(2)}) copy-start(f32[1024,128]{1,0:T(8,128)} %copy-done.27) | copy-start | bytes 1572868
  138.1 5.0 %collective-permute-start.25 = (bf16[1,512,128]{2,1,0:T(8,128)(2,1)S(1)}, bf16[1,512,128]{2,1,0:T(8,128)(2,1)S(1)}, u32[]{:S(2)}, u32[]{:S(2)}) collective-permute-start(bf16[1,512,128]{2,1,0:T(8,128)(2,1)S(1)} %fusion.2), channel_id=1, source_target_pairs={{0,2},{1,3},{2,0},{3,1},{4,6},{5,7},{6,4},{7,5},{8,10},{9,11},{10,... | collective-permute-start | bytes 393224 | tf_op jit(solution)/shard_map/ppermute | solution.py:379
  143.2 3.0 %collective-permute-start.26 = (bf16[2,512,128]{2,1,0:T(8,128)(2,1)S(1)}, bf16[2,512,128]{2,1,0:T(8,128)(2,1)S(1)}, u32[]{:S(2)}, u32[]{:S(2)}) collective-permute-start(bf16[2,512,128]{2,1,0:T(8,128)(2,1)S(1)} %pad_maximum_fusion.13), channel_id=1, source_target_pairs={{0,1},{1,0},{2,3},{3,2},{4,5},{5,4},{6,7},{7,6},{8,9},{9,8},{10,11... | collective-permute-start | bytes 786440 | tf_op jit(solution)/shard_map/ppermute | solution.py:379
  146.3 4.9 %copy-start.22 = (f32[1024,128]{1,0:T(8,128)S(1)}, f32[1024,128]{1,0:T(8,128)}, u32[]{:S(2)}) copy-start(f32[1024,128]{1,0:T(8,128)} %copy-done.21) | copy-start | bytes 1572868
  149.7 5.9 %collective-permute-start.28 = (bf16[512,128]{1,0:T(8,128)(2,1)S(1)}, bf16[512,128]{1,0:T(8,128)(2,1)S(1)}, u32[]{:S(2)}, u32[]{:S(2)}) collective-permute-start(bf16[512,128]{1,0:T(8,128)(2,1)S(1)} %get-tuple-element.122), channel_id=1, source_target_pairs={{0,16},{8,24},{16,0},{24,8},{1,17},{9,25},{17,1},{25,9},{2,18},{10... | collective-permute-start | bytes 393224 | tf_op jit(solution)/shard_map/ppermute | solution.py:379
  150.6 7.4 %copy-start.20 = (f32[1024,128]{1,0:T(8,128)S(1)}, f32[1024,128]{1,0:T(8,128)}, u32[]{:S(2)}) copy-start(f32[1024,128]{1,0:T(8,128)} %copy-done.19) | copy-start | bytes 1572868
  150.6 5.6 %collective-permute-start.27 = (bf16[512,128]{1,0:T(8,128)(2,1)S(1)}, bf16[512,128]{1,0:T(8,128)(2,1)S(1)}, u32[]{:S(2)}, u32[]{:S(2)}) collective-permute-start(bf16[512,128]{1,0:T(8,128)(2,1)S(1)} %get-tuple-element.123), channel_id=1, source_target_pairs={{0,8},{8,0},{16,24},{24,16},{1,9},{9,1},{17,25},{25,17},{2,10},{10... | collective-permute-start | bytes 393224 | tf_op jit(solution)/shard_map/ppermute | solution.py:379
  156.3 5.0 %collective-permute-start.30 = (bf16[512,128]{1,0:T(8,128)(2,1)S(1)}, bf16[512,128]{1,0:T(8,128)(2,1)S(1)}, u32[]{:S(2)}, u32[]{:S(2)}) collective-permute-start(bf16[512,128]{1,0:T(8,128)(2,1)S(1)} %get-tuple-element.120), channel_id=1, source_target_pairs={{0,8},{8,0},{16,24},{24,16},{1,9},{9,1},{17,25},{25,17},{2,10},{10... | collective-permute-start | bytes 393224 | tf_op jit(solution)/shard_map/ppermute | solution.py:379
  156.9 5.0 %collective-permute-start.29 = (bf16[512,128]{1,0:T(8,128)(2,1)S(1)}, bf16[512,128]{1,0:T(8,128)(2,1)S(1)}, u32[]{:S(2)}, u32[]{:S(2)}) collective-permute-start(bf16[512,128]{1,0:T(8,128)(2,1)S(1)} %get-tuple-element.121), channel_id=1, source_target_pairs={{0,16},{8,24},{16,0},{24,8},{1,17},{9,25},{17,1},{25,9},{2,18},{10... | collective-permute-start | bytes 393224 | tf_op jit(solution)/shard_map/ppermute | solution.py:379
  158.0 3.9 %copy-start.16 = (bf16[1024,1024]{1,0:T(8,128)(2,1)S(1)}, bf16[1024,1024]{1,0:T(8,128)(2,1)}, u32[]{:S(2)}) copy-start(bf16[1024,1024]{1,0:T(8,128)(2,1)} %scored_0_1.1.refs_1_) | copy-start | bytes 6291460
  158.0 3.9 %copy-start.17 = (bf16[1024,1024]{1,0:T(8,128)(2,1)S(1)}, bf16[1024,1024]{1,0:T(8,128)(2,1)}, u32[]{:S(2)}) copy-start(bf16[1024,1024]{1,0:T(8,128)(2,1)} %scored_0_3.1.refs_3_) | copy-start | bytes 6291460
  158.0 4.0 %copy-start.18 = (bf16[1024,1024]{1,0:T(8,128)(2,1)S(1)}, bf16[1024,1024]{1,0:T(8,128)(2,1)}, u32[]{:S(2)}) copy-start(bf16[1024,1024]{1,0:T(8,128)(2,1)} %scored_0_2.1.refs_2_) | copy-start | bytes 6291460
  158.1 4.0 %copy-start.26 = (bf16[1024,1024]{1,0:T(8,128)(2,1)S(1)}, bf16[1024,1024]{1,0:T(8,128)(2,1)}, u32[]{:S(2)}) copy-start(bf16[1024,1024]{1,0:T(8,128)(2,1)} %get-tuple-element.101.refs_0_) | copy-start | bytes 6291460
  165.0 3.9 %copy-start.30 = (f32[512,128]{1,0:T(8,128)S(1)}, f32[512,128]{1,0:T(8,128)}, u32[]{:S(2)}) copy-start(f32[512,128]{1,0:T(8,128)} %copy-done.29) | copy-start | bytes 786436
  165.0 3.9 %copy-start.35 = (f32[512,128]{1,0:T(8,128)S(1)}, f32[512,128]{1,0:T(8,128)}, u32[]{:S(2)}) copy-start(f32[512,128]{1,0:T(8,128)} %get-tuple-element.125) | copy-start | bytes 786436
  165.0 3.9 %copy-start.36 = (f32[512,128]{1,0:T(8,128)S(1)}, f32[512,128]{1,0:T(8,128)}, u32[]{:S(2)}) copy-start(f32[512,128]{1,0:T(8,128)} %get-tuple-element.127) | copy-start | bytes 786436
  165.0 2.0 %collective-permute-start.31 = (bf16[4,512,128]{2,1,0:T(8,128)(2,1)S(1)}, bf16[4,512,128]{2,1,0:T(8,128)(2,1)S(1)}, u32[]{:S(2)}, u32[]{:S(2)}) collective-permute-start(bf16[4,512,128]{2,1,0:T(8,128)(2,1)S(1)} %slice.158), channel_id=1, source_target_pairs={{0,1},{1,0},{2,3},{3,2},{4,5},{5,4},{6,7},{7,6},{8,9},{9,8},{10,11... | collective-permute-start | bytes 1572872 | tf_op jit(solution)/shard_map/ppermute | solution.py:379
  167.2 8.4 %collective-permute-start.32 = (bf16[2,512,128]{2,1,0:T(8,128)(2,1)S(1)}, bf16[2,512,128]{2,1,0:T(8,128)(2,1)S(1)}, u32[]{:S(2)}, u32[]{:S(2)}) collective-permute-start(bf16[2,512,128]{2,1,0:T(8,128)(2,1)S(1)} %slice.160), channel_id=1, source_target_pairs={{0,2},{1,3},{2,0},{3,1},{4,6},{5,7},{6,4},{7,5},{8,10},{9,11},{10,... | collective-permute-start | bytes 786440 | tf_op jit(solution)/shard_map/ppermute | solution.py:379
  175.7 6.9 %collective-permute-start.33 = (bf16[1,512,128]{2,1,0:T(8,128)(2,1)S(1)}, bf16[1,512,128]{2,1,0:T(8,128)(2,1)S(1)}, u32[]{:S(2)}, u32[]{:S(2)}) collective-permute-start(bf16[1,512,128]{2,1,0:T(8,128)(2,1)S(1)} %slice.162), channel_id=1, source_target_pairs={{0,6},{1,7},{2,4},{3,5},{4,2},{5,3},{6,0},{7,1},{8,14},{9,15},{10,... | collective-permute-start | bytes 393224 | tf_op jit(solution)/shard_map/ppermute | solution.py:379
  (10 other events, 25.5 us)

commit v3 on v2

--- a/solution.py
+++ b/solution.py
@@ -138,7 +138,7 @@
             def fetch(i, carry):
                 for u in range(group):
                     at = i * group + u
-                    source = pl.multiple_of(located_ref[j * chunk + at] * cuts, cuts)
+                    source = pl.multiple_of(located_ref[j * chunk + at], cuts)
                     held[pl.ds(pl.multiple_of(at * cuts, cuts), cuts), :] = wide[pl.ds(source, cuts), :]
                 return carry
 
@@ -191,7 +191,7 @@
             flops=0, bytes_accessed=6 * rows * dim + 16 * count * dim, transcendentals=0
         ),
         name=name,
-    )(located, pltpu.with_memory_space_constraint(pool, pltpu.HBM))
+    )(located * cuts, pltpu.with_memory_space_constraint(pool, pltpu.HBM))
 
 
 def scored(span, norms, centers, center_sq, slots, weights, earlier, fetch, name):
@@ -232,23 +232,24 @@
             at = slice(i * step, (i + 1) * step)
             rows = span_ref[at, :]
             norm = jnp.concatenate([norm_ref[at, :]] * (size // 128), axis=1)
-            total = None if earlier is None else more_refs[1][at, :]
+            row_values = []
             for t in range(tiles):
                 slot = slots_ref[t]
                 crossed = lax.dot_general(
                     rows, center_ref[slot], (((1,), (1,)), ((), ())), preferred_element_type=f32
                 )
                 value = jnp.exp2((crossed * (-2.0 * scale) + sq_ref[t]) + norm).astype(bf16)
-                place = slice(t * size, (t + 1) * size)
                 if weights is None:
-                    values[i, :, place] = value
+                    values[i, :, t * size : (t + 1) * size] = value
                 else:
-                    part = jnp.dot(value, more_refs[0][place, :], preferred_element_type=f32)
-                    total = part if total is None else total + part
+                    row_values.append(value)
             if weights is None:
                 writes[i].start()
             else:
-                out_ref[at, :] = total
+                total = jnp.dot(
+                    jnp.concatenate(row_values, axis=1), more_refs[0][...], preferred_element_type=f32
+                )
+                out_ref[at, :] = total if earlier is None else total + more_refs[1][at, :]
         for copy in writes + copies:
             copy.wait()
 
@@ -508,7 +509,7 @@
                 first[i] = made
             return made, fetched
 
-        return Piece(2.9 if k > 0 else 2.7, make, True)
+        return Piece(2.5 if k > 0 else 2.7, make, True)
 
     def factor(early, k, kept=None):
         def make(before):
@@ -529,6 +530,7 @@
         return Piece(3.6, make)
 
     work.pieces += [gather(i, group) for i in range(0, chunks, group)]
+    work.pieces += [score(0, i) for i in range(chunks)]
     ahead = []
     for k in range(panels - 1, -1, -1):
         if k == panels - 1:
@@ -538,6 +540,8 @@
                 if early == k:
                     piece.run(None)
             factor(k, k + 1, work.take()).run(None)
+            if k > 0:
+                work.want((inverse_blocks, k))
             own = lax.dynamic_slice(
                 targets, (k, flip, 0, 0), (1, 1) + targets.shape[2:]
             )[0]
@@ -552,14 +556,10 @@
         rounded[k] = solved[k].astype(bf16)
         early = [(e, factor(e, k)) for e in range(k - 2, -1, -1)]
         ahead += early
-        if k == panels - 1:
-            work.pieces += [score(0, i) for i in range(chunks)]
         if k > 0:
-            place = len(work.pieces) - (0 if k == 1 else chunks)
-            place = max(place, 0)
-            later = [score(k, i) for i in range(chunks)]
             early = [piece for _, piece in early]
-            work.pieces[place:place] = early[:1] + later + early[1:]
+            work.pieces[:0] = early[:1]
+            work.pieces += early[1:] + [score(k, i) for i in range(chunks)]
     work.rest()
     estimate = scattered(finished(first, rounded[0], totals, places))
     alpha = jnp.stack(solved).reshape(panels, col_tiles, tile_size, width_out)

time: 186 us -> 180 us (0.968)
  Pallas kernels: 96.3 us -> 91.8 us
  waiting for transfers between devices: 35.2 us -> 32.7 us
  other arithmetic: 10.6 us -> 8.73 us
    pallas_call x10, Pallas kernels: 33.9 us -> 26.7 us  [panel_product(): pl.pallas_call(body, in_specs=[smem] * len(flips) + [stays if kept is Non...]
    pallas_call x16, Pallas kernels: 46.3 us -> 49.9 us  [scored(): pl.pallas_call(body, in_specs=in_specs, out_specs=out_specs, out_shape=ou...]
    ppermute x34, waiting for transfers between devices: 35.2 us -> 32.7 us  [swap(): return lax.ppermute(value, axis, [(i, i ^ mask) for i in range(size)])]
    unnamed x80 -> x82, local copies, waits for them, and re-layouts: 3.14 us -> 4.68 us
  transfers between devices with their start and end apart: 34 -> 34, of which waited for: 25 -> 20; matrix products, arithmetic and copies ran while one was open for 2% -> 1% of each run, Pallas kernels for 38% -> 42%
where the time goes in v3:
time: 180 us; the launch traced here: 177 us
  Pallas kernels  91.8 us (51%)
  starting transfers between devices  35.4 us (20%)
  waiting for transfers between devices  32.7 us (18%)
  other arithmetic  8.73 us (5%)
  local copies, waits for them, and re-layouts  6.06 us (3%)
  between operations  1.89 us (1%)
    pallas_call x16, Pallas kernels, scored(): pl.pallas_call(body, in_specs=in_specs, out_specs=out_specs, out_shape=ou...  49.9 us
    ppermute x34, starting transfers between devices, swap(): return lax.ppermute(value, axis, [(i, i ^ mask) for i in range(size)])  35.4 us
    ppermute x34, waiting for transfers between devices, swap(): return lax.ppermute(value, axis, [(i, i ^ mask) for i in range(size)])  32.7 us
    pallas_call x10, Pallas kernels, panel_product(): pl.pallas_call(body, in_specs=[smem] * len(flips) + [stays if kept is Non...  26.7 us
    pallas_call x1, Pallas kernels, gathered(): pl.pallas_call(body, in_specs=[smem, stays], out_specs=[stays] * (2 * chu...  12.3 us
    unnamed x82, local copies, waits for them, and re-layouts  4.68 us
  transfers between devices with their start and end apart: 34, of which 20 were waited for; matrix products, arithmetic and copies ran while one was open for 1% of the time, Pallas kernels for 42%

profile of v3, /device:TPU:0, one launch (start us, length us, event | category | flops | bytes accessed | tf_op | source)
XLA Modules:
  0.0 176.7 jit_solution(5307602186706716906)
XLA Ops:
  0.6 1.1 slice.109
  1.7 3.3 %inverse_3.1 = bf16[2,512,128]{2,1,0:T(8,128)(2,1)S(1)} custom-call(bf16[4,4,256,8,256]{4,3,2,1,0:T(8,128)(2,1)} %refs_1_.11, bf16[4,512,128]{2,1,0:T(8,128)(2,1)S(1)} %bitcast.69), custom_call_target="tpu_custom_call" | custom-call | flops 1073741824 | bytes 4194304 | tf_op jit(solution)/shard_map/inverse_3/pallas_call | solution.py:85
  5.1 3.0 %collective-permute-start.1 = (bf16[512,128]{1,0:T(8,128)(2,1)S(1)}, bf16[512,128]{1,0:T(8,128)(2,1)S(1)}, u32[]{:S(2)}, u32[]{:S(2)}) collective-permute-start(bf16[512,128]{1,0:T(8,128)(2,1)S(1)} %get-tuple-element.168), channel_id=1, source_target_pairs={{0,16},{8,24},{16,0},{24,8},{1,17},{9,25},{17,1},{25,9},{2,18},{10... | collective-permute-start | bytes 393224 | tf_op jit(solution)/shard_map/ppermute | solution.py:380
  8.1 1.5 collective-permute-start
  9.7 12.3 %gathered_0.1 = (bf16[1024,512]{1,0:T(8,128)(2,1)}, bf16[1024,512]{1,0:T(8,128)(2,1)}, bf16[1024,512]{1,0:T(8,128)(2,1)}, bf16[1024,512]{1,0:T(8,128)(2,1)}, f32...) custom-call(s32[4096]{0:T(1024)S(1)} %broadcast_multiply_fusion.located_ref, ...), custom_call_target="tpu_custom_call" | custom-call | bytes 52428800 | tf_op jit(solution)/shard_map/gathered_0/pallas_call | solution.py:175
  22.9 1.2 copy-done.5
  24.1 1.0 copy-done.8
  25.2 4.1 %scored_0_0.1 = (bf16[1024,1024]{1,0:T(8,128)(2,1)}, f32[4,1,256]{2,1,0:T(1,128)S(1)}, bf16[8,256,4,256]{3,2,1,0:T(4,128)(2,1)S(1)}) custom-call(s32[4]{0:T(128)S(1)} %get-tuple-element.94.slots_ref, bf16[1024,512]{1,0:T(8,128)(2,1)S(1)} %copy-done.5, f32[1024,128]{1,0:T(8,128)S(1)} %copy-done.8, bf16[16,256,512]{2,1,0:T(8,128)(2,1)S(1)} %copy-done, ...), custom_call_target="tpu_custom_call" | custom-call | flops 1610612736 | bytes 1048576 | tf_op jit(solution)/shard_map/scored_0_0/pallas_call | solution.py:275
  29.4 1.7 factor_2_3.1
  31.3 1.5 collective-permute-done.4
  32.9 2.1 %collective-permute-start.5 = (bf16[1,512,128]{2,1,0:T(8,128)(2,1)S(1)}, bf16[1,512,128]{2,1,0:T(8,128)(2,1)S(1)}, u32[]{:S(2)}, u32[]{:S(2)}) collective-permute-start(bf16[1,512,128]{2,1,0:T(8,128)(2,1)S(1)} %slice.142), channel_id=1, source_target_pairs={{0,2},{1,3},{2,0},{3,1},{4,6},{5,7},{6,4},{7,5},{8,10},{9,11},{10,... | collective-permute-start | bytes 393224 | tf_op jit(solution)/shard_map/ppermute | solution.py:380
  35.0 3.7 %factor_1_3.1.refs_3_ = f32[4,512,128]{2,1,0:T(8,128)S(1)} custom-call(s32[1]{0:T(128)} %bitcast.refs_0_, bf16[6,8,256,4,256]{4,3,2,1,0:T(4,128)(2,1)} %refs_3_.1, bf16[1,1024,128]{2,1,0:T(8,128)(2,1)S(1)} %bitcast.66), custom_call_target="tpu_custom_call" | custom-call | flops 1073741824 | bytes 4194304 | tf_op jit(solution)/shard_map/factor_1_3/pallas_call | solution.py:85
  38.8 3.8 %collective-permute-start.6 = (bf16[1,512,128]{2,1,0:T(8,128)(2,1)S(1)}, bf16[1,512,128]{2,1,0:T(8,128)(2,1)S(1)}, u32[]{:S(2)}, u32[]{:S(2)}) collective-permute-start(bf16[1,512,128]{2,1,0:T(8,128)(2,1)S(1)} %add_convert_fusion.13), channel_id=1, source_target_pairs={{0,6},{1,7},{2,4},{3,5},{4,2},{5,3},{6,0},{7,1},{8,14},{9,15},{10,... | collective-permute-start | bytes 393224 | tf_op jit(solution)/shard_map/ppermute | solution.py:380
  42.6 2.7 %scored_0_2.1.refs_2_ = bf16[1024,1024]{1,0:T(8,128)(2,1)} custom-call(s32[4]{0:T(128)S(1)} %get-tuple-element.94.slots_ref, bf16[1024,512]{1,0:T(8,128)(2,1)S(1)} %copy-done.3, f32[1024,128]{1,0:T(8,128)S(1)} %copy-done.12, bf16[16,256,512]{2,1,0:T(8,128)(2,1)S(1)} %copy-done.1, f32[4,1,256]{2,1,0:T(1,128)S(1)} %get-tuple-element.91.refs_0_), custom_call_target="tpu_custom_call" | custom-call | flops 1610612736 | bytes 1048576 | tf_op jit(solution)/shard_map/scored_0_2/pallas_call | solution.py:275
  45.4 2.7 %scored_0_1.1.refs_1_ = bf16[1024,1024]{1,0:T(8,128)(2,1)} custom-call(s32[4]{0:T(128)S(1)} %get-tuple-element.94.slots_ref, bf16[1024,512]{1,0:T(8,128)(2,1)S(1)} %copy-done.4, f32[1024,128]{1,0:T(8,128)S(1)} %copy-done.10, bf16[16,256,512]{2,1,0:T(8,128)(2,1)S(1)} %copy-done.1, f32[4,1,256]{2,1,0:T(1,128)S(1)} %get-tuple-element.91.refs_0_), custom_call_target="tpu_custom_call" | custom-call | flops 1610612736 | bytes 1048576 | tf_op jit(solution)/shard_map/scored_0_1/pallas_call | solution.py:275
  49.4 4.0 %scored_0_3.1 = (bf16[1024,1024]{1,0:T(8,128)(2,1)}, bf16[4,256,8,256]{3,2,1,0:T(8,128)(2,1)S(1)}) custom-call(s32[4]{0:T(128)S(1)} %get-tuple-element.94.slots_ref, bf16[1024,512]{1,0:T(8,128)(2,1)S(1)} %copy-done.7, f32[1024,128]{1,0:T(8,128)S(1)} %copy-done.11, bf16[16,256,512]{2,1,0:T(8,128)(2,1)S(1)} %copy-done.1, ...), custom_call_target="tpu_custom_call" | custom-call | flops 1610612736 | bytes 1048576 | tf_op jit(solution)/shard_map/scored_0_3/pallas_call | solution.py:275
  54.2 1.5 collective-permute-done.8
  55.8 1.7 inverse_2.1
  57.6 1.6 collective-permute-start.10
  59.2 1.5 collective-permute-start.9
  60.7 3.9 %factor_0_3.1.refs_3_ = f32[4,512,128]{2,1,0:T(8,128)S(1)} custom-call(s32[1]{0:T(128)} %bitcast.refs_0_, bf16[6,8,256,4,256]{4,3,2,1,0:T(4,128)(2,1)} %refs_3_.1, bf16[1,1024,128]{2,1,0:T(8,128)(2,1)S(1)} %bitcast.67), custom_call_target="tpu_custom_call" | custom-call | flops 1073741824 | bytes 4194304 | tf_op jit(solution)/shard_map/factor_0_3/pallas_call | solution.py:85
  64.7 1.4 collective-permute-start.12
  66.6 4.6 %scored_3_0.1 = (f32[1024,128]{1,0:T(8,128)S(1)}, f32[4,1,256]{2,1,0:T(1,128)S(1)}, bf16[8,256,4,256]{3,2,1,0:T(4,128)(2,1)S(1)}) custom-call(s32[4]{0:T(128)S(1)} %get-tuple-element.112.slots_ref, bf16[1024,512]{1,0:T(8,128)(2,1)S(1)} %copy-done.6, f32[1024,128]{1,0:T(8,128)S(1)} %copy-done.9, bf16[16,256,512]{2,1,0:T(8,128)(2,1)S(1)} %copy-done.1, ...), custom_call_target="tpu_custom_call" | custom-call | flops 1610612736 | bytes 1048576 | tf_op jit(solution)/shard_map/scored_3_0/pallas_call | solution.py:275
  71.3 1.8 %factor_1_2.1 = bf16[4,512,128]{2,1,0:T(8,128)(2,1)S(1)} custom-call(s32[1]{0:T(128)} %bitcast.refs_0_, bf16[8,256,4,256]{3,2,1,0:T(4,128)(2,1)S(1)} %get-tuple-element.102.refs_1_, bf16[1,1024,128]{2,1,0:T(8,128)(2,1)S(1)} %pad_maximum_fusion.10.refs_2_, f32[4,512,128]{2,1,0:T(8,128)S(1)} %factor_1_3.1.refs_3_), custom_call_target="tpu_custom_call" | custom-call | flops 1073741824 | bytes 4194304 | tf_op jit(solution)/shard_map/factor_1_2/pallas_call | solution.py:85
  73.2 1.5 collective-permute-done.13
  74.8 1.1 collective-permute-start.14
  76.0 3.6 %factor_0_2.1.refs_3_ = f32[4,512,128]{2,1,0:T(8,128)S(1)} custom-call(s32[1]{0:T(128)} %bitcast.refs_0_, bf16[6,8,256,4,256]{4,3,2,1,0:T(4,128)(2,1)} %refs_3_.1, bf16[1,1024,128]{2,1,0:T(8,128)(2,1)S(1)} %bitcast.68, f32[4,512,128]{2,1,0:T(8,128)S(1)} %factor_0_3.1.refs_3_), custom_call_target="tpu_custom_call" | custom-call | flops 1073741824 | bytes 4194304 | tf_op jit(solution)/shard_map/factor_0_2/pallas_call | solution.py:85
  80.5 2.0 %collective-permute-start.15 = (bf16[1,512,128]{2,1,0:T(8,128)(2,1)S(1)}, bf16[1,512,128]{2,1,0:T(8,128)(2,1)S(1)}, u32[]{:S(2)}, u32[]{:S(2)}) collective-permute-start(bf16[1,512,128]{2,1,0:T(8,128)(2,1)S(1)} %add_convert_fusion.10), channel_id=1, source_target_pairs={{0,6},{1,7},{2,4},{3,5},{4,2},{5,3},{6,0},{7,1},{8,14},{9,15},{10,... | collective-permute-start | bytes 393224 | tf_op jit(solution)/shard_map/ppermute | solution.py:380
  82.5 2.5 %scored_3_2.1.refs_2_ = f32[1024,128]{1,0:T(8,128)S(1)} custom-call(s32[4]{0:T(128)S(1)} %get-tuple-element.112.slots_ref, bf16[1024,512]{1,0:T(8,128)(2,1)S(1)} %copy-done.3, f32[1024,128]{1,0:T(8,128)S(1)} %copy-done.12, bf16[16,256,512]{2,1,0:T(8,128)(2,1)S(1)} %copy-done.1, f32[4,1,256]{2,1,0:T(1,128)S(1)} %get-tuple-element.109.refs_0_, ...), custom_call_target="tpu_custom_call" | custom-call | flops 1610612736 | bytes 1048576 | tf_op jit(solution)/shard_map/scored_3_2/pallas_call | solution.py:275
  85.0 2.9 %scored_3_1.1.refs_2_ = f32[1024,128]{1,0:T(8,128)S(1)} custom-call(s32[4]{0:T(128)S(1)} %get-tuple-element.112.slots_ref, bf16[1024,512]{1,0:T(8,128)(2,1)S(1)} %copy-done.4, f32[1024,128]{1,0:T(8,128)S(1)} %copy-done.10, bf16[16,256,512]{2,1,0:T(8,128)(2,1)S(1)} %copy-done.1, f32[4,1,256]{2,1,0:T(1,128)S(1)} %get-tuple-element.109.refs_0_, ...), custom_call_target="tpu_custom_call" | custom-call | flops 1610612736 | bytes 1048576 | tf_op jit(solution)/shard_map/scored_3_1/pallas_call | solution.py:275
  88.9 1.2 collective-permute-start.16
  90.1 4.3 %scored_3_3.1 = (f32[1024,128]{1,0:T(8,128)S(1)}, bf16[4,256,8,256]{3,2,1,0:T(8,128)(2,1)S(1)}) custom-call(s32[4]{0:T(128)S(1)} %get-tuple-element.112.slots_ref, bf16[1024,512]{1,0:T(8,128)(2,1)S(1)} %copy-done.7, f32[1024,128]{1,0:T(8,128)S(1)} %copy-done.11, bf16[16,256,512]{2,1,0:T(8,128)(2,1)S(1)} %copy-done.1, ...), custom_call_target="tpu_custom_call" | custom-call | flops 1610612736 | bytes 1048576 | tf_op jit(solution)/shard_map/scored_3_3/pallas_call | solution.py:275
  94.5 1.5 collective-permute-done.17
  96.1 1.7 inverse_1.1
  97.9 1.6 collective-permute-start.19
  100.2 2.5 %scored_2_0.1 = (f32[1024,128]{1,0:T(8,128)S(1)}, f32[4,1,256]{2,1,0:T(1,128)S(1)}) custom-call(s32[4]{0:T(128)S(1)} %get-tuple-element.128.slots_ref, bf16[1024,512]{1,0:T(8,128)(2,1)S(1)} %copy-done.6, f32[1024,128]{1,0:T(8,128)S(1)} %copy-done.9, bf16[16,256,512]{2,1,0:T(8,128)(2,1)S(1)} %copy-done.1, bf16[1024,128]{1,0:T(8,128)(2,1)S(1)} %fusion.5.refs_0_.refs_1_, ...), custom_call_target="tpu_custom_call" | custom-call | flops 1610612736 | bytes 1048576 | tf_op jit(solution)/shard_map/scored_2_0/pallas_call | solution.py:275
  103.5 1.2 collective-permute-done.18
  106.1 4.4 %scored_2_1.1 = (f32[1024,128]{1,0:T(8,128)S(1)}, bf16[8,256,4,256]{3,2,1,0:T(4,128)(2,1)S(1)}) custom-call(s32[4]{0:T(128)S(1)} %get-tuple-element.128.slots_ref, bf16[1024,512]{1,0:T(8,128)(2,1)S(1)} %copy-done.4, f32[1024,128]{1,0:T(8,128)S(1)} %copy-done.10, bf16[16,256,512]{2,1,0:T(8,128)(2,1)S(1)} %copy-done.1, ...), custom_call_target="tpu_custom_call" | custom-call | flops 1610612736 | bytes 1048576 | tf_op jit(solution)/shard_map/scored_2_1/pallas_call | solution.py:275
  110.7 1.8 %factor_0_1.1 = bf16[4,512,128]{2,1,0:T(8,128)(2,1)S(1)} custom-call(s32[1]{0:T(128)} %bitcast.refs_0_, bf16[8,256,4,256]{3,2,1,0:T(4,128)(2,1)S(1)} %get-tuple-element.122.refs_1_, bf16[1,1024,128]{2,1,0:T(8,128)(2,1)S(1)} %pad_maximum_fusion.12.refs_2_, f32[4,512,128]{2,1,0:T(8,128)S(1)} %factor_0_2.1.refs_3_), custom_call_target="tpu_custom_call" | custom-call | flops 1073741824 | bytes 4194304 | tf_op jit(solution)/shard_map/factor_0_1/pallas_call | solution.py:85
  112.7 1.5 collective-permute-done.22
  115.1 2.5 %scored_2_2.1.refs_2_ = f32[1024,128]{1,0:T(8,128)S(1)} custom-call(s32[4]{0:T(128)S(1)} %get-tuple-element.128.slots_ref, bf16[1024,512]{1,0:T(8,128)(2,1)S(1)} %copy-done.3, f32[1024,128]{1,0:T(8,128)S(1)} %copy-done.12, bf16[16,256,512]{2,1,0:T(8,128)(2,1)S(1)} %copy-done.1, f32[4,1,256]{2,1,0:T(1,128)S(1)} %get-tuple-element.121.refs_0_, ...), custom_call_target="tpu_custom_call" | custom-call | flops 1610612736 | bytes 1048576 | tf_op jit(solution)/shard_map/scored_2_2/pallas_call | solution.py:275
  117.7 2.1 %collective-permute-done.23 = bf16[1,512,128]{2,1,0:T(8,128)(2,1)S(1)} collective-permute-done((bf16[1,512,128]{2,1,0:T(8,128)(2,1)S(1)}, bf16[1,512,128]{2,1,0:T(8,128)(2,1)S(1)}, u32[]{:S(2)}, u32[]{:S(2)}) %collective-permute-start.23) | collective-permute-done | bytes 131104 | tf_op jit(solution)/shard_map/ppermute | solution.py:380
  119.9 2.1 %collective-permute-start.24 = (bf16[1,512,128]{2,1,0:T(8,128)(2,1)S(1)}, bf16[1,512,128]{2,1,0:T(8,128)(2,1)S(1)}, u32[]{:S(2)}, u32[]{:S(2)}) collective-permute-start(bf16[1,512,128]{2,1,0:T(8,128)(2,1)S(1)} %add_convert_fusion.7), channel_id=1, source_target_pairs={{0,6},{1,7},{2,4},{3,5},{4,2},{5,3},{6,0},{7,1},{8,14},{9,15},{10,... | collective-permute-start | bytes 393224 | tf_op jit(solution)/shard_map/ppermute | solution.py:380
  121.9 2.5 %scored_2_3.1.refs_2_ = f32[1024,128]{1,0:T(8,128)S(1)} custom-call(s32[4]{0:T(128)S(1)} %get-tuple-element.128.slots_ref, bf16[1024,512]{1,0:T(8,128)(2,1)S(1)} %copy-done.7, f32[1024,128]{1,0:T(8,128)S(1)} %copy-done.11, bf16[16,256,512]{2,1,0:T(8,128)(2,1)S(1)} %copy-done.1, f32[4,1,256]{2,1,0:T(1,128)S(1)} %get-tuple-element.121.refs_0_, ...), custom_call_target="tpu_custom_call" | custom-call | flops 1610612736 | bytes 1048576 | tf_op jit(solution)/shard_map/scored_2_3/pallas_call | solution.py:275
  125.2 2.6 %scored_1_0.1 = (f32[1024,128]{1,0:T(8,128)S(1)}, f32[4,1,256]{2,1,0:T(1,128)S(1)}) custom-call(s32[4]{0:T(128)S(1)} %get-tuple-element.139.slots_ref, bf16[1024,512]{1,0:T(8,128)(2,1)S(1)} %copy-done.6, f32[1024,128]{1,0:T(8,128)S(1)} %copy-done.9, bf16[16,256,512]{2,1,0:T(8,128)(2,1)S(1)} %copy-done.1, bf16[1024,128]{1,0:T(8,128)(2,1)S(1)} %fusion.4.refs_0_.refs_1_, ...), custom_call_target="tpu_custom_call" | custom-call | flops 1610612736 | bytes 1048576 | tf_op jit(solution)/shard_map/scored_1_0/pallas_call | solution.py:275
  127.8 1.1 fusion.2
  129.4 2.5 %scored_1_1.1.refs_6_ = f32[1024,128]{1,0:T(8,128)S(1)} custom-call(s32[4]{0:T(128)S(1)} %get-tuple-element.139.slots_ref, bf16[1024,512]{1,0:T(8,128)(2,1)S(1)} %copy-done.4, f32[1024,128]{1,0:T(8,128)S(1)} %copy-done.10, bf16[16,256,512]{2,1,0:T(8,128)(2,1)S(1)} %copy-done.1, f32[4,1,256]{2,1,0:T(1,128)S(1)} %get-tuple-element.134.refs_0_, ...), custom_call_target="tpu_custom_call" | custom-call | flops 1610612736 | bytes 1048576 | tf_op jit(solution)/shard_map/scored_1_1/pallas_call | solution.py:275
  132.8 1.2 collective-permute-done.25
  135.4 1.9 %collective-permute-done.26 = bf16[2,512,128]{2,1,0:T(8,128)(2,1)} collective-permute-done((bf16[2,512,128]{2,1,0:T(8,128)(2,1)}, bf16[2,512,128]{2,1,0:T(8,128)(2,1)}, u32[]{:S(2)}, u32[]{:S(2)}) %collective-permute-start.26) | collective-permute-done | bytes 262176 | tf_op jit(solution)/shard_map/ppermute | solution.py:380
  137.2 1.0 pad_maximum_fusion.6.refs_2_
  138.3 3.4 %inverse_0.1 = bf16[2,512,128]{2,1,0:T(8,128)(2,1)S(1)} custom-call(s32[1]{0:T(128)} %bitcast.refs_0_, bf16[4,4,256,8,256]{4,3,2,1,0:T(8,128)(2,1)} %refs_1_.11, bf16[4,512,128]{2,1,0:T(8,128)(2,1)S(1)} %pad_maximum_fusion.6.refs_2_), custom_call_target="tpu_custom_call" | custom-call | flops 1073741824 | bytes 4194304 | tf_op jit(solution)/shard_map/inverse_0/pallas_call | solution.py:85
  141.8 1.5 collective-permute-start.28
  143.3 1.3 collective-permute-start.27
  144.6 2.6 %scored_1_2.1.refs_7_ = f32[1024,128]{1,0:T(8,128)S(1)} custom-call(s32[4]{0:T(128)S(1)} %get-tuple-element.139.slots_ref, bf16[1024,512]{1,0:T(8,128)(2,1)S(1)} %copy-done.3, f32[1024,128]{1,0:T(8,128)S(1)} %copy-done.12, bf16[16,256,512]{2,1,0:T(8,128)(2,1)S(1)} %copy-done.2, f32[4,1,256]{2,1,0:T(1,128)S(1)} %get-tuple-element.134.refs_0_, ...), custom_call_target="tpu_custom_call" | custom-call | flops 1610612736 | bytes 1048576 | tf_op jit(solution)/shard_map/scored_1_2/pallas_call | solution.py:275
  147.4 1.2 collective-permute-done.27
  148.6 1.4 collective-permute-start.30
  150.6 2.6 %scored_1_3.1.refs_8_ = f32[1024,128]{1,0:T(8,128)S(1)} custom-call(s32[4]{0:T(128)S(1)} %get-tuple-element.139.slots_ref, bf16[1024,512]{1,0:T(8,128)(2,1)S(1)} %copy-done.7, f32[1024,128]{1,0:T(8,128)S(1)} %copy-done.11, bf16[16,256,512]{2,1,0:T(8,128)(2,1)S(1)} %copy-done.2, f32[4,1,256]{2,1,0:T(1,128)S(1)} %get-tuple-element.134.refs_0_, ...), custom_call_target="tpu_custom_call" | custom-call | flops 1610612736 | bytes 1048576 | tf_op jit(solution)/shard_map/scored_1_3/pallas_call | solution.py:275
  153.7 1.3 collective-permute-done.29
  155.2 2.9 %finished.1 = bf16[8,512,128]{2,1,0:T(8,128)(2,1)S(1)} custom-call(s32[8]{0:T(128)S(1)} %broadcast_xor_fusion.places_ref, bf16[1024,1024]{1,0:T(8,128)(2,1)S(1)} %copy-done.21, bf16[1024,1024]{1,0:T(8,128)(2,1)S(1)} %copy-done.14, bf16[1024,1024]{1,0:T(8,128)(2,1)S(1)} %copy-done.13, bf16[1024,1024]{1,0:T(8,128)(2,1)S(1)} %copy-done.22, ...), custom_call_target="tpu_custom_call" | custom-call | flops 2147483648 | bytes 8388608 | tf_op jit(solution)/shard_map/finished/pallas_call | solution.py:312
  158.3 1.8 %collective-permute-done.31 = bf16[4,512,128]{2,1,0:T(8,128)(2,1)S(1)} collective-permute-done((bf16[4,512,128]{2,1,0:T(8,128)(2,1)S(1)}, bf16[4,512,128]{2,1,0:T(8,128)(2,1)S(1)}, u32[]{:S(2)}, u32[]{:S(2)}) %collective-permute-start.31) | collective-permute-done | bytes 524320 | tf_op jit(solution)/shard_map/ppermute | solution.py:380
  161.0 7.8 %collective-permute-done.32 = bf16[2,512,128]{2,1,0:T(8,128)(2,1)S(1)} collective-permute-done((bf16[2,512,128]{2,1,0:T(8,128)(2,1)S(1)}, bf16[2,512,128]{2,1,0:T(8,128)(2,1)S(1)}, u32[]{:S(2)}, u32[]{:S(2)}) %collective-permute-start.32) | collective-permute-done | bytes 262176 | tf_op jit(solution)/shard_map/ppermute | solution.py:380
  168.8 2.0 %collective-permute-start.33 = (bf16[1,512,128]{2,1,0:T(8,128)(2,1)S(1)}, bf16[1,512,128]{2,1,0:T(8,128)(2,1)S(1)}, u32[]{:S(2)}, u32[]{:S(2)}) collective-permute-start(bf16[1,512,128]{2,1,0:T(8,128)(2,1)S(1)} %slice.162), channel_id=1, source_target_pairs={{0,6},{1,7},{2,4},{3,5},{4,2},{5,3},{6,0},{7,1},{8,14},{9,15},{10,... | collective-permute-start | bytes 393224 | tf_op jit(solution)/shard_map/ppermute | solution.py:380
  170.9 1.5 pad_maximum_fusion
  172.4 3.4 %collective-permute-done.33 = bf16[1,512,128]{2,1,0:T(8,128)(2,1)S(1)} collective-permute-done((bf16[1,512,128]{2,1,0:T(8,128)(2,1)S(1)}, bf16[1,512,128]{2,1,0:T(8,128)(2,1)S(1)}, u32[]{:S(2)}, u32[]{:S(2)}) %collective-permute-start.33) | collective-permute-done | bytes 131104 | tf_op jit(solution)/shard_map/ppermute | solution.py:380
  (174 shorter events, 17.3 us)
Async XLA Ops:
  1.7 7.9 %copy-start.39 = (s32[16,1]{0,1:T(1,128)S(1)}, s32[16,1]{0,1:T(1,128)}, u32[]{:S(2)}) copy-start(s32[16,1]{0,1:T(1,128)} %param.12) | copy-start | bytes 196
  1.7 8.0 %copy-start.38 = (s32[4096]{0:T(1024)S(1)}, s32[4096]{0:T(1024)}, u32[]{:S(2)}) copy-start(s32[4096]{0:T(1024)} %param.14) | copy-start | bytes 49156
  5.1 17.1 %collective-permute-start.1 = (bf16[512,128]{1,0:T(8,128)(2,1)S(1)}, bf16[512,128]{1,0:T(8,128)(2,1)S(1)}, u32[]{:S(2)}, u32[]{:S(2)}) collective-permute-start(bf16[512,128]{1,0:T(8,128)(2,1)S(1)} %get-tuple-element.168), channel_id=1, source_target_pairs={{0,16},{8,24},{16,0},{24,8},{1,17},{9,25},{17,1},{25,9},{2,18},{10... | collective-permute-start | bytes 393224 | tf_op jit(solution)/shard_map/ppermute | solution.py:380
  8.1 14.1 %collective-permute-start = (bf16[512,128]{1,0:T(8,128)(2,1)S(1)}, bf16[512,128]{1,0:T(8,128)(2,1)S(1)}, u32[]{:S(2)}, u32[]{:S(2)}) collective-permute-start(bf16[512,128]{1,0:T(8,128)(2,1)S(1)} %get-tuple-element.169), channel_id=1, source_target_pairs={{0,8},{8,0},{16,24},{24,16},{1,9},{9,1},{17,25},{25,17},{2,10},{10... | collective-permute-start | bytes 393224 | tf_op jit(solution)/shard_map/ppermute | solution.py:380
  9.7 13.2 %copy-start = (bf16[16,256,512]{2,1,0:T(8,128)(2,1)S(1)}, bf16[16,256,512]{2,1,0:T(8,128)(2,1)}, u32[]{:S(2)}) copy-start(bf16[16,256,512]{2,1,0:T(8,128)(2,1)} %center_ref.31) | copy-start | bytes 12582916
  22.2 7.1 %collective-permute-start.3 = (bf16[512,128]{1,0:T(8,128)(2,1)S(1)}, bf16[512,128]{1,0:T(8,128)(2,1)S(1)}, u32[]{:S(2)}, u32[]{:S(2)}) collective-permute-start(bf16[512,128]{1,0:T(8,128)(2,1)S(1)} %get-tuple-element.166), channel_id=1, source_target_pairs={{0,8},{8,0},{16,24},{24,16},{1,9},{9,1},{17,25},{25,17},{2,10},{10... | collective-permute-start | bytes 393224 | tf_op jit(solution)/shard_map/ppermute | solution.py:380
  22.8 6.5 %collective-permute-start.2 = (bf16[512,128]{1,0:T(8,128)(2,1)S(1)}, bf16[512,128]{1,0:T(8,128)(2,1)S(1)}, u32[]{:S(2)}, u32[]{:S(2)}) collective-permute-start(bf16[512,128]{1,0:T(8,128)(2,1)S(1)} %get-tuple-element.167), channel_id=1, source_target_pairs={{0,16},{8,24},{16,0},{24,8},{1,17},{9,25},{17,1},{25,9},{2,18},{10... | collective-permute-start | bytes 393224 | tf_op jit(solution)/shard_map/ppermute | solution.py:380
  29.4 5.6 %copy-start.25 = (f32[512,128]{1,0:T(8,128)}, f32[512,128]{1,0:T(8,128)S(1)}, u32[]{:S(2)}) copy-start(f32[512,128]{1,0:T(8,128)S(1)} %get-tuple-element.165) | copy-start | bytes 786436
  29.4 5.5 %copy-start.27 = (f32[512,128]{1,0:T(8,128)}, f32[512,128]{1,0:T(8,128)S(1)}, u32[]{:S(2)}) copy-start(f32[512,128]{1,0:T(8,128)S(1)} %get-tuple-element.174) | copy-start | bytes 786436
  31.2 1.6 collective-permute-start.4
  32.9 5.9 %collective-permute-start.5 = (bf16[1,512,128]{2,1,0:T(8,128)(2,1)S(1)}, bf16[1,512,128]{2,1,0:T(8,128)(2,1)S(1)}, u32[]{:S(2)}, u32[]{:S(2)}) collective-permute-start(bf16[1,512,128]{2,1,0:T(8,128)(2,1)S(1)} %slice.142), channel_id=1, source_target_pairs={{0,2},{1,3},{2,0},{3,1},{4,6},{5,7},{6,4},{7,5},{8,10},{9,11},{10,... | collective-permute-start | bytes 393224 | tf_op jit(solution)/shard_map/ppermute | solution.py:380
  35.0 7.6 %copy-start.1 = (bf16[16,256,512]{2,1,0:T(8,128)(2,1)S(1)}, bf16[16,256,512]{2,1,0:T(8,128)(2,1)}, u32[]{:S(2)}) copy-start(bf16[16,256,512]{2,1,0:T(8,128)(2,1)} %center_ref.31) | copy-start | bytes 12582916
  35.0 7.6 %copy-start.3 = (bf16[1024,512]{1,0:T(8,128)(2,1)S(1)}, bf16[1024,512]{1,0:T(8,128)(2,1)}, u32[]{:S(2)}) copy-start(bf16[1024,512]{1,0:T(8,128)(2,1)} %get-tuple-element.75.span_ref) | copy-start | bytes 3145732
  35.0 7.6 %copy-start.12 = (f32[1024,128]{1,0:T(8,128)S(1)}, f32[1024,128]{1,0:T(8,128)}, u32[]{:S(2)}) copy-start(f32[1024,128]{1,0:T(8,128)} %get-tuple-element.79.norm_ref) | copy-start | bytes 1572868
  38.8 9.3 %collective-permute-start.6 = (bf16[1,512,128]{2,1,0:T(8,128)(2,1)S(1)}, bf16[1,512,128]{2,1,0:T(8,128)(2,1)S(1)}, u32[]{:S(2)}, u32[]{:S(2)}) collective-permute-start(bf16[1,512,128]{2,1,0:T(8,128)(2,1)S(1)} %add_convert_fusion.13), channel_id=1, source_target_pairs={{0,6},{1,7},{2,4},{3,5},{4,2},{5,3},{6,0},{7,1},{8,14},{9,15},{10,... | collective-permute-start | bytes 393224 | tf_op jit(solution)/shard_map/ppermute | solution.py:380
  42.6 2.7 %copy-start.4 = (bf16[1024,512]{1,0:T(8,128)(2,1)S(1)}, bf16[1024,512]{1,0:T(8,128)(2,1)}, u32[]{:S(2)}) copy-start(bf16[1024,512]{1,0:T(8,128)(2,1)} %get-tuple-element.74.span_ref) | copy-start | bytes 3145732
  42.6 2.7 %copy-start.10 = (f32[1024,128]{1,0:T(8,128)S(1)}, f32[1024,128]{1,0:T(8,128)}, u32[]{:S(2)}) copy-start(f32[1024,128]{1,0:T(8,128)} %get-tuple-element.78.norm_ref) | copy-start | bytes 1572868
  45.4 4.0 %copy-start.7 = (bf16[1024,512]{1,0:T(8,128)(2,1)S(1)}, bf16[1024,512]{1,0:T(8,128)(2,1)}, u32[]{:S(2)}) copy-start(bf16[1024,512]{1,0:T(8,128)(2,1)} %get-tuple-element.76.span_ref) | copy-start | bytes 3145732
  45.4 4.0 %copy-start.11 = (f32[1024,128]{1,0:T(8,128)S(1)}, f32[1024,128]{1,0:T(8,128)}, u32[]{:S(2)}) copy-start(f32[1024,128]{1,0:T(8,128)} %get-tuple-element.80.norm_ref) | copy-start | bytes 1572868
  49.1 5.0 %collective-permute-start.7 = (bf16[1,512,128]{2,1,0:T(8,128)(2,1)S(1)}, bf16[1,512,128]{2,1,0:T(8,128)(2,1)S(1)}, u32[]{:S(2)}, u32[]{:S(2)}) collective-permute-start(bf16[1,512,128]{2,1,0:T(8,128)(2,1)S(1)} %fusion), channel_id=1, source_target_pairs={{0,2},{1,3},{2,0},{3,1},{4,6},{5,7},{6,4},{7,5},{8,10},{9,11},{10,... | collective-permute-start | bytes 393224 | tf_op jit(solution)/shard_map/ppermute | solution.py:380
  54.1 1.6 collective-permute-start.8
  57.6 7.0 %collective-permute-start.10 = (bf16[512,128]{1,0:T(8,128)(2,1)S(1)}, bf16[512,128]{1,0:T(8,128)(2,1)S(1)}, u32[]{:S(2)}, u32[]{:S(2)}) collective-permute-start(bf16[512,128]{1,0:T(8,128)(2,1)S(1)} %get-tuple-element.160), channel_id=1, source_target_pairs={{0,16},{8,24},{16,0},{24,8},{1,17},{9,25},{17,1},{25,9},{2,18},{10... | collective-permute-start | bytes 393224 | tf_op jit(solution)/shard_map/ppermute | solution.py:380
  59.2 5.4 %collective-permute-start.9 = (bf16[512,128]{1,0:T(8,128)(2,1)S(1)}, bf16[512,128]{1,0:T(8,128)(2,1)S(1)}, u32[]{:S(2)}, u32[]{:S(2)}) collective-permute-start(bf16[512,128]{1,0:T(8,128)(2,1)S(1)} %get-tuple-element.161), channel_id=1, source_target_pairs={{0,8},{8,0},{16,24},{24,16},{1,9},{9,1},{17,25},{25,17},{2,10},{10... | collective-permute-start | bytes 393224 | tf_op jit(solution)/shard_map/ppermute | solution.py:380
  60.6 5.9 %copy-start.6 = (bf16[1024,512]{1,0:T(8,128)(2,1)S(1)}, bf16[1024,512]{1,0:T(8,128)(2,1)}, u32[]{:S(2)}) copy-start(bf16[1024,512]{1,0:T(8,128)(2,1)} %get-tuple-element.73.span_ref) | copy-start | bytes 3145732
  60.6 5.9 %copy-start.9 = (f32[1024,128]{1,0:T(8,128)S(1)}, f32[1024,128]{1,0:T(8,128)}, u32[]{:S(2)}) copy-start(f32[1024,128]{1,0:T(8,128)} %get-tuple-element.77.norm_ref) | copy-start | bytes 1572868
  64.7 6.5 %collective-permute-start.12 = (bf16[512,128]{1,0:T(8,128)(2,1)S(1)}, bf16[512,128]{1,0:T(8,128)(2,1)S(1)}, u32[]{:S(2)}, u32[]{:S(2)}) collective-permute-start(bf16[512,128]{1,0:T(8,128)(2,1)S(1)} %get-tuple-element.158), channel_id=1, source_target_pairs={{0,8},{8,0},{16,24},{24,16},{1,9},{9,1},{17,25},{25,17},{2,10},{10... | collective-permute-start | bytes 393224 | tf_op jit(solution)/shard_map/ppermute | solution.py:380
  66.0 5.1 %collective-permute-start.11 = (bf16[512,128]{1,0:T(8,128)(2,1)S(1)}, bf16[512,128]{1,0:T(8,128)(2,1)S(1)}, u32[]{:S(2)}, u32[]{:S(2)}) collective-permute-start(bf16[512,128]{1,0:T(8,128)(2,1)S(1)} %get-tuple-element.159), channel_id=1, source_target_pairs={{0,16},{8,24},{16,0},{24,8},{1,17},{9,25},{17,1},{25,9},{2,18},{10... | collective-permute-start | bytes 393224 | tf_op jit(solution)/shard_map/ppermute | solution.py:380
  71.2 4.7 %copy-start.29 = (f32[512,128]{1,0:T(8,128)}, f32[512,128]{1,0:T(8,128)S(1)}, u32[]{:S(2)}) copy-start(f32[512,128]{1,0:T(8,128)S(1)} %get-tuple-element.155) | copy-start | bytes 786436
  71.3 4.7 %copy-start.31 = (f32[512,128]{1,0:T(8,128)}, f32[512,128]{1,0:T(8,128)S(1)}, u32[]{:S(2)}) copy-start(f32[512,128]{1,0:T(8,128)S(1)} %get-tuple-element.157) | copy-start | bytes 786436
  73.1 1.6 collective-permute-start.13
  74.8 5.6 %collective-permute-start.14 = (bf16[1,512,128]{2,1,0:T(8,128)(2,1)S(1)}, bf16[1,512,128]{2,1,0:T(8,128)(2,1)S(1)}, u32[]{:S(2)}, u32[]{:S(2)}) collective-permute-start(bf16[1,512,128]{2,1,0:T(8,128)(2,1)S(1)} %slice.148), channel_id=1, source_target_pairs={{0,2},{1,3},{2,0},{3,1},{4,6},{5,7},{6,4},{7,5},{8,10},{9,11},{10,... | collective-permute-start | bytes 393224 | tf_op jit(solution)/shard_map/ppermute | solution.py:380
  80.5 7.4 %collective-permute-start.15 = (bf16[1,512,128]{2,1,0:T(8,128)(2,1)S(1)}, bf16[1,512,128]{2,1,0:T(8,128)(2,1)S(1)}, u32[]{:S(2)}, u32[]{:S(2)}) collective-permute-start(bf16[1,512,128]{2,1,0:T(8,128)(2,1)S(1)} %add_convert_fusion.10), channel_id=1, source_target_pairs={{0,6},{1,7},{2,4},{3,5},{4,2},{5,3},{6,0},{7,1},{8,14},{9,15},{10,... | collective-permute-start | bytes 393224 | tf_op jit(solution)/shard_map/ppermute | solution.py:380
  88.9 5.5 %collective-permute-start.16 = (bf16[1,512,128]{2,1,0:T(8,128)(2,1)S(1)}, bf16[1,512,128]{2,1,0:T(8,128)(2,1)S(1)}, u32[]{:S(2)}, u32[]{:S(2)}) collective-permute-start(bf16[1,512,128]{2,1,0:T(8,128)(2,1)S(1)} %fusion.1), channel_id=1, source_target_pairs={{0,2},{1,3},{2,0},{3,1},{4,6},{5,7},{6,4},{7,5},{8,10},{9,11},{10,... | collective-permute-start | bytes 393224 | tf_op jit(solution)/shard_map/ppermute | solution.py:380
  94.5 1.6 collective-permute-start.17
  97.9 5.6 %collective-permute-start.19 = (bf16[512,128]{1,0:T(8,128)(2,1)S(1)}, bf16[512,128]{1,0:T(8,128)(2,1)S(1)}, u32[]{:S(2)}, u32[]{:S(2)}) collective-permute-start(bf16[512,128]{1,0:T(8,128)(2,1)S(1)} %get-tuple-element.152), channel_id=1, source_target_pairs={{0,16},{8,24},{16,0},{24,8},{1,17},{9,25},{17,1},{25,9},{2,18},{10... | collective-permute-start | bytes 393224 | tf_op jit(solution)/shard_map/ppermute | solution.py:380
  99.5 5.3 %collective-permute-start.18 = (bf16[512,128]{1,0:T(8,128)(2,1)S(1)}, bf16[512,128]{1,0:T(8,128)(2,1)S(1)}, u32[]{:S(2)}, u32[]{:S(2)}) collective-permute-start(bf16[512,128]{1,0:T(8,128)(2,1)S(1)} %get-tuple-element.153), channel_id=1, source_target_pairs={{0,8},{8,0},{16,24},{24,16},{1,9},{9,1},{17,25},{25,17},{2,10},{10... | collective-permute-start | bytes 393224 | tf_op jit(solution)/shard_map/ppermute | solution.py:380
  104.8 5.7 %collective-permute-start.21 = (bf16[512,128]{1,0:T(8,128)(2,1)S(1)}, bf16[512,128]{1,0:T(8,128)(2,1)S(1)}, u32[]{:S(2)}, u32[]{:S(2)}) collective-permute-start(bf16[512,128]{1,0:T(8,128)(2,1)S(1)} %get-tuple-element.150), channel_id=1, source_target_pairs={{0,8},{8,0},{16,24},{24,16},{1,9},{9,1},{17,25},{25,17},{2,10},{10... | collective-permute-start | bytes 393224 | tf_op jit(solution)/shard_map/ppermute | solution.py:380
  105.6 5.0 %collective-permute-start.20 = (bf16[512,128]{1,0:T(8,128)(2,1)S(1)}, bf16[512,128]{1,0:T(8,128)(2,1)S(1)}, u32[]{:S(2)}, u32[]{:S(2)}) collective-permute-start(bf16[512,128]{1,0:T(8,128)(2,1)S(1)} %get-tuple-element.151), channel_id=1, source_target_pairs={{0,16},{8,24},{16,0},{24,8},{1,17},{9,25},{17,1},{25,9},{2,18},{10... | collective-permute-start | bytes 393224 | tf_op jit(solution)/shard_map/ppermute | solution.py:380
  112.5 1.6 collective-permute-start.22
  114.2 5.6 %collective-permute-start.23 = (bf16[1,512,128]{2,1,0:T(8,128)(2,1)S(1)}, bf16[1,512,128]{2,1,0:T(8,128)(2,1)S(1)}, u32[]{:S(2)}, u32[]{:S(2)}) collective-permute-start(bf16[1,512,128]{2,1,0:T(8,128)(2,1)S(1)} %slice.154), channel_id=1, source_target_pairs={{0,2},{1,3},{2,0},{3,1},{4,6},{5,7},{6,4},{7,5},{8,10},{9,11},{10,... | collective-permute-start | bytes 393224 | tf_op jit(solution)/shard_map/ppermute | solution.py:380
  117.7 6.8 %copy-start.19 = (f32[1024,128]{1,0:T(8,128)}, f32[1024,128]{1,0:T(8,128)S(1)}, u32[]{:S(2)}) copy-start(f32[1024,128]{1,0:T(8,128)S(1)} %scored_2_2.1.refs_2_) | copy-start | bytes 1572868
  119.9 8.0 %collective-permute-start.24 = (bf16[1,512,128]{2,1,0:T(8,128)(2,1)S(1)}, bf16[1,512,128]{2,1,0:T(8,128)(2,1)S(1)}, u32[]{:S(2)}, u32[]{:S(2)}) collective-permute-start(bf16[1,512,128]{2,1,0:T(8,128)(2,1)S(1)} %add_convert_fusion.7), channel_id=1, source_target_pairs={{0,6},{1,7},{2,4},{3,5},{4,2},{5,3},{6,0},{7,1},{8,14},{9,15},{10,... | collective-permute-start | bytes 393224 | tf_op jit(solution)/shard_map/ppermute | solution.py:380
  129.0 5.0 %collective-permute-start.25 = (bf16[1,512,128]{2,1,0:T(8,128)(2,1)S(1)}, bf16[1,512,128]{2,1,0:T(8,128)(2,1)S(1)}, u32[]{:S(2)}, u32[]{:S(2)}) collective-permute-start(bf16[1,512,128]{2,1,0:T(8,128)(2,1)S(1)} %fusion.2), channel_id=1, source_target_pairs={{0,2},{1,3},{2,0},{3,1},{4,6},{5,7},{6,4},{7,5},{8,10},{9,11},{10,... | collective-permute-start | bytes 393224 | tf_op jit(solution)/shard_map/ppermute | solution.py:380
  129.4 5.9 %copy-start.40 = (s32[8]{0:T(128)S(1)}, s32[8]{0:T(128)}, u32[]{:S(2)}) copy-start(s32[8]{0:T(128)} %constant.22.clone) | copy-start | bytes 100
  135.4 1.9 %collective-permute-start.26 = (bf16[2,512,128]{2,1,0:T(8,128)(2,1)}, bf16[2,512,128]{2,1,0:T(8,128)(2,1)}, u32[]{:S(2)}, u32[]{:S(2)}) collective-permute-start(bf16[2,512,128]{2,1,0:T(8,128)(2,1)} %pad_maximum_fusion.13), channel_id=1, source_target_pairs={{0,1},{1,0},{2,3},{3,2},{4,5},{5,4},{6,7},{7,6},{8,9},{9,8},{10,11... | collective-permute-start | bytes 786440 | tf_op jit(solution)/shard_map/ppermute | solution.py:380
  138.3 6.4 %copy-start.2 = (bf16[16,256,512]{2,1,0:T(8,128)(2,1)S(1)}, bf16[16,256,512]{2,1,0:T(8,128)(2,1)}, u32[]{:S(2)}) copy-start(bf16[16,256,512]{2,1,0:T(8,128)(2,1)} %center_ref.31) | copy-start | bytes 12582916
  138.3 6.3 %copy-start.20 = (f32[1024,128]{1,0:T(8,128)S(1)}, f32[1024,128]{1,0:T(8,128)}, u32[]{:S(2)}) copy-start(f32[1024,128]{1,0:T(8,128)} %copy-done.19) | copy-start | bytes 1572868
  141.8 5.6 %collective-permute-start.28 = (bf16[512,128]{1,0:T(8,128)(2,1)S(1)}, bf16[512,128]{1,0:T(8,128)(2,1)S(1)}, u32[]{:S(2)}, u32[]{:S(2)}) collective-permute-start(bf16[512,128]{1,0:T(8,128)(2,1)S(1)} %get-tuple-element.144), channel_id=1, source_target_pairs={{0,16},{8,24},{16,0},{24,8},{1,17},{9,25},{17,1},{25,9},{2,18},{10... | collective-permute-start | bytes 393224 | tf_op jit(solution)/shard_map/ppermute | solution.py:380
  143.3 7.3 %copy-start.16 = (f32[1024,128]{1,0:T(8,128)S(1)}, f32[1024,128]{1,0:T(8,128)}, u32[]{:S(2)}) copy-start(f32[1024,128]{1,0:T(8,128)} %copy-done.15) | copy-start | bytes 1572868
  143.3 5.3 %collective-permute-start.27 = (bf16[512,128]{1,0:T(8,128)(2,1)S(1)}, bf16[512,128]{1,0:T(8,128)(2,1)S(1)}, u32[]{:S(2)}, u32[]{:S(2)}) collective-permute-start(bf16[512,128]{1,0:T(8,128)(2,1)S(1)} %get-tuple-element.145), channel_id=1, source_target_pairs={{0,8},{8,0},{16,24},{24,16},{1,9},{9,1},{17,25},{25,17},{2,10},{10... | collective-permute-start | bytes 393224 | tf_op jit(solution)/shard_map/ppermute | solution.py:380
  148.6 6.5 %copy-start.24 = (f32[1024,128]{1,0:T(8,128)S(1)}, f32[1024,128]{1,0:T(8,128)}, u32[]{:S(2)}) copy-start(f32[1024,128]{1,0:T(8,128)} %copy-done.23) | copy-start | bytes 1572868
  148.6 5.0 %collective-permute-start.30 = (bf16[512,128]{1,0:T(8,128)(2,1)S(1)}, bf16[512,128]{1,0:T(8,128)(2,1)S(1)}, u32[]{:S(2)}, u32[]{:S(2)}) collective-permute-start(bf16[512,128]{1,0:T(8,128)(2,1)S(1)} %get-tuple-element.142), channel_id=1, source_target_pairs={{0,8},{8,0},{16,24},{24,16},{1,9},{9,1},{17,25},{25,17},{2,10},{10... | collective-permute-start | bytes 393224 | tf_op jit(solution)/shard_map/ppermute | solution.py:380
  150.0 5.0 %collective-permute-start.29 = (bf16[512,128]{1,0:T(8,128)(2,1)S(1)}, bf16[512,128]{1,0:T(8,128)(2,1)S(1)}, u32[]{:S(2)}, u32[]{:S(2)}) collective-permute-start(bf16[512,128]{1,0:T(8,128)(2,1)S(1)} %get-tuple-element.143), channel_id=1, source_target_pairs={{0,16},{8,24},{16,0},{24,8},{1,17},{9,25},{17,1},{25,9},{2,18},{10... | collective-permute-start | bytes 393224 | tf_op jit(solution)/shard_map/ppermute | solution.py:380
  150.6 4.6 %copy-start.13 = (bf16[1024,1024]{1,0:T(8,128)(2,1)S(1)}, bf16[1024,1024]{1,0:T(8,128)(2,1)}, u32[]{:S(2)}) copy-start(bf16[1024,1024]{1,0:T(8,128)(2,1)} %scored_0_2.1.refs_2_) | copy-start | bytes 6291460
  150.6 4.6 %copy-start.14 = (bf16[1024,1024]{1,0:T(8,128)(2,1)S(1)}, bf16[1024,1024]{1,0:T(8,128)(2,1)}, u32[]{:S(2)}) copy-start(bf16[1024,1024]{1,0:T(8,128)(2,1)} %scored_0_1.1.refs_1_) | copy-start | bytes 6291460
  150.6 4.6 %copy-start.21 = (bf16[1024,1024]{1,0:T(8,128)(2,1)S(1)}, bf16[1024,1024]{1,0:T(8,128)(2,1)}, u32[]{:S(2)}) copy-start(bf16[1024,1024]{1,0:T(8,128)(2,1)} %get-tuple-element.85.refs_0_) | copy-start | bytes 6291460
  150.6 4.6 %copy-start.22 = (bf16[1024,1024]{1,0:T(8,128)(2,1)S(1)}, bf16[1024,1024]{1,0:T(8,128)(2,1)}, u32[]{:S(2)}) copy-start(bf16[1024,1024]{1,0:T(8,128)(2,1)} %get-tuple-element.96.refs_3_) | copy-start | bytes 6291460
  155.2 3.1 %copy-start.26 = (f32[512,128]{1,0:T(8,128)S(1)}, f32[512,128]{1,0:T(8,128)}, u32[]{:S(2)}) copy-start(f32[512,128]{1,0:T(8,128)} %copy-done.25) | copy-start | bytes 786436
  155.2 3.1 %copy-start.28 = (f32[512,128]{1,0:T(8,128)S(1)}, f32[512,128]{1,0:T(8,128)}, u32[]{:S(2)}) copy-start(f32[512,128]{1,0:T(8,128)} %copy-done.27) | copy-start | bytes 786436
  158.1 2.7 %copy-start.30 = (f32[512,128]{1,0:T(8,128)S(1)}, f32[512,128]{1,0:T(8,128)}, u32[]{:S(2)}) copy-start(f32[512,128]{1,0:T(8,128)} %copy-done.29) | copy-start | bytes 786436
  158.1 2.7 %copy-start.32 = (f32[512,128]{1,0:T(8,128)S(1)}, f32[512,128]{1,0:T(8,128)}, u32[]{:S(2)}) copy-start(f32[512,128]{1,0:T(8,128)} %copy-done.31) | copy-start | bytes 786436
  158.2 2.0 %collective-permute-start.31 = (bf16[4,512,128]{2,1,0:T(8,128)(2,1)S(1)}, bf16[4,512,128]{2,1,0:T(8,128)(2,1)S(1)}, u32[]{:S(2)}, u32[]{:S(2)}) collective-permute-start(bf16[4,512,128]{2,1,0:T(8,128)(2,1)S(1)} %slice.158), channel_id=1, source_target_pairs={{0,1},{1,0},{2,3},{3,2},{4,5},{5,4},{6,7},{7,6},{8,9},{9,8},{10,11... | collective-permute-start | bytes 1572872 | tf_op jit(solution)/shard_map/ppermute | solution.py:380
  160.3 8.4 %collective-permute-start.32 = (bf16[2,512,128]{2,1,0:T(8,128)(2,1)S(1)}, bf16[2,512,128]{2,1,0:T(8,128)(2,1)S(1)}, u32[]{:S(2)}, u32[]{:S(2)}) collective-permute-start(bf16[2,512,128]{2,1,0:T(8,128)(2,1)S(1)} %slice.160), channel_id=1, source_target_pairs={{0,2},{1,3},{2,0},{3,1},{4,6},{5,7},{6,4},{7,5},{8,10},{9,11},{10,... | collective-permute-start | bytes 786440 | tf_op jit(solution)/shard_map/ppermute | solution.py:380
  168.8 6.9 %collective-permute-start.33 = (bf16[1,512,128]{2,1,0:T(8,128)(2,1)S(1)}, bf16[1,512,128]{2,1,0:T(8,128)(2,1)S(1)}, u32[]{:S(2)}, u32[]{:S(2)}) collective-permute-start(bf16[1,512,128]{2,1,0:T(8,128)(2,1)S(1)} %slice.162), channel_id=1, source_target_pairs={{0,6},{1,7},{2,4},{3,5},{4,2},{5,3},{6,0},{7,1},{8,14},{9,15},{10,... | collective-permute-start | bytes 393224 | tf_op jit(solution)/shard_map/ppermute | solution.py:380
  (11 other events, 17.5 us)

commit v4 on v3

--- a/solution.py
+++ b/solution.py
@@ -175,8 +175,12 @@
     return pl.pallas_call(
         body,
         in_specs=[smem, stays],
-        out_specs=[stays] * (2 * chunks),
-        out_shape=[pltpu.HBM((chunk, dim), bf16)] * chunks + [pltpu.HBM((chunk, 128), f32)] * chunks,
+        out_specs=([vmem] + [stays] * (chunks - 1)) * 2,
+        out_shape=[
+            (jax.ShapeDtypeStruct if j == 0 else pltpu.HBM)((chunk, width), kind)
+            for width, kind in ((dim, bf16), (128, f32))
+            for j in range(chunks)
+        ],
         scratch_shapes=[
             pltpu.VMEM((rows * cuts, 128), f32),
             pltpu.VMEM((chunk * cuts, 128), f32),

time: 180 us -> 175 us (0.972)
  local copies, waits for them, and re-layouts: 6.06 us -> 3.2 us
    unnamed x82 -> x80, local copies, waits for them, and re-layouts: 4.68 us -> 1.82 us
  transfers between devices with their start and end apart: 34 -> 34, of which waited for: 20 -> 22; matrix products, arithmetic and copies ran while one was open for 1% -> 1% of each run, Pallas kernels for 42% -> 43%
where the time goes in v4:
time: 175 us; the launch traced here: 172 us
  Pallas kernels  91.8 us (52%)
  starting transfers between devices  35.3 us (20%)
  waiting for transfers between devices  32.6 us (19%)
  other arithmetic  7.03 us (4%)
  local copies, waits for them, and re-layouts  3.2 us (2%)
  between operations  1.93 us (1%)
    pallas_call x16, Pallas kernels, scored(): pl.pallas_call(body, in_specs=in_specs, out_specs=out_specs, out_shape=ou...  49.8 us
    ppermute x34, starting transfers between devices, swap(): return lax.ppermute(value, axis, [(i, i ^ mask) for i in range(size)])  35.3 us
    ppermute x34, waiting for transfers between devices, swap(): return lax.ppermute(value, axis, [(i, i ^ mask) for i in range(size)])  32.6 us
    pallas_call x10, Pallas kernels, panel_product(): pl.pallas_call(body, in_specs=[smem] * len(flips) + [stays if kept is Non...  26.6 us
    pallas_call x1, Pallas kernels, gathered(): pl.pallas_call(body, in_specs=[smem, stays], out_specs=([vmem] + [stays]...  12.4 us
  transfers between devices with their start and end apart: 34, of which 22 were waited for; matrix products, arithmetic and copies ran while one was open for 1% of the time, Pallas kernels for 43%

profile of v4, /device:TPU:0, one launch (start us, length us, event | category | flops | bytes accessed | tf_op | source)
XLA Modules:
  0.0 171.9 jit_solution(18421620098767626738)
XLA Ops:
  0.6 1.1 slice.109
  1.7 3.3 %inverse_3.1 = bf16[2,512,128]{2,1,0:T(8,128)(2,1)S(1)} custom-call(bf16[4,4,256,8,256]{4,3,2,1,0:T(8,128)(2,1)} %refs_1_.11, bf16[4,512,128]{2,1,0:T(8,128)(2,1)S(1)} %bitcast.69), custom_call_target="tpu_custom_call" | custom-call | flops 1073741824 | bytes 4194304 | tf_op jit(solution)/shard_map/inverse_3/pallas_call | solution.py:85
  5.1 3.0 %collective-permute-start.1 = (bf16[512,128]{1,0:T(8,128)(2,1)S(1)}, bf16[512,128]{1,0:T(8,128)(2,1)S(1)}, u32[]{:S(2)}, u32[]{:S(2)}) collective-permute-start(bf16[512,128]{1,0:T(8,128)(2,1)S(1)} %get-tuple-element.168), channel_id=1, source_target_pairs={{0,16},{8,24},{16,0},{24,8},{1,17},{9,25},{17,1},{25,9},{2,18},{10... | collective-permute-start | bytes 393224 | tf_op jit(solution)/shard_map/ppermute | solution.py:384
  8.1 1.5 collective-permute-start
  9.7 12.4 %gathered_0.1 = (bf16[1024,512]{1,0:T(8,128)(2,1)S(1)}, bf16[1024,512]{1,0:T(8,128)(2,1)}, bf16[1024,512]{1,0:T(8,128)(2,1)}, bf16[1024,512]{1,0:T(8,128)(2,1)},...) custom-call(s32[4096]{0:T(1024)S(1)} %broadcast_multiply_fusion.located_ref, ...), custom_call_target="tpu_custom_call" | custom-call | bytes 52428800 | tf_op jit(solution)/shard_map/gathered_0/pallas_call | solution.py:175
  23.0 4.1 %scored_0_0.1 = (bf16[1024,1024]{1,0:T(8,128)(2,1)}, f32[4,1,256]{2,1,0:T(1,128)S(1)}, bf16[8,256,4,256]{3,2,1,0:T(4,128)(2,1)S(1)}) custom-call(s32[4]{0:T(128)S(1)} %get-tuple-element.94.slots_ref, bf16[1024,512]{1,0:T(8,128)(2,1)S(1)} %get-tuple-element.73.span_ref, f32[1024,128]{1,0:T(8,128)S(1)} %get-tuple-element.77.norm_ref, ...), custom_call_target="tpu_custom_call" | custom-call | flops 1610612736 | bytes 1048576 | tf_op jit(solution)/shard_map/scored_0_0/pallas_call | solution.py:279
  28.1 1.7 %factor_2_3.1 = bf16[4,512,128]{2,1,0:T(8,128)(2,1)S(1)} custom-call(s32[1]{0:T(128)} %bitcast.refs_0_, bf16[8,256,4,256]{3,2,1,0:T(4,128)(2,1)S(1)} %get-tuple-element.84.refs_1_, bf16[1,1024,128]{2,1,0:T(8,128)(2,1)S(1)} %pad_maximum_fusion.8.refs_2_), custom_call_target="tpu_custom_call" | custom-call | flops 1073741824 | bytes 4194304 | tf_op jit(solution)/shard_map/factor_2_3/pallas_call | solution.py:85
  29.9 1.5 collective-permute-done.4
  31.5 1.6 collective-permute-start.5
  33.2 3.7 %factor_1_3.1.refs_3_ = f32[4,512,128]{2,1,0:T(8,128)S(1)} custom-call(s32[1]{0:T(128)} %bitcast.refs_0_, bf16[6,8,256,4,256]{4,3,2,1,0:T(4,128)(2,1)} %refs_3_.1, bf16[1,1024,128]{2,1,0:T(8,128)(2,1)S(1)} %bitcast.66), custom_call_target="tpu_custom_call" | custom-call | flops 1073741824 | bytes 4194304 | tf_op jit(solution)/shard_map/factor_1_3/pallas_call | solution.py:85
  37.2 3.7 %collective-permute-start.6 = (bf16[1,512,128]{2,1,0:T(8,128)(2,1)S(1)}, bf16[1,512,128]{2,1,0:T(8,128)(2,1)S(1)}, u32[]{:S(2)}, u32[]{:S(2)}) collective-permute-start(bf16[1,512,128]{2,1,0:T(8,128)(2,1)S(1)} %add_convert_fusion.13), channel_id=1, source_target_pairs={{0,6},{1,7},{2,4},{3,5},{4,2},{5,3},{6,0},{7,1},{8,14},{9,15},{10,... | collective-permute-start | bytes 393224 | tf_op jit(solution)/shard_map/ppermute | solution.py:384
  40.8 2.7 %scored_0_2.1.refs_2_ = bf16[1024,1024]{1,0:T(8,128)(2,1)} custom-call(s32[4]{0:T(128)S(1)} %get-tuple-element.94.slots_ref, bf16[1024,512]{1,0:T(8,128)(2,1)S(1)} %copy-done.3, f32[1024,128]{1,0:T(8,128)S(1)} %copy-done.11, bf16[16,256,512]{2,1,0:T(8,128)(2,1)S(1)} %copy-done.1, f32[4,1,256]{2,1,0:T(1,128)S(1)} %get-tuple-element.91.refs_0_), custom_call_target="tpu_custom_call" | custom-call | flops 1610612736 | bytes 1048576 | tf_op jit(solution)/shard_map/scored_0_2/pallas_call | solution.py:279
  43.6 2.7 %scored_0_1.1.refs_1_ = bf16[1024,1024]{1,0:T(8,128)(2,1)} custom-call(s32[4]{0:T(128)S(1)} %get-tuple-element.94.slots_ref, bf16[1024,512]{1,0:T(8,128)(2,1)S(1)} %copy-done.4, f32[1024,128]{1,0:T(8,128)S(1)} %copy-done.8, bf16[16,256,512]{2,1,0:T(8,128)(2,1)S(1)} %copy-done.1, f32[4,1,256]{2,1,0:T(1,128)S(1)} %get-tuple-element.91.refs_0_), custom_call_target="tpu_custom_call" | custom-call | flops 1610612736 | bytes 1048576 | tf_op jit(solution)/shard_map/scored_0_1/pallas_call | solution.py:279
  46.3 1.0 fusion
  47.6 4.0 %scored_0_3.1 = (bf16[1024,1024]{1,0:T(8,128)(2,1)}, bf16[4,256,8,256]{3,2,1,0:T(8,128)(2,1)S(1)}) custom-call(s32[4]{0:T(128)S(1)} %get-tuple-element.94.slots_ref, bf16[1024,512]{1,0:T(8,128)(2,1)S(1)} %copy-done.5, f32[1024,128]{1,0:T(8,128)S(1)} %copy-done.9, bf16[16,256,512]{2,1,0:T(8,128)(2,1)S(1)} %copy-done.1, ...), custom_call_target="tpu_custom_call" | custom-call | flops 1610612736 | bytes 1048576 | tf_op jit(solution)/shard_map/scored_0_3/pallas_call | solution.py:279
  52.4 1.5 collective-permute-done.8
  54.0 1.7 inverse_2.1
  55.7 1.3 collective-permute-start.10
  57.0 1.5 collective-permute-start.9
  58.5 3.8 %factor_0_3.1.refs_3_ = f32[4,512,128]{2,1,0:T(8,128)S(1)} custom-call(s32[1]{0:T(128)} %bitcast.refs_0_, bf16[6,8,256,4,256]{4,3,2,1,0:T(4,128)(2,1)} %refs_3_.1, bf16[1,1024,128]{2,1,0:T(8,128)(2,1)S(1)} %bitcast.67), custom_call_target="tpu_custom_call" | custom-call | flops 1073741824 | bytes 4194304 | tf_op jit(solution)/shard_map/factor_0_3/pallas_call | solution.py:85
  62.4 1.5 collective-permute-start.12
  64.7 4.6 %scored_3_0.1 = (f32[1024,128]{1,0:T(8,128)S(1)}, f32[4,1,256]{2,1,0:T(1,128)S(1)}, bf16[8,256,4,256]{3,2,1,0:T(4,128)(2,1)S(1)}) custom-call(s32[4]{0:T(128)S(1)} %get-tuple-element.112.slots_ref, bf16[1024,512]{1,0:T(8,128)(2,1)S(1)} %get-tuple-element.73.span_ref, f32[1024,128]{1,0:T(8,128)S(1)} %copy-done.7, bf16[16,256,512]{2,1,0:T(8,128)(2,1)S(1)} %copy-done.1, ...), custom_call_target="tpu_custom_call" | custom-call | flops 1610612736 | bytes 1048576 | tf_op jit(solution)/shard_map/scored_3_0/pallas_call | solution.py:279
  69.4 1.8 %factor_1_2.1 = bf16[4,512,128]{2,1,0:T(8,128)(2,1)S(1)} custom-call(s32[1]{0:T(128)} %bitcast.refs_0_, bf16[8,256,4,256]{3,2,1,0:T(4,128)(2,1)S(1)} %get-tuple-element.102.refs_1_, bf16[1,1024,128]{2,1,0:T(8,128)(2,1)S(1)} %pad_maximum_fusion.10.refs_2_, f32[4,512,128]{2,1,0:T(8,128)S(1)} %factor_1_3.1.refs_3_), custom_call_target="tpu_custom_call" | custom-call | flops 1073741824 | bytes 4194304 | tf_op jit(solution)/shard_map/factor_1_2/pallas_call | solution.py:85
  71.3 1.5 collective-permute-done.13
  72.9 1.1 collective-permute-start.14
  74.1 3.6 %factor_0_2.1.refs_3_ = f32[4,512,128]{2,1,0:T(8,128)S(1)} custom-call(s32[1]{0:T(128)} %bitcast.refs_0_, bf16[6,8,256,4,256]{4,3,2,1,0:T(4,128)(2,1)} %refs_3_.1, bf16[1,1024,128]{2,1,0:T(8,128)(2,1)S(1)} %bitcast.68, f32[4,512,128]{2,1,0:T(8,128)S(1)} %factor_0_3.1.refs_3_), custom_call_target="tpu_custom_call" | custom-call | flops 1073741824 | bytes 4194304 | tf_op jit(solution)/shard_map/factor_0_2/pallas_call | solution.py:85
  78.6 2.0 %collective-permute-start.15 = (bf16[1,512,128]{2,1,0:T(8,128)(2,1)S(1)}, bf16[1,512,128]{2,1,0:T(8,128)(2,1)S(1)}, u32[]{:S(2)}, u32[]{:S(2)}) collective-permute-start(bf16[1,512,128]{2,1,0:T(8,128)(2,1)S(1)} %add_convert_fusion.10), channel_id=1, source_target_pairs={{0,6},{1,7},{2,4},{3,5},{4,2},{5,3},{6,0},{7,1},{8,14},{9,15},{10,... | collective-permute-start | bytes 393224 | tf_op jit(solution)/shard_map/ppermute | solution.py:384
  80.6 2.5 %scored_3_2.1.refs_2_ = f32[1024,128]{1,0:T(8,128)S(1)} custom-call(s32[4]{0:T(128)S(1)} %get-tuple-element.112.slots_ref, bf16[1024,512]{1,0:T(8,128)(2,1)S(1)} %copy-done.3, f32[1024,128]{1,0:T(8,128)S(1)} %copy-done.11, bf16[16,256,512]{2,1,0:T(8,128)(2,1)S(1)} %copy-done.1, f32[4,1,256]{2,1,0:T(1,128)S(1)} %get-tuple-element.109.refs_0_, ...), custom_call_target="tpu_custom_call" | custom-call | flops 1610612736 | bytes 1048576 | tf_op jit(solution)/shard_map/scored_3_2/pallas_call | solution.py:279
  83.1 2.9 %scored_3_1.1.refs_2_ = f32[1024,128]{1,0:T(8,128)S(1)} custom-call(s32[4]{0:T(128)S(1)} %get-tuple-element.112.slots_ref, bf16[1024,512]{1,0:T(8,128)(2,1)S(1)} %copy-done.4, f32[1024,128]{1,0:T(8,128)S(1)} %copy-done.8, bf16[16,256,512]{2,1,0:T(8,128)(2,1)S(1)} %copy-done.1, f32[4,1,256]{2,1,0:T(1,128)S(1)} %get-tuple-element.109.refs_0_, ...), custom_call_target="tpu_custom_call" | custom-call | flops 1610612736 | bytes 1048576 | tf_op jit(solution)/shard_map/scored_3_1/pallas_call | solution.py:279
  86.1 1.0 fusion.1
  87.0 1.2 collective-permute-start.16
  88.2 4.3 %scored_3_3.1 = (f32[1024,128]{1,0:T(8,128)S(1)}, bf16[4,256,8,256]{3,2,1,0:T(8,128)(2,1)S(1)}) custom-call(s32[4]{0:T(128)S(1)} %get-tuple-element.112.slots_ref, bf16[1024,512]{1,0:T(8,128)(2,1)S(1)} %copy-done.5, f32[1024,128]{1,0:T(8,128)S(1)} %copy-done.9, bf16[16,256,512]{2,1,0:T(8,128)(2,1)S(1)} %copy-done.1, ...), custom_call_target="tpu_custom_call" | custom-call | flops 1610612736 | bytes 1048576 | tf_op jit(solution)/shard_map/scored_3_3/pallas_call | solution.py:279
  92.7 1.5 collective-permute-done.17
  94.2 1.7 %inverse_1.1 = bf16[2,512,128]{2,1,0:T(8,128)(2,1)S(1)} custom-call(s32[1]{0:T(128)} %bitcast.refs_0_, bf16[4,256,8,256]{3,2,1,0:T(8,128)(2,1)S(1)} %get-tuple-element.113.refs_1_, bf16[4,512,128]{2,1,0:T(8,128)(2,1)S(1)} %pad_maximum_fusion.4.refs_2_), custom_call_target="tpu_custom_call" | custom-call | flops 1073741824 | bytes 4194304 | tf_op jit(solution)/shard_map/inverse_1/pallas_call | solution.py:85
  96.0 1.3 collective-permute-start.19
  97.9 2.5 %scored_2_0.1 = (f32[1024,128]{1,0:T(8,128)S(1)}, f32[4,1,256]{2,1,0:T(1,128)S(1)}) custom-call(s32[4]{0:T(128)S(1)} %get-tuple-element.128.slots_ref, bf16[1024,512]{1,0:T(8,128)(2,1)S(1)} %get-tuple-element.73.span_ref, f32[1024,128]{1,0:T(8,128)S(1)} %copy-done.7, bf16[16,256,512]{2,1,0:T(8,128)(2,1)S(1)} %copy-done.1, ...), custom_call_target="tpu_custom_call" | custom-call | flops 1610612736 | bytes 1048576 | tf_op jit(solution)/shard_map/scored_2_0/pallas_call | solution.py:279
  100.4 1.2 collective-permute-done.19
  104.1 4.4 %scored_2_1.1 = (f32[1024,128]{1,0:T(8,128)S(1)}, bf16[8,256,4,256]{3,2,1,0:T(4,128)(2,1)S(1)}) custom-call(s32[4]{0:T(128)S(1)} %get-tuple-element.128.slots_ref, bf16[1024,512]{1,0:T(8,128)(2,1)S(1)} %copy-done.4, f32[1024,128]{1,0:T(8,128)S(1)} %copy-done.8, bf16[16,256,512]{2,1,0:T(8,128)(2,1)S(1)} %copy-done.1, ...), custom_call_target="tpu_custom_call" | custom-call | flops 1610612736 | bytes 1048576 | tf_op jit(solution)/shard_map/scored_2_1/pallas_call | solution.py:279
  108.7 1.8 %factor_0_1.1 = bf16[4,512,128]{2,1,0:T(8,128)(2,1)S(1)} custom-call(s32[1]{0:T(128)} %bitcast.refs_0_, bf16[8,256,4,256]{3,2,1,0:T(4,128)(2,1)S(1)} %get-tuple-element.122.refs_1_, bf16[1,1024,128]{2,1,0:T(8,128)(2,1)S(1)} %pad_maximum_fusion.12.refs_2_, f32[4,512,128]{2,1,0:T(8,128)S(1)} %factor_0_2.1.refs_3_), custom_call_target="tpu_custom_call" | custom-call | flops 1073741824 | bytes 4194304 | tf_op jit(solution)/shard_map/factor_0_1/pallas_call | solution.py:85
  110.6 1.5 collective-permute-done.22
  112.2 0.9 collective-permute-start.23
  113.2 2.5 %scored_2_2.1.refs_2_ = f32[1024,128]{1,0:T(8,128)S(1)} custom-call(s32[4]{0:T(128)S(1)} %get-tuple-element.128.slots_ref, bf16[1024,512]{1,0:T(8,128)(2,1)S(1)} %copy-done.3, f32[1024,128]{1,0:T(8,128)S(1)} %copy-done.11, bf16[16,256,512]{2,1,0:T(8,128)(2,1)S(1)} %copy-done.1, f32[4,1,256]{2,1,0:T(1,128)S(1)} %get-tuple-element.121.refs_0_, ...), custom_call_target="tpu_custom_call" | custom-call | flops 1610612736 | bytes 1048576 | tf_op jit(solution)/shard_map/scored_2_2/pallas_call | solution.py:279
  115.7 2.1 %collective-permute-done.23 = bf16[1,512,128]{2,1,0:T(8,128)(2,1)S(1)} collective-permute-done((bf16[1,512,128]{2,1,0:T(8,128)(2,1)S(1)}, bf16[1,512,128]{2,1,0:T(8,128)(2,1)S(1)}, u32[]{:S(2)}, u32[]{:S(2)}) %collective-permute-start.23) | collective-permute-done | bytes 131104 | tf_op jit(solution)/shard_map/ppermute | solution.py:384
  117.9 2.1 %collective-permute-start.24 = (bf16[1,512,128]{2,1,0:T(8,128)(2,1)S(1)}, bf16[1,512,128]{2,1,0:T(8,128)(2,1)S(1)}, u32[]{:S(2)}, u32[]{:S(2)}) collective-permute-start(bf16[1,512,128]{2,1,0:T(8,128)(2,1)S(1)} %add_convert_fusion.7), channel_id=1, source_target_pairs={{0,6},{1,7},{2,4},{3,5},{4,2},{5,3},{6,0},{7,1},{8,14},{9,15},{10,... | collective-permute-start | bytes 393224 | tf_op jit(solution)/shard_map/ppermute | solution.py:384
  119.9 2.5 %scored_2_3.1.refs_2_ = f32[1024,128]{1,0:T(8,128)S(1)} custom-call(s32[4]{0:T(128)S(1)} %get-tuple-element.128.slots_ref, bf16[1024,512]{1,0:T(8,128)(2,1)S(1)} %copy-done.5, f32[1024,128]{1,0:T(8,128)S(1)} %copy-done.9, bf16[16,256,512]{2,1,0:T(8,128)(2,1)S(1)} %copy-done.1, f32[4,1,256]{2,1,0:T(1,128)S(1)} %get-tuple-element.121.refs_0_, ...), custom_call_target="tpu_custom_call" | custom-call | flops 1610612736 | bytes 1048576 | tf_op jit(solution)/shard_map/scored_2_3/pallas_call | solution.py:279
  123.3 2.5 %scored_1_0.1 = (f32[1024,128]{1,0:T(8,128)S(1)}, f32[4,1,256]{2,1,0:T(1,128)S(1)}) custom-call(s32[4]{0:T(128)S(1)} %get-tuple-element.139.slots_ref, bf16[1024,512]{1,0:T(8,128)(2,1)S(1)} %get-tuple-element.73.span_ref, f32[1024,128]{1,0:T(8,128)S(1)} %copy-done.7, bf16[16,256,512]{2,1,0:T(8,128)(2,1)S(1)} %copy-done.1, ...), custom_call_target="tpu_custom_call" | custom-call | flops 1610612736 | bytes 1048576 | tf_op jit(solution)/shard_map/scored_1_0/pallas_call | solution.py:279
  125.8 1.1 fusion.2
  127.6 2.5 %scored_1_1.1.refs_6_ = f32[1024,128]{1,0:T(8,128)S(1)} custom-call(s32[4]{0:T(128)S(1)} %get-tuple-element.139.slots_ref, bf16[1024,512]{1,0:T(8,128)(2,1)S(1)} %copy-done.4, f32[1024,128]{1,0:T(8,128)S(1)} %copy-done.8, bf16[16,256,512]{2,1,0:T(8,128)(2,1)S(1)} %copy-done.1, f32[4,1,256]{2,1,0:T(1,128)S(1)} %get-tuple-element.134.refs_0_, ...), custom_call_target="tpu_custom_call" | custom-call | flops 1610612736 | bytes 1048576 | tf_op jit(solution)/shard_map/scored_1_1/pallas_call | solution.py:279
  131.0 1.0 collective-permute-done.25
  132.1 1.5 collective-permute-done.26
  133.7 3.4 %inverse_0.1 = bf16[2,512,128]{2,1,0:T(8,128)(2,1)S(1)} custom-call(s32[1]{0:T(128)} %bitcast.refs_0_, bf16[4,4,256,8,256]{4,3,2,1,0:T(8,128)(2,1)} %refs_1_.11, bf16[4,512,128]{2,1,0:T(8,128)(2,1)S(1)} %pad_maximum_fusion.6.refs_2_), custom_call_target="tpu_custom_call" | custom-call | flops 1073741824 | bytes 4194304 | tf_op jit(solution)/shard_map/inverse_0/pallas_call | solution.py:85
  137.2 1.3 collective-permute-start.28
  138.5 1.4 collective-permute-start.27
  139.9 2.5 %scored_1_2.1.refs_7_ = f32[1024,128]{1,0:T(8,128)S(1)} custom-call(s32[4]{0:T(128)S(1)} %get-tuple-element.139.slots_ref, bf16[1024,512]{1,0:T(8,128)(2,1)S(1)} %copy-done.3, f32[1024,128]{1,0:T(8,128)S(1)} %copy-done.12, bf16[16,256,512]{2,1,0:T(8,128)(2,1)S(1)} %copy-done.2, f32[4,1,256]{2,1,0:T(1,128)S(1)} %get-tuple-element.134.refs_0_, ...), custom_call_target="tpu_custom_call" | custom-call | flops 1610612736 | bytes 1048576 | tf_op jit(solution)/shard_map/scored_1_2/pallas_call | solution.py:279
  142.8 0.9 collective-permute-done.27
  143.8 1.5 collective-permute-start.30
  146.1 2.5 %scored_1_3.1.refs_8_ = f32[1024,128]{1,0:T(8,128)S(1)} custom-call(s32[4]{0:T(128)S(1)} %get-tuple-element.139.slots_ref, bf16[1024,512]{1,0:T(8,128)(2,1)S(1)} %copy-done.5, f32[1024,128]{1,0:T(8,128)S(1)} %copy-done.10, bf16[16,256,512]{2,1,0:T(8,128)(2,1)S(1)} %copy-done.2, f32[4,1,256]{2,1,0:T(1,128)S(1)} %get-tuple-element.134.refs_0_, ...), custom_call_target="tpu_custom_call" | custom-call | flops 1610612736 | bytes 1048576 | tf_op jit(solution)/shard_map/scored_1_3/pallas_call | solution.py:279
  148.8 1.4 collective-permute-done.29
  150.4 2.9 %finished.1 = bf16[8,512,128]{2,1,0:T(8,128)(2,1)S(1)} custom-call(s32[8]{0:T(128)S(1)} %broadcast_xor_fusion.places_ref, bf16[1024,1024]{1,0:T(8,128)(2,1)S(1)} %copy-done.21, bf16[1024,1024]{1,0:T(8,128)(2,1)S(1)} %copy-done.14, bf16[1024,1024]{1,0:T(8,128)(2,1)S(1)} %copy-done.13, bf16[1024,1024]{1,0:T(8,128)(2,1)S(1)} %copy-done.22, ...), custom_call_target="tpu_custom_call" | custom-call | flops 2147483648 | bytes 8388608 | tf_op jit(solution)/shard_map/finished/pallas_call | solution.py:316
  153.5 1.8 %collective-permute-done.31 = bf16[4,512,128]{2,1,0:T(8,128)(2,1)S(1)} collective-permute-done((bf16[4,512,128]{2,1,0:T(8,128)(2,1)S(1)}, bf16[4,512,128]{2,1,0:T(8,128)(2,1)S(1)}, u32[]{:S(2)}, u32[]{:S(2)}) %collective-permute-start.31) | collective-permute-done | bytes 524320 | tf_op jit(solution)/shard_map/ppermute | solution.py:384
  156.3 7.7 %collective-permute-done.32 = bf16[2,512,128]{2,1,0:T(8,128)(2,1)S(1)} collective-permute-done((bf16[2,512,128]{2,1,0:T(8,128)(2,1)S(1)}, bf16[2,512,128]{2,1,0:T(8,128)(2,1)S(1)}, u32[]{:S(2)}, u32[]{:S(2)}) %collective-permute-start.32) | collective-permute-done | bytes 262176 | tf_op jit(solution)/shard_map/ppermute | solution.py:384
  164.1 2.0 %collective-permute-start.33 = (bf16[1,512,128]{2,1,0:T(8,128)(2,1)S(1)}, bf16[1,512,128]{2,1,0:T(8,128)(2,1)S(1)}, u32[]{:S(2)}, u32[]{:S(2)}) collective-permute-start(bf16[1,512,128]{2,1,0:T(8,128)(2,1)S(1)} %slice.162), channel_id=1, source_target_pairs={{0,6},{1,7},{2,4},{3,5},{4,2},{5,3},{6,0},{7,1},{8,14},{9,15},{10,... | collective-permute-start | bytes 393224 | tf_op jit(solution)/shard_map/ppermute | solution.py:384
  166.1 1.5 pad_maximum_fusion
  167.5 3.4 %collective-permute-done.33 = bf16[1,512,128]{2,1,0:T(8,128)(2,1)S(1)} collective-permute-done((bf16[1,512,128]{2,1,0:T(8,128)(2,1)S(1)}, bf16[1,512,128]{2,1,0:T(8,128)(2,1)S(1)}, u32[]{:S(2)}, u32[]{:S(2)}) %collective-permute-start.33) | collective-permute-done | bytes 131104 | tf_op jit(solution)/shard_map/ppermute | solution.py:384
  (172 shorter events, 15.1 us)
Async XLA Ops:
  1.7 7.9 %copy-start.38 = (s32[16,1]{0,1:T(1,128)S(1)}, s32[16,1]{0,1:T(1,128)}, u32[]{:S(2)}) copy-start(s32[16,1]{0,1:T(1,128)} %param.12) | copy-start | bytes 196
  1.7 8.0 %copy-start.37 = (s32[4096]{0:T(1024)S(1)}, s32[4096]{0:T(1024)}, u32[]{:S(2)}) copy-start(s32[4096]{0:T(1024)} %param.14) | copy-start | bytes 49156
  5.1 17.2 %collective-permute-start.1 = (bf16[512,128]{1,0:T(8,128)(2,1)S(1)}, bf16[512,128]{1,0:T(8,128)(2,1)S(1)}, u32[]{:S(2)}, u32[]{:S(2)}) collective-permute-start(bf16[512,128]{1,0:T(8,128)(2,1)S(1)} %get-tuple-element.168), channel_id=1, source_target_pairs={{0,16},{8,24},{16,0},{24,8},{1,17},{9,25},{17,1},{25,9},{2,18},{10... | collective-permute-start | bytes 393224 | tf_op jit(solution)/shard_map/ppermute | solution.py:384
  8.1 14.2 %collective-permute-start = (bf16[512,128]{1,0:T(8,128)(2,1)S(1)}, bf16[512,128]{1,0:T(8,128)(2,1)S(1)}, u32[]{:S(2)}, u32[]{:S(2)}) collective-permute-start(bf16[512,128]{1,0:T(8,128)(2,1)S(1)} %get-tuple-element.169), channel_id=1, source_target_pairs={{0,8},{8,0},{16,24},{24,16},{1,9},{9,1},{17,25},{25,17},{2,10},{10... | collective-permute-start | bytes 393224 | tf_op jit(solution)/shard_map/ppermute | solution.py:384
  9.7 13.3 %copy-start = (bf16[16,256,512]{2,1,0:T(8,128)(2,1)S(1)}, bf16[16,256,512]{2,1,0:T(8,128)(2,1)}, u32[]{:S(2)}) copy-start(bf16[16,256,512]{2,1,0:T(8,128)(2,1)} %center_ref.31) | copy-start | bytes 12582916
  22.2 5.0 %copy-start.6 = (f32[1024,128]{1,0:T(8,128)}, f32[1024,128]{1,0:T(8,128)S(1)}, u32[]{:S(2)}) copy-start(f32[1024,128]{1,0:T(8,128)S(1)} %get-tuple-element.77.norm_ref) | copy-start | bytes 1572868
  22.4 5.0 %collective-permute-start.3 = (bf16[512,128]{1,0:T(8,128)(2,1)S(1)}, bf16[512,128]{1,0:T(8,128)(2,1)S(1)}, u32[]{:S(2)}, u32[]{:S(2)}) collective-permute-start(bf16[512,128]{1,0:T(8,128)(2,1)S(1)} %get-tuple-element.166), channel_id=1, source_target_pairs={{0,8},{8,0},{16,24},{24,16},{1,9},{9,1},{17,25},{25,17},{2,10},{10... | collective-permute-start | bytes 393224 | tf_op jit(solution)/shard_map/ppermute | solution.py:384
  23.0 5.0 %collective-permute-start.2 = (bf16[512,128]{1,0:T(8,128)(2,1)S(1)}, bf16[512,128]{1,0:T(8,128)(2,1)S(1)}, u32[]{:S(2)}, u32[]{:S(2)}) collective-permute-start(bf16[512,128]{1,0:T(8,128)(2,1)S(1)} %get-tuple-element.167), channel_id=1, source_target_pairs={{0,16},{8,24},{16,0},{24,8},{1,17},{9,25},{17,1},{25,9},{2,18},{10... | collective-permute-start | bytes 393224 | tf_op jit(solution)/shard_map/ppermute | solution.py:384
  28.0 5.2 %copy-start.25 = (f32[512,128]{1,0:T(8,128)}, f32[512,128]{1,0:T(8,128)S(1)}, u32[]{:S(2)}) copy-start(f32[512,128]{1,0:T(8,128)S(1)} %get-tuple-element.165) | copy-start | bytes 786436
  28.0 5.1 %copy-start.27 = (f32[512,128]{1,0:T(8,128)}, f32[512,128]{1,0:T(8,128)S(1)}, u32[]{:S(2)}) copy-start(f32[512,128]{1,0:T(8,128)S(1)} %get-tuple-element.174) | copy-start | bytes 786436
  29.8 1.6 collective-permute-start.4
  31.5 5.6 %collective-permute-start.5 = (bf16[1,512,128]{2,1,0:T(8,128)(2,1)S(1)}, bf16[1,512,128]{2,1,0:T(8,128)(2,1)S(1)}, u32[]{:S(2)}, u32[]{:S(2)}) collective-permute-start(bf16[1,512,128]{2,1,0:T(8,128)(2,1)S(1)} %slice.142), channel_id=1, source_target_pairs={{0,2},{1,3},{2,0},{3,1},{4,6},{5,7},{6,4},{7,5},{8,10},{9,11},{10,... | collective-permute-start | bytes 393224 | tf_op jit(solution)/shard_map/ppermute | solution.py:384
  33.2 7.6 %copy-start.1 = (bf16[16,256,512]{2,1,0:T(8,128)(2,1)S(1)}, bf16[16,256,512]{2,1,0:T(8,128)(2,1)}, u32[]{:S(2)}) copy-start(bf16[16,256,512]{2,1,0:T(8,128)(2,1)} %center_ref.31) | copy-start | bytes 12582916
  33.2 7.6 %copy-start.3 = (bf16[1024,512]{1,0:T(8,128)(2,1)S(1)}, bf16[1024,512]{1,0:T(8,128)(2,1)}, u32[]{:S(2)}) copy-start(bf16[1024,512]{1,0:T(8,128)(2,1)} %get-tuple-element.75.span_ref) | copy-start | bytes 3145732
  33.2 7.6 %copy-start.11 = (f32[1024,128]{1,0:T(8,128)S(1)}, f32[1024,128]{1,0:T(8,128)}, u32[]{:S(2)}) copy-start(f32[1024,128]{1,0:T(8,128)} %get-tuple-element.79.norm_ref) | copy-start | bytes 1572868
  37.2 9.1 %collective-permute-start.6 = (bf16[1,512,128]{2,1,0:T(8,128)(2,1)S(1)}, bf16[1,512,128]{2,1,0:T(8,128)(2,1)S(1)}, u32[]{:S(2)}, u32[]{:S(2)}) collective-permute-start(bf16[1,512,128]{2,1,0:T(8,128)(2,1)S(1)} %add_convert_fusion.13), channel_id=1, source_target_pairs={{0,6},{1,7},{2,4},{3,5},{4,2},{5,3},{6,0},{7,1},{8,14},{9,15},{10,... | collective-permute-start | bytes 393224 | tf_op jit(solution)/shard_map/ppermute | solution.py:384
  43.6 4.0 %copy-start.5 = (bf16[1024,512]{1,0:T(8,128)(2,1)S(1)}, bf16[1024,512]{1,0:T(8,128)(2,1)}, u32[]{:S(2)}) copy-start(bf16[1024,512]{1,0:T(8,128)(2,1)} %get-tuple-element.76.span_ref) | copy-start | bytes 3145732
  43.6 4.0 %copy-start.9 = (f32[1024,128]{1,0:T(8,128)S(1)}, f32[1024,128]{1,0:T(8,128)}, u32[]{:S(2)}) copy-start(f32[1024,128]{1,0:T(8,128)} %get-tuple-element.80.norm_ref) | copy-start | bytes 1572868
  47.3 5.0 %collective-permute-start.7 = (bf16[1,512,128]{2,1,0:T(8,128)(2,1)S(1)}, bf16[1,512,128]{2,1,0:T(8,128)(2,1)S(1)}, u32[]{:S(2)}, u32[]{:S(2)}) collective-permute-start(bf16[1,512,128]{2,1,0:T(8,128)(2,1)S(1)} %fusion), channel_id=1, source_target_pairs={{0,2},{1,3},{2,0},{3,1},{4,6},{5,7},{6,4},{7,5},{8,10},{9,11},{10,... | collective-permute-start | bytes 393224 | tf_op jit(solution)/shard_map/ppermute | solution.py:384
  52.3 1.6 collective-permute-start.8
  55.7 6.6 %collective-permute-start.10 = (bf16[512,128]{1,0:T(8,128)(2,1)S(1)}, bf16[512,128]{1,0:T(8,128)(2,1)S(1)}, u32[]{:S(2)}, u32[]{:S(2)}) collective-permute-start(bf16[512,128]{1,0:T(8,128)(2,1)S(1)} %get-tuple-element.160), channel_id=1, source_target_pairs={{0,16},{8,24},{16,0},{24,8},{1,17},{9,25},{17,1},{25,9},{2,18},{10... | collective-permute-start | bytes 393224 | tf_op jit(solution)/shard_map/ppermute | solution.py:384
  57.0 5.3 %collective-permute-start.9 = (bf16[512,128]{1,0:T(8,128)(2,1)S(1)}, bf16[512,128]{1,0:T(8,128)(2,1)S(1)}, u32[]{:S(2)}, u32[]{:S(2)}) collective-permute-start(bf16[512,128]{1,0:T(8,128)(2,1)S(1)} %get-tuple-element.161), channel_id=1, source_target_pairs={{0,8},{8,0},{16,24},{24,16},{1,9},{9,1},{17,25},{25,17},{2,10},{10... | collective-permute-start | bytes 393224 | tf_op jit(solution)/shard_map/ppermute | solution.py:384
  58.4 6.2 %copy-start.7 = (f32[1024,128]{1,0:T(8,128)S(1)}, f32[1024,128]{1,0:T(8,128)}, u32[]{:S(2)}) copy-start(f32[1024,128]{1,0:T(8,128)} %copy-done.6) | copy-start | bytes 1572868
  62.4 6.9 %collective-permute-start.12 = (bf16[512,128]{1,0:T(8,128)(2,1)S(1)}, bf16[512,128]{1,0:T(8,128)(2,1)S(1)}, u32[]{:S(2)}, u32[]{:S(2)}) collective-permute-start(bf16[512,128]{1,0:T(8,128)(2,1)S(1)} %get-tuple-element.158), channel_id=1, source_target_pairs={{0,8},{8,0},{16,24},{24,16},{1,9},{9,1},{17,25},{25,17},{2,10},{10... | collective-permute-start | bytes 393224 | tf_op jit(solution)/shard_map/ppermute | solution.py:384
  63.9 5.4 %collective-permute-start.11 = (bf16[512,128]{1,0:T(8,128)(2,1)S(1)}, bf16[512,128]{1,0:T(8,128)(2,1)S(1)}, u32[]{:S(2)}, u32[]{:S(2)}) collective-permute-start(bf16[512,128]{1,0:T(8,128)(2,1)S(1)} %get-tuple-element.159), channel_id=1, source_target_pairs={{0,16},{8,24},{16,0},{24,8},{1,17},{9,25},{17,1},{25,9},{2,18},{10... | collective-permute-start | bytes 393224 | tf_op jit(solution)/shard_map/ppermute | solution.py:384
  69.3 4.7 %copy-start.29 = (f32[512,128]{1,0:T(8,128)}, f32[512,128]{1,0:T(8,128)S(1)}, u32[]{:S(2)}) copy-start(f32[512,128]{1,0:T(8,128)S(1)} %get-tuple-element.155) | copy-start | bytes 786436
  69.4 4.7 %copy-start.31 = (f32[512,128]{1,0:T(8,128)}, f32[512,128]{1,0:T(8,128)S(1)}, u32[]{:S(2)}) copy-start(f32[512,128]{1,0:T(8,128)S(1)} %get-tuple-element.157) | copy-start | bytes 786436
  71.2 1.6 collective-permute-start.13
  72.9 5.6 %collective-permute-start.14 = (bf16[1,512,128]{2,1,0:T(8,128)(2,1)S(1)}, bf16[1,512,128]{2,1,0:T(8,128)(2,1)S(1)}, u32[]{:S(2)}, u32[]{:S(2)}) collective-permute-start(bf16[1,512,128]{2,1,0:T(8,128)(2,1)S(1)} %slice.148), channel_id=1, source_target_pairs={{0,2},{1,3},{2,0},{3,1},{4,6},{5,7},{6,4},{7,5},{8,10},{9,11},{10,... | collective-permute-start | bytes 393224 | tf_op jit(solution)/shard_map/ppermute | solution.py:384
  78.6 7.5 %collective-permute-start.15 = (bf16[1,512,128]{2,1,0:T(8,128)(2,1)S(1)}, bf16[1,512,128]{2,1,0:T(8,128)(2,1)S(1)}, u32[]{:S(2)}, u32[]{:S(2)}) collective-permute-start(bf16[1,512,128]{2,1,0:T(8,128)(2,1)S(1)} %add_convert_fusion.10), channel_id=1, source_target_pairs={{0,6},{1,7},{2,4},{3,5},{4,2},{5,3},{6,0},{7,1},{8,14},{9,15},{10,... | collective-permute-start | bytes 393224 | tf_op jit(solution)/shard_map/ppermute | solution.py:384
  87.0 5.5 %collective-permute-start.16 = (bf16[1,512,128]{2,1,0:T(8,128)(2,1)S(1)}, bf16[1,512,128]{2,1,0:T(8,128)(2,1)S(1)}, u32[]{:S(2)}, u32[]{:S(2)}) collective-permute-start(bf16[1,512,128]{2,1,0:T(8,128)(2,1)S(1)} %fusion.1), channel_id=1, source_target_pairs={{0,2},{1,3},{2,0},{3,1},{4,6},{5,7},{6,4},{7,5},{8,10},{9,11},{10,... | collective-permute-start | bytes 393224 | tf_op jit(solution)/shard_map/ppermute | solution.py:384
  92.6 1.6 collective-permute-start.17
  96.0 5.6 %collective-permute-start.19 = (bf16[512,128]{1,0:T(8,128)(2,1)S(1)}, bf16[512,128]{1,0:T(8,128)(2,1)S(1)}, u32[]{:S(2)}, u32[]{:S(2)}) collective-permute-start(bf16[512,128]{1,0:T(8,128)(2,1)S(1)} %get-tuple-element.152), channel_id=1, source_target_pairs={{0,16},{8,24},{16,0},{24,8},{1,17},{9,25},{17,1},{25,9},{2,18},{10... | collective-permute-start | bytes 393224 | tf_op jit(solution)/shard_map/ppermute | solution.py:384
  97.3 5.3 %collective-permute-start.18 = (bf16[512,128]{1,0:T(8,128)(2,1)S(1)}, bf16[512,128]{1,0:T(8,128)(2,1)S(1)}, u32[]{:S(2)}, u32[]{:S(2)}) collective-permute-start(bf16[512,128]{1,0:T(8,128)(2,1)S(1)} %get-tuple-element.153), channel_id=1, source_target_pairs={{0,8},{8,0},{16,24},{24,16},{1,9},{9,1},{17,25},{25,17},{2,10},{10... | collective-permute-start | bytes 393224 | tf_op jit(solution)/shard_map/ppermute | solution.py:384
  102.6 5.9 %collective-permute-start.21 = (bf16[512,128]{1,0:T(8,128)(2,1)S(1)}, bf16[512,128]{1,0:T(8,128)(2,1)S(1)}, u32[]{:S(2)}, u32[]{:S(2)}) collective-permute-start(bf16[512,128]{1,0:T(8,128)(2,1)S(1)} %get-tuple-element.150), channel_id=1, source_target_pairs={{0,8},{8,0},{16,24},{24,16},{1,9},{9,1},{17,25},{25,17},{2,10},{10... | collective-permute-start | bytes 393224 | tf_op jit(solution)/shard_map/ppermute | solution.py:384
  103.3 5.2 %collective-permute-start.20 = (bf16[512,128]{1,0:T(8,128)(2,1)S(1)}, bf16[512,128]{1,0:T(8,128)(2,1)S(1)}, u32[]{:S(2)}, u32[]{:S(2)}) collective-permute-start(bf16[512,128]{1,0:T(8,128)(2,1)S(1)} %get-tuple-element.151), channel_id=1, source_target_pairs={{0,16},{8,24},{16,0},{24,8},{1,17},{9,25},{17,1},{25,9},{2,18},{10... | collective-permute-start | bytes 393224 | tf_op jit(solution)/shard_map/ppermute | solution.py:384
  110.5 1.6 collective-permute-start.22
  112.2 5.6 %collective-permute-start.23 = (bf16[1,512,128]{2,1,0:T(8,128)(2,1)S(1)}, bf16[1,512,128]{2,1,0:T(8,128)(2,1)S(1)}, u32[]{:S(2)}, u32[]{:S(2)}) collective-permute-start(bf16[1,512,128]{2,1,0:T(8,128)(2,1)S(1)} %slice.154), channel_id=1, source_target_pairs={{0,2},{1,3},{2,0},{3,1},{4,6},{5,7},{6,4},{7,5},{8,10},{9,11},{10,... | collective-permute-start | bytes 393224 | tf_op jit(solution)/shard_map/ppermute | solution.py:384
  115.7 6.8 %copy-start.19 = (f32[1024,128]{1,0:T(8,128)}, f32[1024,128]{1,0:T(8,128)S(1)}, u32[]{:S(2)}) copy-start(f32[1024,128]{1,0:T(8,128)S(1)} %scored_2_2.1.refs_2_) | copy-start | bytes 1572868
  117.9 8.0 %collective-permute-start.24 = (bf16[1,512,128]{2,1,0:T(8,128)(2,1)S(1)}, bf16[1,512,128]{2,1,0:T(8,128)(2,1)S(1)}, u32[]{:S(2)}, u32[]{:S(2)}) collective-permute-start(bf16[1,512,128]{2,1,0:T(8,128)(2,1)S(1)} %add_convert_fusion.7), channel_id=1, source_target_pairs={{0,6},{1,7},{2,4},{3,5},{4,2},{5,3},{6,0},{7,1},{8,14},{9,15},{10,... | collective-permute-start | bytes 393224 | tf_op jit(solution)/shard_map/ppermute | solution.py:384
  127.0 5.0 %collective-permute-start.25 = (bf16[1,512,128]{2,1,0:T(8,128)(2,1)S(1)}, bf16[1,512,128]{2,1,0:T(8,128)(2,1)S(1)}, u32[]{:S(2)}, u32[]{:S(2)}) collective-permute-start(bf16[1,512,128]{2,1,0:T(8,128)(2,1)S(1)} %fusion.2), channel_id=1, source_target_pairs={{0,2},{1,3},{2,0},{3,1},{4,6},{5,7},{6,4},{7,5},{8,10},{9,11},{10,... | collective-permute-start | bytes 393224 | tf_op jit(solution)/shard_map/ppermute | solution.py:384
  127.6 4.5 %copy-start.39 = (s32[8]{0:T(128)S(1)}, s32[8]{0:T(128)}, u32[]{:S(2)}) copy-start(s32[8]{0:T(128)} %constant.22.clone) | copy-start | bytes 100
  132.0 1.6 collective-permute-start.26
  133.7 6.2 %copy-start.2 = (bf16[16,256,512]{2,1,0:T(8,128)(2,1)S(1)}, bf16[16,256,512]{2,1,0:T(8,128)(2,1)}, u32[]{:S(2)}) copy-start(bf16[16,256,512]{2,1,0:T(8,128)(2,1)} %center_ref.31) | copy-start | bytes 12582916
  133.7 6.2 %copy-start.12 = (f32[1024,128]{1,0:T(8,128)S(1)}, f32[1024,128]{1,0:T(8,128)}, u32[]{:S(2)}) copy-start(f32[1024,128]{1,0:T(8,128)} %get-tuple-element.79.norm_ref) | copy-start | bytes 1572868
  133.7 6.2 %copy-start.20 = (f32[1024,128]{1,0:T(8,128)S(1)}, f32[1024,128]{1,0:T(8,128)}, u32[]{:S(2)}) copy-start(f32[1024,128]{1,0:T(8,128)} %copy-done.19) | copy-start | bytes 1572868
  137.2 5.6 %collective-permute-start.28 = (bf16[512,128]{1,0:T(8,128)(2,1)S(1)}, bf16[512,128]{1,0:T(8,128)(2,1)S(1)}, u32[]{:S(2)}, u32[]{:S(2)}) collective-permute-start(bf16[512,128]{1,0:T(8,128)(2,1)S(1)} %get-tuple-element.144), channel_id=1, source_target_pairs={{0,16},{8,24},{16,0},{24,8},{1,17},{9,25},{17,1},{25,9},{2,18},{10... | collective-permute-start | bytes 393224 | tf_op jit(solution)/shard_map/ppermute | solution.py:384
  138.4 7.6 %copy-start.10 = (f32[1024,128]{1,0:T(8,128)S(1)}, f32[1024,128]{1,0:T(8,128)}, u32[]{:S(2)}) copy-start(f32[1024,128]{1,0:T(8,128)} %get-tuple-element.80.norm_ref) | copy-start | bytes 1572868
  138.4 7.6 %copy-start.16 = (f32[1024,128]{1,0:T(8,128)S(1)}, f32[1024,128]{1,0:T(8,128)}, u32[]{:S(2)}) copy-start(f32[1024,128]{1,0:T(8,128)} %copy-done.15) | copy-start | bytes 1572868
  138.5 5.3 %collective-permute-start.27 = (bf16[512,128]{1,0:T(8,128)(2,1)S(1)}, bf16[512,128]{1,0:T(8,128)(2,1)S(1)}, u32[]{:S(2)}, u32[]{:S(2)}) collective-permute-start(bf16[512,128]{1,0:T(8,128)(2,1)S(1)} %get-tuple-element.145), channel_id=1, source_target_pairs={{0,8},{8,0},{16,24},{24,16},{1,9},{9,1},{17,25},{25,17},{2,10},{10... | collective-permute-start | bytes 393224 | tf_op jit(solution)/shard_map/ppermute | solution.py:384
  143.7 6.6 %copy-start.24 = (f32[1024,128]{1,0:T(8,128)S(1)}, f32[1024,128]{1,0:T(8,128)}, u32[]{:S(2)}) copy-start(f32[1024,128]{1,0:T(8,128)} %copy-done.23) | copy-start | bytes 1572868
  143.8 5.0 %collective-permute-start.30 = (bf16[512,128]{1,0:T(8,128)(2,1)S(1)}, bf16[512,128]{1,0:T(8,128)(2,1)S(1)}, u32[]{:S(2)}, u32[]{:S(2)}) collective-permute-start(bf16[512,128]{1,0:T(8,128)(2,1)S(1)} %get-tuple-element.142), channel_id=1, source_target_pairs={{0,8},{8,0},{16,24},{24,16},{1,9},{9,1},{17,25},{25,17},{2,10},{10... | collective-permute-start | bytes 393224 | tf_op jit(solution)/shard_map/ppermute | solution.py:384
  145.3 5.0 %collective-permute-start.29 = (bf16[512,128]{1,0:T(8,128)(2,1)S(1)}, bf16[512,128]{1,0:T(8,128)(2,1)S(1)}, u32[]{:S(2)}, u32[]{:S(2)}) collective-permute-start(bf16[512,128]{1,0:T(8,128)(2,1)S(1)} %get-tuple-element.143), channel_id=1, source_target_pairs={{0,16},{8,24},{16,0},{24,8},{1,17},{9,25},{17,1},{25,9},{2,18},{10... | collective-permute-start | bytes 393224 | tf_op jit(solution)/shard_map/ppermute | solution.py:384
  146.1 4.3 %copy-start.13 = (bf16[1024,1024]{1,0:T(8,128)(2,1)S(1)}, bf16[1024,1024]{1,0:T(8,128)(2,1)}, u32[]{:S(2)}) copy-start(bf16[1024,1024]{1,0:T(8,128)(2,1)} %scored_0_2.1.refs_2_) | copy-start | bytes 6291460
  146.1 4.3 %copy-start.14 = (bf16[1024,1024]{1,0:T(8,128)(2,1)S(1)}, bf16[1024,1024]{1,0:T(8,128)(2,1)}, u32[]{:S(2)}) copy-start(bf16[1024,1024]{1,0:T(8,128)(2,1)} %scored_0_1.1.refs_1_) | copy-start | bytes 6291460
  146.1 4.3 %copy-start.21 = (bf16[1024,1024]{1,0:T(8,128)(2,1)S(1)}, bf16[1024,1024]{1,0:T(8,128)(2,1)}, u32[]{:S(2)}) copy-start(bf16[1024,1024]{1,0:T(8,128)(2,1)} %get-tuple-element.85.refs_0_) | copy-start | bytes 6291460
  146.1 4.3 %copy-start.22 = (bf16[1024,1024]{1,0:T(8,128)(2,1)S(1)}, bf16[1024,1024]{1,0:T(8,128)(2,1)}, u32[]{:S(2)}) copy-start(bf16[1024,1024]{1,0:T(8,128)(2,1)} %get-tuple-element.96.refs_3_) | copy-start | bytes 6291460
  150.4 3.1 %copy-start.26 = (f32[512,128]{1,0:T(8,128)S(1)}, f32[512,128]{1,0:T(8,128)}, u32[]{:S(2)}) copy-start(f32[512,128]{1,0:T(8,128)} %copy-done.25) | copy-start | bytes 786436
  150.4 3.1 %copy-start.28 = (f32[512,128]{1,0:T(8,128)S(1)}, f32[512,128]{1,0:T(8,128)}, u32[]{:S(2)}) copy-start(f32[512,128]{1,0:T(8,128)} %copy-done.27) | copy-start | bytes 786436
  153.3 2.8 %copy-start.30 = (f32[512,128]{1,0:T(8,128)S(1)}, f32[512,128]{1,0:T(8,128)}, u32[]{:S(2)}) copy-start(f32[512,128]{1,0:T(8,128)} %copy-done.29) | copy-start | bytes 786436
  153.3 2.8 %copy-start.32 = (f32[512,128]{1,0:T(8,128)S(1)}, f32[512,128]{1,0:T(8,128)}, u32[]{:S(2)}) copy-start(f32[512,128]{1,0:T(8,128)} %copy-done.31) | copy-start | bytes 786436
  153.4 2.0 %collective-permute-start.31 = (bf16[4,512,128]{2,1,0:T(8,128)(2,1)S(1)}, bf16[4,512,128]{2,1,0:T(8,128)(2,1)S(1)}, u32[]{:S(2)}, u32[]{:S(2)}) collective-permute-start(bf16[4,512,128]{2,1,0:T(8,128)(2,1)S(1)} %slice.158), channel_id=1, source_target_pairs={{0,1},{1,0},{2,3},{3,2},{4,5},{5,4},{6,7},{7,6},{8,9},{9,8},{10,11... | collective-permute-start | bytes 1572872 | tf_op jit(solution)/shard_map/ppermute | solution.py:384
  155.5 8.4 %collective-permute-start.32 = (bf16[2,512,128]{2,1,0:T(8,128)(2,1)S(1)}, bf16[2,512,128]{2,1,0:T(8,128)(2,1)S(1)}, u32[]{:S(2)}, u32[]{:S(2)}) collective-permute-start(bf16[2,512,128]{2,1,0:T(8,128)(2,1)S(1)} %slice.160), channel_id=1, source_target_pairs={{0,2},{1,3},{2,0},{3,1},{4,6},{5,7},{6,4},{7,5},{8,10},{9,11},{10,... | collective-permute-start | bytes 786440 | tf_op jit(solution)/shard_map/ppermute | solution.py:384
  164.1 6.9 %collective-permute-start.33 = (bf16[1,512,128]{2,1,0:T(8,128)(2,1)S(1)}, bf16[1,512,128]{2,1,0:T(8,128)(2,1)S(1)}, u32[]{:S(2)}, u32[]{:S(2)}) collective-permute-start(bf16[1,512,128]{2,1,0:T(8,128)(2,1)S(1)} %slice.162), channel_id=1, source_target_pairs={{0,6},{1,7},{2,4},{3,5},{4,2},{5,3},{6,0},{7,1},{8,14},{9,15},{10,... | collective-permute-start | bytes 393224 | tf_op jit(solution)/shard_map/ppermute | solution.py:384
  (10 other events, 20.2 us)
